TPU v7x, 256 devices: a whole 4x4x8 slice. The times are simulated.
256 devices in a mesh: dp: 4 (over x), seq: 64 (over y, z, core).
Axes of the slice: x: 4, y: 4, z: 8, core: 2. Of those that a mesh axis runs over, the one named last changes fastest.
Arguments:
- tokens: bfloat16 [4, 8192, 1152], P('dp', 'seq'), may hold values from -40 to 40
- d_out: bfloat16 [4, 8192, 1152], P('dp', 'seq'), may hold values from -16 to 16
- frames: int32 [4], P('dp'), may hold values from 16 to 32, as said below
- frame_order: int32 [4, 32], P('dp'), may hold values from 0 to 31, each once within a row
- w_qkv: bfloat16 [1152, 3456], replicated, may hold values from -4 to 4
- w_out: bfloat16 [1152, 1152], replicated, may hold values from -0.1875 to 0.1875
Outputs:
- d_tokens: bfloat16 [4, 8192, 1152], P('dp', 'seq')
- d_w_out: float32 [1152, 1152], P('seq', 'dp')
Inputs may be any that keep to these rules, and one draw needn't show every extreme that they name: Some clip has 32 frames. `frame_order`: each row holds every number of 0 to 31 once.
All inputs are finite; a program needn't handle non-finite values.
Results may differ from a plain program's by a relative error of at most 0.012.
The roundings to bfloat16 on the way count: a program that leaves them out, or rounds other values in their place, can miss the bound.
Values may be sent and summed in bfloat16 or wider, within the bound.
No kernel may reach another device: no remote copies, remote signals or barrier semaphores. Data moves between devices by JAX's collectives and lax.ppermute only.
A program may use at most 64 MiB of HBM per device.

v0:
```python
import math

import jax
import jax.numpy as jnp
from jax import lax
from jax.sharding import PartitionSpec as P

H = 16


def layer_stats(tokens):
    values = tokens.astype(jnp.float32)
    center = values - jnp.mean(values, axis=-1, keepdims=True)
    spread = jnp.mean(center * center, axis=-1, keepdims=True)
    inverse = lax.rsqrt(spread + 1e-06)
    return (center * inverse, inverse)


def attend_forward(queries, keys_in, values, live_slots, score_scale):
    scores = (
        jnp.einsum("ciqhe,cjqhe->cqhij", queries, keys_in, preferred_element_type=jnp.float32)
        * score_scale
    )
    scores = jnp.where(live_slots[:, None, None, None, :] > 0.5, scores, -1e30)
    row_max = jnp.max(scores, axis=-1, keepdims=True)
    exponent = jnp.exp(scores - row_max)
    softmax_out = exponent / jnp.sum(exponent, axis=-1, keepdims=True)
    rounded = softmax_out.astype(jnp.bfloat16)
    attended = jnp.einsum(
        "cqhij,cjqhe->ciqhe", rounded, values, preferred_element_type=jnp.float32
    ).astype(jnp.bfloat16)
    return (softmax_out, rounded, attended)


def attend_backward(queries, keys_in, values, softmax_out, rounded, head_grad, score_scale):
    d_values = jnp.einsum(
        "cqhij,ciqhe->cjqhe", rounded, head_grad, preferred_element_type=jnp.float32
    ).astype(jnp.bfloat16)
    prob_grad = jnp.einsum(
        "ciqhe,cjqhe->cqhij", head_grad, values, preferred_element_type=jnp.float32
    )
    inner_sum = jnp.sum(softmax_out * prob_grad, axis=-1, keepdims=True)
    score_grad = (softmax_out * (prob_grad - inner_sum) * score_scale).astype(jnp.bfloat16)
    d_queries = jnp.einsum(
        "cqhij,cjqhe->ciqhe", score_grad, keys_in, preferred_element_type=jnp.float32
    ).astype(jnp.bfloat16)
    d_keys = jnp.einsum(
        "cqhij,ciqhe->cjqhe", score_grad, queries, preferred_element_type=jnp.float32
    ).astype(jnp.bfloat16)
    return (d_queries, d_keys, d_values)


def body(tokens, d_out, frames, frame_order, w_qkv, w_out):
    clip_count, row_count, model_width = tokens.shape
    seq_size = lax.axis_size("seq")
    slot_count = frame_order.shape[1]
    stripe = row_count // slot_count
    patch_count = row_count * seq_size // slot_count
    head_dim = model_width // H
    score_scale = 1.0 / math.sqrt(head_dim)
    live_slots = (frame_order < frames[:, None]).astype(jnp.float32)
    position = lax.axis_index("seq") * row_count + jnp.arange(row_count, dtype=jnp.int32)
    slot_hit = (
        position[:, None] // patch_count == jnp.arange(slot_count, dtype=jnp.int32)[None, :]
    ).astype(jnp.float32)
    row_live = jnp.einsum("rs,cs->cr", slot_hit, live_slots)
    normalized, inverse = layer_stats(tokens)
    normed = normalized.astype(jnp.bfloat16)
    joined = jnp.einsum("crd,dk->crk", normed, w_qkv, preferred_element_type=jnp.float32).astype(
        jnp.bfloat16
    )
    masked = (d_out.astype(jnp.float32) * row_live[:, :, None]).astype(jnp.bfloat16)
    spread_rows = lax.all_to_all(
        joined.reshape(clip_count, row_count // seq_size, seq_size, 3 * model_width),
        "seq",
        split_axis=2,
        concat_axis=1,
        tiled=True,
    )
    head_grid = spread_rows.reshape(clip_count, slot_count, stripe, 3, H, head_dim)
    queries = head_grid[:, :, :, 0]
    keys_in = head_grid[:, :, :, 1]
    values = head_grid[:, :, :, 2]
    softmax_out, rounded, attended = attend_forward(
        queries, keys_in, values, live_slots, score_scale
    )
    returned = lax.all_to_all(
        attended.reshape(clip_count, row_count, 1, model_width),
        "seq",
        split_axis=1,
        concat_axis=2,
        tiled=True,
    )
    attended_rows = returned.reshape(clip_count, row_count, model_width)
    head_rows = jnp.einsum("cre,de->crd", masked, w_out, preferred_element_type=jnp.float32).astype(
        jnp.bfloat16
    )
    grad_out = jnp.einsum("crd,cre->de", attended_rows, masked, preferred_element_type=jnp.float32)
    sent_rows = lax.all_to_all(
        head_rows.reshape(clip_count, row_count // seq_size, seq_size, model_width),
        "seq",
        split_axis=2,
        concat_axis=1,
        tiled=True,
    )
    head_grad = sent_rows.reshape(clip_count, slot_count, stripe, H, head_dim)
    d_queries, d_keys, d_values = attend_backward(
        queries, keys_in, values, softmax_out, rounded, head_grad, score_scale
    )
    stacked = jnp.stack((d_queries, d_keys, d_values), axis=3).reshape(
        clip_count, row_count, 1, 3 * model_width
    )
    returned_grads = lax.all_to_all(stacked, "seq", split_axis=1, concat_axis=2, tiled=True)
    qkv_grad = returned_grads.reshape(clip_count, row_count, 3 * model_width)
    normed_grad = jnp.einsum("crk,dk->crd", qkv_grad, w_qkv, preferred_element_type=jnp.float32)
    mean_grad = jnp.mean(normed_grad, axis=-1, keepdims=True)
    mean_cross = jnp.mean(normed_grad * normalized, axis=-1, keepdims=True)
    d_tokens = (
        masked.astype(jnp.float32) + inverse * (normed_grad - mean_grad - normalized * mean_cross)
    ).astype(jnp.bfloat16)
    share = lax.psum_scatter(grad_out, "seq", scatter_dimension=0, tiled=True)
    final_out = lax.psum_scatter(
        share.astype(jnp.bfloat16), "dp", scatter_dimension=1, tiled=True
    ).astype(jnp.float32)
    return (d_tokens, final_out)


def solution(mesh):
    placed = (P("dp", "seq", None), P("dp", "seq", None), P("dp"), P("dp", None), P(), P())
    return jax.shard_map(
        body,
        mesh=mesh,
        in_specs=placed,
        out_specs=(P("dp", "seq", None), P("seq", "dp")),
        check_vma=False,
    )
```

profile of v0, /device:TPU:32, one launch (start us, length us, event | category | flops | bytes accessed | tf_op | source)
XLA Modules:
  0.0 501.7 jit_solution(2760273383965222090)
XLA Ops:
  8.0 0.9 convolution_bitcast_fusion
  8.9 1.9 convolution_convert_fusion.1
  10.8 1.0 copy.26
  11.9 11.8 %all-to-all-start.1 = ((bf16[1,2,64,1152]{3,1,0,2:T(2,128)(2,1)}), bf16[1,2,64,1152]{3,1,0,2:T(2,128)(2,1)S(1)}, u32[]{:S(2)}, u32[]{:S(2)}) async-start(bf16[1,2,64,1152]{3,1,0,2:T(2,128)(2,1)} %copy.26), calls=%async_computation.1 | async-start | bytes 589824 | tf_op jit(solution)/shard_map/all_to_all | solution.py:99
  24.0 4.7 convolution_convert_fusion
  28.7 1.8 copy.23
  30.6 5.4 %all-to-all-done.1 = bf16[1,2,64,1152]{3,1,0,2:T(2,128)(2,1)S(1)} async-done(((bf16[1,2,64,1152]{3,1,0,2:T(2,128)(2,1)}), bf16[1,2,64,1152]{3,1,0,2:T(2,128)(2,1)S(1)}, u32[]{:S(2)}, u32[]{:S(2)}) %all-to-all-start.1) | async-done | bytes 294944 | tf_op jit(solution)/shard_map/all_to_all | solution.py:99
  36.0 6.9 %all-to-all-start = ((bf16[1,2,64,3456]{3,1,0,2:T(2,128)(2,1)}), bf16[1,2,64,3456]{3,1,0,2:T(2,128)(2,1)}, u32[]{:S(2)}, u32[]{:S(2)}) async-start(bf16[1,2,64,3456]{3,1,0,2:T(2,128)(2,1)} %copy.23), calls=%async_computation | async-start | bytes 1769472 | tf_op jit(solution)/shard_map/all_to_all | solution.py:73
  42.9 0.6 dynamic-slice
  44.1 1.9 reshape.224
  46.0 21.1 %all-to-all-done = bf16[1,2,64,3456]{3,1,0,2:T(2,128)(2,1)} async-done(((bf16[1,2,64,3456]{3,1,0,2:T(2,128)(2,1)}), bf16[1,2,64,3456]{3,1,0,2:T(2,128)(2,1)}, u32[]{:S(2)}, u32[]{:S(2)}) %all-to-all-start) | async-done | bytes 884768 | tf_op jit(solution)/shard_map/all_to_all | solution.py:73
  67.2 5.5 %reshape.219 = bf16[1,32,4,3,16,72]{5,4,3,2,1,0:T(8,128)(2,1)} reshape(bf16[1,64,2,1,3456]{4,2,1,3,0:T(2,128)(2,1)} %bitcast.7) | data formatting | bytes 1769472 | tf_op jit(solution)/shard_map/reshape | solution.py:80
  72.7 2.7 fusion.51
  75.4 1.8 fusion.31
  77.2 3.2 fusion.52
  80.4 1.8 fusion.12
  82.2 1.0 copy.35
  83.2 2.7 reshape.233
  86.5 3.1 reduce.16
  89.6 1.8 reshape.241
  91.4 7.3 %all-to-all-start.3 = ((bf16[64,2,1152]{2,1,0:T(2,128)(2,1)}), bf16[64,2,1152]{2,1,0:T(2,128)(2,1)}, u32[]{:S(2)}, u32[]{:S(2)}) async-start(bf16[64,2,1152]{2,1,0:T(2,128)(2,1)} %reshape.241), calls=%async_computation.3 | async-start | bytes 589824 | tf_op jit(solution)/shard_map/all_to_all | solution.py:87
  98.7 3.9 fusion.9
  102.6 3.9 fusion.10
  106.6 1.8 fusion.11
  108.7 1.8 copy.31
  110.5 6.7 %reshape.232 = bf16[1,128,1,3456]{3,2,0,1:T(2,128)(2,1)} reshape(bf16[1,32,4,3,16,72]{5,4,3,2,1,0:T(8,128)(2,1)} %copy.31) | data formatting | bytes 1769472 | tf_op jit(solution)/shard_map/reshape | solution.py:110
  117.2 8.0 %reduce.15 = bf16[128,3456]{1,0:T(8,128)(2,1)} reduce(bf16[128,1,1,3456]{3,2,1,0:T(2,128)(2,1)} %bitcast.99, bf16[]{:T(256)} %broadcast.130), dimensions={1,2}, to_apply=%bitcast.82.reduce_sub_computation | reduce | bytes 1769474
  125.1 3.0 reshape.239
  128.2 10.6 %all-to-all-start.2 = ((bf16[64,2,3456]{2,1,0:T(2,128)(2,1)}), bf16[64,2,3456]{2,1,0:T(2,128)(2,1)}, u32[]{:S(2)}, u32[]{:S(2)}) async-start(bf16[64,2,3456]{2,1,0:T(2,128)(2,1)} %reshape.239), calls=%async_computation.2 | async-start | bytes 1769472 | tf_op jit(solution)/shard_map/all_to_all | solution.py:113
  139.1 3.0 reshape.242
  142.2 2.8 bitcast_reduce_fusion.1
  144.9 0.8 all_to_all.54
  145.8 1.0 copy.37
  146.8 3.2 fusion.36
  150.0 291.1 %all-reduce.2 = bf16[1152,1152]{1,0:T(8,128)(2,1)} all-reduce(f32[1152,1152]{1,0:T(8,128)} %fusion.36), channel_id=2, replica_groups=mesh['dp'=4,'seq'=64] {'seq'}, use_global_device_ids=true, to_apply=%region_7.8.clone | all-reduce | flops 1327104 | bytes 7962624
  441.1 0.9 dynamic-slice_convert_fusion
  442.0 0.9 copy.40
  443.0 22.7 %reduce-scatter.4.cloned.1.call-done = bf16[288,18]{1,0:T(8,128)(2,1)} async-done(((bf16[1152,18]{1,0:T(8,128)(2,1)}), bf16[288,18]{1,0:T(8,128)(2,1)}) %reduce-scatter.4.cloned.1.call-update) | async-done | bytes 10384
  465.7 1.0 copy.41
  466.7 0.6 convert_element_type.104
  467.3 6.2 %reshape.240 = bf16[128,1,1,3456]{3,2,1,0:T(2,128)(2,1)} reshape(bf16[64,2,3456]{2,1,0:T(2,128)(2,1)} %all-to-all-done.2) | data formatting | bytes 1769472
  473.5 7.5 %bitcast_reduce_fusion = bf16[128,3456]{1,0:T(8,128)(2,1)} fusion(bf16[128,1,1,3456]{3,2,1,0:T(2,128)(2,1)} %reshape.240), kind=kLoop, calls=%fused_computation.77 | loop fusion | bytes 1769472 | tf_op jit(solution)/shard_map/all_to_all | solution.py:113
  481.0 3.0 all_to_all.51
  484.0 1.3 copy.33
  485.3 5.8 %fusion.23 = (f32[128]{0:T(128)S(1)}, f32[128,1152]{1,0:T(8,128)S(1)}) fusion(bf16[1,128,1152]{2,1,0:T(8,128)(2,1)S(1)} %copy-done.1, f32[128]{0:T(128)S(1)} %add_rsqrt_fusion, f32[128]{0:T(128)S(1)} %broadcast_multiply_fusion.2, bf16[128,3456]{1,0:T(8,128)(2,1)S(1)} %bitcast.100, bf16[1152,3456]{1,0:T(8,128)(2,1)} %param.10), kind=kOutput, calls=%fused_computation.31 | convolution fusion | flops 1019953024 | bytes 9733632 | tf_op jit(solution)/shard_map/crk,dk->crd/dot_general | solution.py:115
  491.1 0.6 reduce_sum.58
  491.8 0.7 broadcast_multiply_fusion
  492.4 2.0 fusion.27
  (40 shorter events, 1.7 us)
Async XLA Ops:
  7.2 1.8 copy-start
  7.2 16.5 %copy-start.1 = (bf16[1,128,1152]{2,1,0:T(8,128)(2,1)S(1)}, bf16[1,128,1152]{2,1,0:T(8,128)(2,1)}, u32[]{:S(2)}) copy-start(bf16[1,128,1152]{2,1,0:T(8,128)(2,1)} %param.6) | copy-start | bytes 884740
  11.9 24.1 %all-to-all-start.1 = ((bf16[1,2,64,1152]{3,1,0,2:T(2,128)(2,1)}), bf16[1,2,64,1152]{3,1,0,2:T(2,128)(2,1)S(1)}, u32[]{:S(2)}, u32[]{:S(2)}) async-start(bf16[1,2,64,1152]{3,1,0,2:T(2,128)(2,1)} %copy.26), calls=%async_computation.1 | async-start | bytes 589824 | tf_op jit(solution)/shard_map/all_to_all | solution.py:99
  28.7 14.2 %copy-start.11 = (u32[256]{0:T(256)S(1)}, u32[256]{0:T(256)}, u32[]{:S(2)}) copy-start(u32[256]{0:T(256)} %constant.46) | copy-start | bytes 3076
  28.7 15.3 %copy-start.10 = (s32[1,32]{1,0:T(1,128)S(1)}, s32[1,32]{1,0:T(1,128)}, u32[]{:S(2)}) copy-start(s32[1,32]{1,0:T(1,128)} %param.9) | copy-start | bytes 388
  36.0 8.1 %copy-start.7 = (bf16[1,2,64,1152]{3,1,0,2:T(2,128)(2,1)}, bf16[1,2,64,1152]{3,1,0,2:T(2,128)(2,1)S(1)}, u32[]{:S(2)}) copy-start(bf16[1,2,64,1152]{3,1,0,2:T(2,128)(2,1)S(1)} %all-to-all-done.1) | copy-start | bytes 884740
  36.0 31.2 %all-to-all-start = ((bf16[1,2,64,3456]{3,1,0,2:T(2,128)(2,1)}), bf16[1,2,64,3456]{3,1,0,2:T(2,128)(2,1)}, u32[]{:S(2)}, u32[]{:S(2)}) async-start(bf16[1,2,64,3456]{3,1,0,2:T(2,128)(2,1)} %copy.23), calls=%async_computation | async-start | bytes 1769472 | tf_op jit(solution)/shard_map/all_to_all | solution.py:73
  46.0 29.3 %copy-start.3 = (bf16[32,4,16,72]{3,2,1,0:T(8,128)(2,1)}, bf16[32,4,16,72]{3,2,1,0:T(8,128)(2,1)S(1)}, u32[]{:S(2)}) copy-start(bf16[32,4,16,72]{3,2,1,0:T(8,128)(2,1)S(1)} %reshape.224) | copy-start | bytes 884740
  75.4 1.8 copy-start.5
  77.2 3.2 copy-start.6
  80.4 1.8 copy-start.12
  91.4 36.8 %all-to-all-start.3 = ((bf16[64,2,1152]{2,1,0:T(2,128)(2,1)}), bf16[64,2,1152]{2,1,0:T(2,128)(2,1)}, u32[]{:S(2)}, u32[]{:S(2)}) async-start(bf16[64,2,1152]{2,1,0:T(2,128)(2,1)} %reshape.241), calls=%async_computation.3 | async-start | bytes 589824 | tf_op jit(solution)/shard_map/all_to_all | solution.py:87
  98.7 3.9 copy-start.13
  102.6 3.9 copy-start.4
  106.5 1.8 copy-start.8
  106.5 1.8 copy-start.9
  128.2 18.6 %copy-start.2 = (bf16[1,128,1152]{2,1,0:T(8,128)(2,1)S(1)}, bf16[1,128,1152]{2,1,0:T(8,128)(2,1)}, u32[]{:S(2)}) copy-start(bf16[1,128,1152]{2,1,0:T(8,128)(2,1)} %param.7) | copy-start | bytes 884740
  128.2 339.1 %all-to-all-start.2 = ((bf16[64,2,3456]{2,1,0:T(2,128)(2,1)}), bf16[64,2,3456]{2,1,0:T(2,128)(2,1)}, u32[]{:S(2)}, u32[]{:S(2)}) async-start(bf16[64,2,3456]{2,1,0:T(2,128)(2,1)} %reshape.239), calls=%async_computation.2 | async-start | bytes 1769472 | tf_op jit(solution)/shard_map/all_to_all | solution.py:113
  138.8 326.9 %reduce-scatter.4.cloned.1.call-start = ((), (), s32[]{:S(2)}) async-start(), calls=%async_computation.5 | async-start | bytes 368640
Sparse Core Ops, SparseCore 0:
  443.1 22.5 reduce-scatter.3
where the time goes:
time: 508 us; the launch traced here: 502 us
  blocking collectives  291 us (57%)
  local copies, waits for them, and re-layouts  59.6 us (12%)
  waiting for transfers between devices  49.3 us (10%)
  starting transfers between devices  36.8 us (7%)
  matrix products  33 us (6%)
  between operations  16.1 us (3%)
  other arithmetic  15.8 us (3%)
    unnamed x1, blocking collectives  291 us
    unnamed x2, waiting for transfers between devices  22.8 us
    all_to_all x1, waiting for transfers between devices, body(): lax.all_to_all(joined.reshape(clip_count, row_count // seq_size, seq_size...  21.1 us
    unnamed x36, local copies, waits for them, and re-layouts  17.2 us
    all_to_all x3, local copies, waits for them, and re-layouts, body(): lax.all_to_all(stacked, 'seq', split_axis=1, concat_axis=2, tiled=True)  11.8 us
    all_to_all x1, starting transfers between devices, body(): lax.all_to_all(head_rows.reshape(clip_count, row_count // seq_size, seq_s...  11.8 us
    unnamed x2, other arithmetic  11.1 us
    all_to_all x1, starting transfers between devices, body(): lax.all_to_all(stacked, 'seq', split_axis=1, concat_axis=2, tiled=True)  10.6 us
  transfers between devices with their start and end apart: 5, of which 3 were waited for; matrix products, arithmetic and copies ran while one was open for 10% of the time, Pallas kernels for 0%

commit v1 on v0

v1 whole, which is shorter than its diff:
```python
import math

import jax
import jax.numpy as jnp
from jax import lax
from jax.experimental import pallas as pl
from jax.experimental.pallas import tpu as pltpu
from jax.sharding import Mesh, PartitionSpec as P

H = 16
D = 1152
E = D // H
SLOTS = 32
PATCHES = 4
ROWS = SLOTS * PATCHES
SCALE = 1.0 / math.sqrt(E)
BF = jnp.bfloat16
F32 = jnp.float32
MIB = 1024 * 1024
COLS = 288
WIDE = 384
OUT_ROWS = 18
PAD_ROWS = 24

NN = (((1,), (0,)), ((), ()))
NT = (((1,), (1,)), ((), ()))
TN = (((0,), (0,)), ((), ()))


def dot(a, b, dims=NN):
    return lax.dot_general(a, b, dims, preferred_element_type=F32)


def whole():
    return pl.BlockSpec(memory_space=pltpu.VMEM)


def call(kernel, out_shape, inputs, scratch=(), limit=32, flops=0, data=0, smem=()):
    specs = [
        pl.BlockSpec(memory_space=pltpu.SMEM) if i in smem else whole() for i in range(len(inputs))
    ]
    return pl.pallas_call(
        kernel,
        out_shape=out_shape,
        in_specs=specs,
        out_specs=jax.tree.map(lambda _: whole(), out_shape),
        scratch_shapes=list(scratch),
        compiler_params=pltpu.CompilerParams(vmem_limit_bytes=limit * MIB),
        cost_estimate=pl.CostEstimate(flops=flops, bytes_accessed=data, transcendentals=0),
    )(*inputs)


def interleave(rows_first):
    packed = lax.broadcasted_iota(jnp.int32, (256, 256), 0 if rows_first else 1)
    plain = lax.broadcasted_iota(jnp.int32, (256, 256), 1 if rows_first else 0)
    inner = packed % 8
    target = (packed // 8) * 4 + inner % 4 + jnp.where(inner >= 4, 128, 0)
    return (plain == target).astype(F32).astype(BF)


def pack_kernel(tokens_ref, d_out_ref, packed_ref):
    both = jnp.concatenate([tokens_ref[...], d_out_ref[...]], axis=0)
    packed_ref[...] = dot(interleave(True), both).astype(BF)


def row_stats(tokens):
    values = tokens.astype(F32)
    center = values - jnp.mean(values, axis=-1, keepdims=True)
    spread = jnp.mean(center * center, axis=-1, keepdims=True)
    inverse = lax.rsqrt(spread + 1e-06)
    return center * inverse, inverse


def window(head):
    low = head * E
    base = low // 128 * 128
    width = 128 if low + E <= base + 128 else 256
    lane = lax.broadcasted_iota(jnp.int32, (ROWS, width), 1)
    inside = (lane >= low - base) & (lane < low - base + E)
    return base, width, inside


def only(inside, array):
    return jnp.where(inside, array, jnp.zeros_like(array))


def forward_kernel(
    place_ref, packed_ref, live_row_ref, live_col_ref, w_qkv_ref,
    tokens_ref, masked_ref, joined_ref, probs_ref, own_ref, one_ref, two_ref, three_ref,
    slice_ref,
):
    plain = dot(interleave(False), packed_ref[...])
    tokens = plain[:ROWS].astype(BF)
    tokens_ref[...] = tokens
    masked = (plain[ROWS:] * live_row_ref[...]).astype(BF)
    masked_ref[...] = masked
    normalized, _ = row_stats(tokens)
    normed = normalized.astype(BF)
    for chunk in range(9):
        columns = slice(chunk * 384, (chunk + 1) * 384)
        joined_ref[:, columns] = dot(normed, w_qkv_ref[:, columns]).astype(BF)
    for part in range(4):
        slice_ref[part, :, :COLS] = masked[:, part * COLS : (part + 1) * COLS]
        slice_ref[part, :, COLS:] = jnp.zeros((ROWS, WIDE - COLS), BF)
    me = place_ref[0]
    sends = (own_ref, one_ref, two_ref, three_ref)
    for step, out_ref in enumerate(sends):
        out_ref[:, D:] = slice_ref[(me + step) % 4]
    row = lax.broadcasted_iota(jnp.int32, (ROWS, ROWS), 0)
    col = lax.broadcasted_iota(jnp.int32, (ROWS, ROWS), 1)
    allowed = (row % PATCHES == col % PATCHES) & (live_col_ref[...] > 0.5)
    for head in range(H):
        base, width, inside = window(head)
        queries = only(inside, joined_ref[:, base : base + width])
        keys_in = joined_ref[:, D + base : D + base + width]
        values = joined_ref[:, 2 * D + base : 2 * D + base + width]
        scores = jnp.where(allowed, dot(queries, keys_in, NT) * SCALE, -1e30)
        exponent = jnp.exp(scores - jnp.max(scores, axis=-1, keepdims=True))
        probs = exponent / jnp.sum(exponent, axis=-1, keepdims=True)
        probs_ref[head] = probs
        attended = dot(probs.astype(BF), values).astype(BF)
        if head == 0:
            own_ref[:, base : base + width] = attended
        else:
            before = own_ref[:, base : base + width]
            own_ref[:, base : base + width] = jnp.where(inside, attended, before)
    attended = own_ref[:, :D]
    one_ref[:, :D] = attended
    two_ref[:, :D] = attended
    three_ref[:, :D] = attended


def backward_kernel(
    tokens_ref, masked_ref, joined_ref, probs_ref, w_qkv_ref, w_out_ref, d_tokens_ref, grad_ref, head_ref
):
    masked = masked_ref[...]
    for chunk in range(3):
        columns = slice(chunk * 384, (chunk + 1) * 384)
        head_ref[:, columns] = dot(masked, w_out_ref[columns, :], NT).astype(BF)
    for head in range(H):
        base, width, inside = window(head)
        queries = only(inside, joined_ref[:, base : base + width])
        keys_in = joined_ref[:, D + base : D + base + width]
        values = joined_ref[:, 2 * D + base : 2 * D + base + width]
        head_grad = only(inside, head_ref[:, base : base + width])
        probs = probs_ref[head]
        prob_grad = dot(head_grad, values, NT)
        inner = jnp.sum(probs * prob_grad, axis=-1, keepdims=True)
        score_grad = (probs * (prob_grad - inner) * SCALE).astype(BF)
        parts = (
            dot(score_grad, keys_in).astype(BF),
            dot(score_grad, queries, TN).astype(BF),
            dot(probs.astype(BF), head_grad, TN).astype(BF),
        )
        for index, part in enumerate(parts):
            at = index * D + base
            if head == 0:
                grad_ref[:, at : at + width] = part
            else:
                grad_ref[:, at : at + width] = jnp.where(inside, part, grad_ref[:, at : at + width])
    normed_grad = jnp.concatenate(
        [dot(grad_ref[...], w_qkv_ref[c * 384 : (c + 1) * 384, :], NT) for c in range(3)], axis=1
    )
    normalized, inverse = row_stats(tokens_ref[...])
    mean_grad = jnp.mean(normed_grad, axis=-1, keepdims=True)
    mean_cross = jnp.mean(normed_grad * normalized, axis=-1, keepdims=True)
    d_tokens_ref[...] = (
        masked.astype(F32) + inverse * (normed_grad - mean_grad - normalized * mean_cross)
    ).astype(BF)


def weight_kernel(own_ref, one_ref, two_ref, three_ref, mine_ref, theirs_ref, keep_ref, send_ref):
    refs = (own_ref, one_ref, two_ref, three_ref)
    attended = jnp.concatenate([ref[:, :D] for ref in refs], axis=0)
    masked = jnp.concatenate([ref[:, D:] for ref in refs], axis=0)
    theirs = dot(attended, theirs_ref[...]).astype(BF)
    send_ref[...] = dot(theirs, masked, TN).astype(BF)
    mine = dot(attended, mine_ref[...]).astype(BF)
    keep_ref[...] = dot(mine, masked, TN)


def chosen_columns(core):
    lane = jnp.arange(SLOTS * PAD_ROWS, dtype=jnp.int32)
    inner = lane % PAD_ROWS
    target = lane // PAD_ROWS * (2 * OUT_ROWS) + core * OUT_ROWS + inner
    target = jnp.where(inner < OUT_ROWS, target, -1)
    return (jnp.arange(D, dtype=jnp.int32)[:, None] == target[None, :]).astype(BF)


def body(tokens, d_out, frames, frame_order, w_qkv, w_out):
    place = lax.axis_index("dp")
    core = lax.axis_index("core")
    shape = jax.ShapeDtypeStruct
    live = (frame_order[0] < frames[0]).astype(F32)
    live_rows = jnp.repeat(live, PATCHES)
    packed = call(pack_kernel, shape((256, D), BF), (tokens[0], d_out[0]), limit=16)
    arrived = lax.all_to_all(
        packed.reshape(SLOTS, 8, D), ("y", "z"), split_axis=0, concat_axis=0, tiled=True
    ).reshape(256, D)
    kept, masked, joined, probs, own, one, two, three = call(
        forward_kernel,
        (
            shape((ROWS, D), BF),
            shape((ROWS, D), BF),
            shape((ROWS, 3 * D), BF),
            shape((H, ROWS, ROWS), F32),
        )
        + (shape((ROWS, D + WIDE), BF),) * 4,
        (place.reshape(1), arrived, live_rows[:, None], live_rows[None, :], w_qkv),
        scratch=(pltpu.VMEM((4, ROWS, WIDE), BF),),
        smem=(0,),
        flops=int(2e9),
        data=int(14e6),
    )
    ring = lambda step: [(i, (i + step) % 4) for i in range(4)]
    from_one = lax.ppermute(one, "dp", ring(1))
    from_two = lax.ppermute(two, "dp", ring(2))
    from_three = lax.ppermute(three, "dp", ring(3))
    d_rows = call(
        backward_kernel,
        shape((ROWS, D), BF),
        (kept, masked, joined, probs, w_qkv, w_out),
        scratch=(pltpu.VMEM((ROWS, 3 * D), BF), pltpu.VMEM((ROWS, D), BF)),
        flops=int(3e9),
        data=int(16e6),
    )
    returned = lax.all_to_all(
        d_rows.reshape(SLOTS, PATCHES, D), ("y", "z"), split_axis=0, concat_axis=0, tiled=True
    )
    d_tokens = returned.reshape(1, ROWS, D)
    keep, send = call(
        weight_kernel,
        (shape((SLOTS * PAD_ROWS, WIDE), F32), shape((SLOTS * PAD_ROWS, WIDE), BF)),
        (own, from_one, from_two, from_three, chosen_columns(core), chosen_columns(1 - core)),
        flops=int(3e9),
        data=int(8e6),
    )
    got = lax.ppermute(send, "core", [(0, 1), (1, 0)])
    partial = (keep + got.astype(F32)).astype(BF).reshape(SLOTS, PAD_ROWS, WIDE)
    terms = lax.all_to_all(partial, ("y", "z"), split_axis=0, concat_axis=0, tiled=True)
    total = jnp.sum(terms.astype(F32), axis=0)
    return d_tokens, total[:OUT_ROWS, :COLS]


def solution(mesh):
    fine = Mesh(mesh.devices.reshape(4, 4, 8, 2), ("dp", "y", "z", "core"))
    seq = ("y", "z", "core")
    placed = (P("dp", seq, None), P("dp", seq, None), P("dp"), P("dp", None), P(), P())
    return jax.shard_map(
        body,
        mesh=fine,
        in_specs=placed,
        out_specs=(P("dp", seq, None), P(seq, "dp")),
        check_vma=False,
    )
```

time: 508 us -> 120 us (0.24); the launches traced: 502 us -> 120 us
  blocking collectives: 291 us -> 0 us
  local copies, waits for them, and re-layouts: 59.6 us -> 7.02 us
  matrix products: 33 us -> 0 us
  Pallas kernels: 0 us -> 18.9 us
  between operations: 16.1 us -> 1.44 us
  other arithmetic: 15.8 us -> 3.1 us
  waiting for transfers between devices: 49.3 us -> 60.5 us
  starting transfers between devices: 36.8 us -> 28.6 us
    unnamed x1 -> x0, blocking collectives: 291 us -> none
    dot_general x10 -> x0, matrix products: 29.8 us -> none  [the longest x1 5.84 us: body(): jnp.einsum('crk,dk->crd', qkv_grad, w_qkv, preferred_element_type=jnp.flo...]
    unnamed x2 -> x0, waiting for transfers between devices: 22.8 us -> none
    all_to_all x4 -> x3, waiting for transfers between devices: 26.6 us -> 48.6 us  [the longest x1 18 us: body(): lax.all_to_all(packed.reshape(SLOTS, 8, D), ('y', 'z'), split_axis=0, con...]
    pallas_call x0 -> x4, Pallas kernels: none -> 18.9 us  [call(): pl.pallas_call(kernel, out_shape=out_shape, in_specs=specs, out_specs=jax...]
    all_to_all x6 -> x0, local copies, waits for them, and re-layouts: 16.3 us -> none  [the longest x3 11.8 us: body(): lax.all_to_all(stacked, 'seq', split_axis=1, concat_axis=2, tiled=True)]
    reshape x5 -> x2, local copies, waits for them, and re-layouts: 17.8 us -> 1.58 us  [the longest x1 0.79 us: body(): d_rows.reshape(SLOTS, PATCHES, D)]
    all_to_all x4 -> x3, starting transfers between devices: 36.5 us -> 22.6 us  [the longest x1 11.4 us: body(): lax.all_to_all(packed.reshape(SLOTS, 8, D), ('y', 'z'), split_axis=0, con...]
  transfers between devices with their start and end apart: 5 -> 7, of which waited for: 3 -> 5; matrix products, arithmetic and copies ran while one was open for 10% -> 4% of each run, Pallas kernels for 0% -> 7%
where the time goes in v1:
time: 120 us
  waiting for transfers between devices  60.5 us (50%)
  starting transfers between devices  28.6 us (24%)
  Pallas kernels  18.9 us (16%)
  local copies, waits for them, and re-layouts  7.02 us (6%)
  other arithmetic  3.1 us (3%)
  between operations  1.44 us (1%)
    pallas_call x4, Pallas kernels, call(): pl.pallas_call(kernel, out_shape=out_shape, in_specs=specs, out_specs=jax...  18.9 us
    all_to_all x1, waiting for transfers between devices, body(): lax.all_to_all(packed.reshape(SLOTS, 8, D), ('y', 'z'), split_axis=0, con...  18 us
    all_to_all x1, waiting for transfers between devices, body(): lax.all_to_all(partial, ('y', 'z'), split_axis=0, concat_axis=0, tiled=True)  18 us
    all_to_all x1, waiting for transfers between devices, body(): lax.all_to_all(d_rows.reshape(SLOTS, PATCHES, D), ('y', 'z'), split_axis=...  12.6 us
    all_to_all x1, starting transfers between devices, body(): lax.all_to_all(packed.reshape(SLOTS, 8, D), ('y', 'z'), split_axis=0, con...  11.4 us
    ppermute x1, waiting for transfers between devices, body(): from_two = lax.ppermute(two, 'dp', ring(2))  6.72 us
    all_to_all x1, starting transfers between devices, body(): lax.all_to_all(d_rows.reshape(SLOTS, PATCHES, D), ('y', 'z'), split_axis=...  6.63 us
    unnamed x14, local copies, waits for them, and re-layouts  5.2 us
  transfers between devices with their start and end apart: 7, of which 5 were waited for; matrix products, arithmetic and copies ran while one was open for 4% of the time, Pallas kernels for 7%

profile of v1, /device:TPU:32, one launch (start us, length us, event | category | flops | bytes accessed | tf_op | source)
XLA Modules:
  0.0 119.5 jit_solution(3449428401643898510)
XLA Ops:
  0.6 0.0 copy-start.4
  0.6 0.0 copy-start.2
  0.6 1.0 copy-done.2
  1.6 0.0 copy-start.3
  1.6 1.0 copy-done.3
  2.6 1.2 shard_map.77
  3.7 11.4 %all-to-all-start = ((bf16[32,8,1152]{2,1,0:T(8,128)(2,1)}), bf16[32,8,1152]{2,1,0:T(8,128)(2,1)S(1)}, u32[]{:S(2)}, u32[]{:S(2)}) async-start(bf16[32,8,1152]{2,1,0:T(8,128)(2,1)} %bitcast.3), calls=%async_computation | async-start | bytes 1179648 | tf_op jit(solution)/shard_map/all_to_all | solution.py:197
  15.8 0.0 copy-done.4
  15.8 0.1 broadcast_in_dim.5
  15.8 0.1 broadcast_in_dim_reshape.7.live_col_ref
  16.0 0.1 broadcast_in_dim_reshape.8.live_row_ref
  16.1 18.0 %all-to-all-done = bf16[32,8,1152]{2,1,0:T(8,128)(2,1)S(1)} async-done(((bf16[32,8,1152]{2,1,0:T(8,128)(2,1)}), bf16[32,8,1152]{2,1,0:T(8,128)(2,1)S(1)}, u32[]{:S(2)}, u32[]{:S(2)}) %all-to-all-start) | async-done | bytes 589856 | tf_op jit(solution)/shard_map/all_to_all | solution.py:197
  34.1 0.0 copy-start
  34.1 3.3 %copy-done = bf16[1152,3456]{1,0:T(8,128)(2,1)S(1)} copy-done((bf16[1152,3456]{1,0:T(8,128)(2,1)S(1)}, bf16[1152,3456]{1,0:T(8,128)(2,1)}, u32[]{:S(2)}) %copy-start) | copy-done | bytes 7962648
  37.4 5.5 %shard_map.78 = (bf16[128,1152]{1,0:T(8,128)(2,1)S(1)}, bf16[128,1152]{1,0:T(8,128)(2,1)S(1)}, bf16[128,3456]{1,0:T(8,128)(2,1)S(1)}, f32[16,128,128]{2,1,0:T(8,...) custom-call(s32[1]{0:T(128)} %bitcast.place_ref, ...), custom_call_target="tpu_custom_call" | custom-call | flops 2000000000 | bytes 14000000 | tf_op jit(solution)/shard_map/pallas_call | solution.py:42
  42.9 1.6 %collective-permute-start = (bf16[128,1536]{1,0:T(8,128)(2,1)S(1)}, bf16[128,1536]{1,0:T(8,128)(2,1)S(1)}, u32[]{:S(2)}, u32[]{:S(2)}) collective-permute-start(bf16[128,1536]{1,0:T(8,128)(2,1)S(1)} %get-tuple-element.17), channel_id=1, source_target_pairs={{0,64},{64,128},{128,192},{192,0},{1,65},{65,129},{129,193},{193,1... | collective-permute-start | bytes 1179656 | tf_op jit(solution)/shard_map/ppermute | solution.py:216
  44.5 2.7 %collective-permute-start.1 = (bf16[128,1536]{1,0:T(8,128)(2,1)S(1)}, bf16[128,1536]{1,0:T(8,128)(2,1)S(1)}, u32[]{:S(2)}, u32[]{:S(2)}) collective-permute-start(bf16[128,1536]{1,0:T(8,128)(2,1)S(1)} %get-tuple-element.18), channel_id=1, source_target_pairs={{0,128},{64,192},{128,0},{192,64},{1,129},{65,193},{129,1},{193,65... | collective-permute-start | bytes 1179656 | tf_op jit(solution)/shard_map/ppermute | solution.py:217
  47.2 1.4 %collective-permute-start.2 = (bf16[128,1536]{1,0:T(8,128)(2,1)S(1)}, bf16[128,1536]{1,0:T(8,128)(2,1)S(1)}, u32[]{:S(2)}, u32[]{:S(2)}) collective-permute-start(bf16[128,1536]{1,0:T(8,128)(2,1)S(1)} %get-tuple-element.19), channel_id=1, source_target_pairs={{0,192},{64,0},{128,64},{192,128},{1,193},{65,1},{129,65},{193,129... | collective-permute-start | bytes 1179656 | tf_op jit(solution)/shard_map/ppermute | solution.py:218
  48.6 0.0 slice-start
  48.6 1.4 %fusion = (bf16[1152,768]{1,0:T(8,128)(2,1)S(1)}, bf16[1152,768]{1,0:T(8,128)(2,1)S(1)}) fusion(s32[768]{0:T(1024)S(1)} %add_select_fusion.3, s32[768]{0:T(1024)S(1)} %add_select_fusion.2), kind=kLoop, calls=%fused_computation.2 | loop fusion | flops 3538944 | bytes 3545088 | tf_op jit(solution)/shard_map/convert_element_type | solution.py:187
  50.0 5.2 %collective-permute-done.one_ref = bf16[128,1536]{1,0:T(8,128)(2,1)S(1)} collective-permute-done((bf16[128,1536]{1,0:T(8,128)(2,1)S(1)}, bf16[128,1536]{1,0:T(8,128)(2,1)S(1)}, u32[]{:S(2)}, u32[]{:S(2)}) %collective-permute-start) | collective-permute-done | bytes 393248 | tf_op jit(solution)/shard_map/ppermute | solution.py:216
  55.2 6.7 %collective-permute-done.1.two_ref = bf16[128,1536]{1,0:T(8,128)(2,1)S(1)} collective-permute-done((bf16[128,1536]{1,0:T(8,128)(2,1)S(1)}, bf16[128,1536]{1,0:T(8,128)(2,1)S(1)}, u32[]{:S(2)}, u32[]{:S(2)}) %collective-permute-start.1) | collective-permute-done | bytes 393248 | tf_op jit(solution)/shard_map/ppermute | solution.py:217
  62.0 0.0 collective-permute-done.2.three_ref
  62.0 0.0 slice-start.1
  62.0 0.0 copy-start.1
  62.0 3.9 %shard_map.80 = (f32[768,384]{1,0:T(8,128)S(1)}, bf16[768,384]{1,0:T(8,128)(2,1)S(1)}) custom-call(bf16[128,1536]{1,0:T(8,128)(2,1)S(1)} %get-tuple-element.16.own_ref, bf16[128,1536]{1,0:T(8,128)(2,1)S(1)} %collective-permute-done.one_ref, bf16[128,1536]{1,0:T(8,128)(2,1)S(1)} %collective-permute-done.1.two_ref, ...), custom_call_target="tpu_custom_call" | custom-call | flops 3000000000 | bytes 8000000 | tf_op jit(solution)/shard_map/pallas_call | solution.py:42
  65.9 0.3 collective-permute-start.3
  66.2 0.0 slice-done
  66.2 0.0 slice-done.1
  66.2 0.0 copy-done.1
  66.2 8.3 %shard_map.79 = bf16[128,1152]{1,0:T(8,128)(2,1)S(1)} custom-call(bf16[128,1152]{1,0:T(8,128)(2,1)S(1)} %get-tuple-element.12.tokens_ref, bf16[128,1152]{1,0:T(8,128)(2,1)S(1)} %get-tuple-element.13.masked_ref, bf16[128,3456]{1,0:T(8,128)(2,1)S(1)} %get-tuple-element.14.joined_ref, f32[16,128,128]{2,1,0:T(8,128)S(1)} %get-tuple-element.15.probs_ref, ...), custom_call_target="tpu_custom_call" | custom-call | flops 3000000000 | bytes 16000000 | tf_op jit(solution)/shard_map/pallas_call | solution.py:42
  74.5 0.8 reshape.56
  75.3 6.6 %all-to-all-start.1 = ((bf16[32,4,1152]{2,1,0:T(4,128)(2,1)}), bf16[32,4,1152]{2,1,0:T(4,128)(2,1)S(1)}, u32[]{:S(2)}, u32[]{:S(2)}) async-start(bf16[32,4,1152]{2,1,0:T(4,128)(2,1)} %reshape.56), calls=%async_computation.1 | async-start | bytes 589824 | tf_op jit(solution)/shard_map/all_to_all | solution.py:227
  81.9 0.0 collective-permute-done.3
  81.9 0.9 add_convert_fusion
  82.9 12.6 %all-to-all-done.1 = bf16[32,4,1152]{2,1,0:T(4,128)(2,1)S(1)} async-done(((bf16[32,4,1152]{2,1,0:T(4,128)(2,1)}), bf16[32,4,1152]{2,1,0:T(4,128)(2,1)S(1)}, u32[]{:S(2)}, u32[]{:S(2)}) %all-to-all-start.1) | async-done | bytes 294944 | tf_op jit(solution)/shard_map/all_to_all | solution.py:227
  95.5 4.6 %all-to-all-start.2 = ((bf16[32,24,384]{2,1,0:T(8,128)(2,1)}), bf16[32,24,384]{2,1,0:T(8,128)(2,1)S(1)}, u32[]{:S(2)}, u32[]{:S(2)}) async-start(bf16[32,24,384]{2,1,0:T(8,128)(2,1)} %bitcast.7), calls=%async_computation.2 | async-start | bytes 1179648 | tf_op jit(solution)/shard_map/all_to_all | solution.py:240
  100.1 0.8 reshape.57
  100.9 18.0 %all-to-all-done.2 = bf16[32,24,384]{2,1,0:T(8,128)(2,1)S(1)} async-done(((bf16[32,24,384]{2,1,0:T(8,128)(2,1)}), bf16[32,24,384]{2,1,0:T(8,128)(2,1)S(1)}, u32[]{:S(2)}, u32[]{:S(2)}) %all-to-all-start.2) | async-done | bytes 589856 | tf_op jit(solution)/shard_map/all_to_all | solution.py:240
  118.8 0.7 convert_reduce_fusion
  (4 shorter events, 0.0 us)
Async XLA Ops:
  0.6 15.1 %copy-start.4 = (s32[1,32]{1,0:T(1,128)S(1)}, s32[1,32]{1,0:T(1,128)}, u32[]{:S(2)}) copy-start(s32[1,32]{1,0:T(1,128)} %param.9) | copy-start | bytes 388
  0.6 1.0 copy-start.2
  1.6 1.0 copy-start.3
  3.7 30.4 %all-to-all-start = ((bf16[32,8,1152]{2,1,0:T(8,128)(2,1)}), bf16[32,8,1152]{2,1,0:T(8,128)(2,1)S(1)}, u32[]{:S(2)}, u32[]{:S(2)}) async-start(bf16[32,8,1152]{2,1,0:T(8,128)(2,1)} %bitcast.3), calls=%async_computation | async-start | bytes 1179648 | tf_op jit(solution)/shard_map/all_to_all | solution.py:197
  34.1 3.3 %copy-start = (bf16[1152,3456]{1,0:T(8,128)(2,1)S(1)}, bf16[1152,3456]{1,0:T(8,128)(2,1)}, u32[]{:S(2)}) copy-start(bf16[1152,3456]{1,0:T(8,128)(2,1)} %w_qkv_ref.3) | copy-start | bytes 23887876
  42.9 12.3 %collective-permute-start = (bf16[128,1536]{1,0:T(8,128)(2,1)S(1)}, bf16[128,1536]{1,0:T(8,128)(2,1)S(1)}, u32[]{:S(2)}, u32[]{:S(2)}) collective-permute-start(bf16[128,1536]{1,0:T(8,128)(2,1)S(1)} %get-tuple-element.17), channel_id=1, source_target_pairs={{0,64},{64,128},{128,192},{192,0},{1,65},{65,129},{129,193},{193,1... | collective-permute-start | bytes 1179656 | tf_op jit(solution)/shard_map/ppermute | solution.py:216
  44.5 17.5 %collective-permute-start.1 = (bf16[128,1536]{1,0:T(8,128)(2,1)S(1)}, bf16[128,1536]{1,0:T(8,128)(2,1)S(1)}, u32[]{:S(2)}, u32[]{:S(2)}) collective-permute-start(bf16[128,1536]{1,0:T(8,128)(2,1)S(1)} %get-tuple-element.18), channel_id=1, source_target_pairs={{0,128},{64,192},{128,0},{192,64},{1,129},{65,193},{129,1},{193,65... | collective-permute-start | bytes 1179656 | tf_op jit(solution)/shard_map/ppermute | solution.py:217
  47.2 14.8 %collective-permute-start.2 = (bf16[128,1536]{1,0:T(8,128)(2,1)S(1)}, bf16[128,1536]{1,0:T(8,128)(2,1)S(1)}, u32[]{:S(2)}, u32[]{:S(2)}) collective-permute-start(bf16[128,1536]{1,0:T(8,128)(2,1)S(1)} %get-tuple-element.19), channel_id=1, source_target_pairs={{0,192},{64,0},{128,64},{192,128},{1,193},{65,1},{129,65},{193,129... | collective-permute-start | bytes 1179656 | tf_op jit(solution)/shard_map/ppermute | solution.py:218
  48.6 17.5 %slice-start = ((s8[7962624]{0:T(1024)(128)(4,1)}), s8[4194304]{0:T(1024)(128)(4,1)S(1)}, s32[]{:S(2)}) async-start(s8[7962624]{0:T(1024)(128)(4,1)} %bitcast.11), calls=%async_computation.3 | async-start | bytes 8388608
  62.0 4.2 %slice-start.1 = ((s8[7962624]{0:T(1024)(128)(4,1)}), s8[3768320]{0:T(1024)(128)(4,1)S(1)}, s32[]{:S(2)}) async-start(s8[7962624]{0:T(1024)(128)(4,1)} %bitcast.11), calls=%async_computation.4 | async-start | bytes 7536640
  62.0 4.2 %copy-start.1 = (bf16[1152,1152]{1,0:T(8,128)(2,1)S(1)}, bf16[1152,1152]{1,0:T(8,128)(2,1)}, u32[]{:S(2)}) copy-start(bf16[1152,1152]{1,0:T(8,128)(2,1)} %w_out_ref.1) | copy-start | bytes 7962628
  65.9 16.0 %collective-permute-start.3 = (bf16[768,384]{1,0:T(8,128)(2,1)S(1)}, bf16[768,384]{1,0:T(8,128)(2,1)S(1)}, u32[]{:S(2)}, u32[]{:S(2)}) collective-permute-start(bf16[768,384]{1,0:T(8,128)(2,1)S(1)} %get-tuple-element.21), channel_id=1, source_target_pairs={{0,1},{1,0},{2,3},{3,2},{4,5},{5,4},{6,7},{7,6},{8,9},{9,8},{10,11... | collective-permute-start | bytes 1769480 | tf_op jit(solution)/shard_map/ppermute | solution.py:238
  75.3 20.2 %all-to-all-start.1 = ((bf16[32,4,1152]{2,1,0:T(4,128)(2,1)}), bf16[32,4,1152]{2,1,0:T(4,128)(2,1)S(1)}, u32[]{:S(2)}, u32[]{:S(2)}) async-start(bf16[32,4,1152]{2,1,0:T(4,128)(2,1)} %reshape.56), calls=%async_computation.1 | async-start | bytes 589824 | tf_op jit(solution)/shard_map/all_to_all | solution.py:227
  95.5 23.4 %all-to-all-start.2 = ((bf16[32,24,384]{2,1,0:T(8,128)(2,1)}), bf16[32,24,384]{2,1,0:T(8,128)(2,1)S(1)}, u32[]{:S(2)}, u32[]{:S(2)}) async-start(bf16[32,24,384]{2,1,0:T(8,128)(2,1)} %bitcast.7), calls=%async_computation.2 | async-start | bytes 1179648 | tf_op jit(solution)/shard_map/all_to_all | solution.py:240

commit v2 on v1

v2 whole, which is shorter than its diff:
```python
import math

import jax
import jax.numpy as jnp
from jax import lax
from jax.experimental import pallas as pl
from jax.experimental.pallas import tpu as pltpu
from jax.sharding import Mesh, PartitionSpec as P

H = 16
D = 1152
E = D // H
SLOTS = 32
PATCHES = 4
ROWS = SLOTS * PATCHES
SCALE = 1.0 / math.sqrt(E)
BF = jnp.bfloat16
F32 = jnp.float32
MIB = 1024 * 1024
COLS = 288
WIDE = 384
OUT_ROWS = 18
PAD_ROWS = 24

NN = (((1,), (0,)), ((), ()))
NT = (((1,), (1,)), ((), ()))
TN = (((0,), (0,)), ((), ()))


def dot(a, b, dims=NN):
    return lax.dot_general(a, b, dims, preferred_element_type=F32)


def whole():
    return pl.BlockSpec(memory_space=pltpu.VMEM)


def call(kernel, out_shape, inputs, scratch=(), limit=32, flops=0, data=0, smem=(), far=()):
    spaces = {i: pltpu.SMEM for i in smem} | {i: pl.ANY for i in far}
    specs = [
        pl.BlockSpec(memory_space=spaces.get(i, pltpu.VMEM)) for i in range(len(inputs))
    ]
    return pl.pallas_call(
        kernel,
        out_shape=out_shape,
        in_specs=specs,
        out_specs=jax.tree.map(lambda _: whole(), out_shape),
        scratch_shapes=list(scratch),
        compiler_params=pltpu.CompilerParams(vmem_limit_bytes=limit * MIB),
        cost_estimate=pl.CostEstimate(flops=flops, bytes_accessed=data, transcendentals=0),
    )(*inputs)


def interleave(rows_first):
    packed = lax.broadcasted_iota(jnp.int32, (256, 256), 0 if rows_first else 1)
    plain = lax.broadcasted_iota(jnp.int32, (256, 256), 1 if rows_first else 0)
    inner = packed % 8
    target = (packed // 8) * 4 + inner % 4 + jnp.where(inner >= 4, 128, 0)
    return (plain == target).astype(F32).astype(BF)


def pack_kernel(tokens_ref, d_out_ref, packed_ref, both_ref, sems):
    copies = [
        pltpu.make_async_copy(ref, both_ref.at[pl.ds(i * ROWS, ROWS)], sems.at[i])
        for i, ref in enumerate((tokens_ref, d_out_ref))
    ]
    for copy in copies:
        copy.start()
    chooser = interleave(True)
    for copy in copies:
        copy.wait()
    packed_ref[...] = dot(chooser, both_ref[...]).astype(BF)


def row_stats(tokens):
    values = tokens.astype(F32)
    center = values - jnp.mean(values, axis=-1, keepdims=True)
    spread = jnp.mean(center * center, axis=-1, keepdims=True)
    inverse = lax.rsqrt(spread + 1e-06)
    return center * inverse, inverse


def window(head):
    low = head * E
    base = low // 128 * 128
    width = 128 if low + E <= base + 128 else 256
    lane = lax.broadcasted_iota(jnp.int32, (ROWS, width), 1)
    inside = (lane >= low - base) & (lane < low - base + E)
    return base, width, inside


def only(inside, array):
    return jnp.where(inside, array, jnp.zeros_like(array))


def forward_kernel(
    place_ref, packed_ref, live_row_ref, live_col_ref, w_qkv_ref,
    tokens_ref, masked_ref, joined_ref, probs_ref, own_ref, one_ref, two_ref, three_ref,
    slice_ref, attended_ref, weight_ref, sems,
):
    copies = [
        pltpu.make_async_copy(
            w_qkv_ref.at[:, pl.ds(chunk * WIDE, WIDE)],
            weight_ref.at[:, pl.ds(chunk * WIDE, WIDE)],
            sems.at[chunk],
        )
        for chunk in range(9)
    ]
    for copy in copies:
        copy.start()
    plain = dot(interleave(False), packed_ref[...])
    tokens = plain[:ROWS].astype(BF)
    tokens_ref[...] = tokens
    normalized, _ = row_stats(tokens)
    normed = normalized.astype(BF)
    masked = (plain[ROWS:] * live_row_ref[...]).astype(BF)
    masked_ref[...] = masked
    for part in range(4):
        slice_ref[part, :, :COLS] = masked[:, part * COLS : (part + 1) * COLS]
        slice_ref[part, :, COLS:] = jnp.zeros((ROWS, WIDE - COLS), BF)
    me = place_ref[0]
    sends = (own_ref, one_ref, two_ref, three_ref)
    for step, out_ref in enumerate(sends):
        chosen = slice_ref[(me + step) % 4]
        for third in range(3):
            out_ref[D + third * ROWS : D + (third + 1) * ROWS, :] = chosen[
                :, third * 128 : (third + 1) * 128
            ]
    for chunk in range(9):
        copies[chunk].wait()
        columns = slice(chunk * WIDE, (chunk + 1) * WIDE)
        joined_ref[:, columns] = dot(normed, weight_ref[:, columns]).astype(BF)
    row = lax.broadcasted_iota(jnp.int32, (ROWS, ROWS), 0)
    col = lax.broadcasted_iota(jnp.int32, (ROWS, ROWS), 1)
    allowed = (row % PATCHES == col % PATCHES) & (live_col_ref[...] > 0.5)
    for head in range(H):
        base, width, inside = window(head)
        queries = only(inside, joined_ref[:, base : base + width])
        keys_in = joined_ref[:, D + base : D + base + width]
        values = joined_ref[:, 2 * D + base : 2 * D + base + width]
        scores = jnp.where(allowed, dot(queries, keys_in, NT) * SCALE, -1e30)
        exponent = jnp.exp(scores - jnp.max(scores, axis=-1, keepdims=True))
        probs = exponent / jnp.sum(exponent, axis=-1, keepdims=True)
        probs_ref[head] = probs
        attended = dot(probs.astype(BF), values)
        if head == 0:
            attended_ref[:, base : base + width] = attended
        else:
            before = attended_ref[:, base : base + width]
            attended_ref[:, base : base + width] = jnp.where(inside, attended, before)
    for block in range(9):
        lanes = slice(block * 128, (block + 1) * 128)
        turned = attended_ref[:, lanes].T.astype(BF)
        for out_ref in sends:
            out_ref[lanes, :] = turned


def spread_rows(to_packed):
    shape = (512, 384) if to_packed else (384, 512)
    packed = lax.broadcasted_iota(jnp.int32, shape, 0 if to_packed else 1)
    plain = lax.broadcasted_iota(jnp.int32, shape, 1 if to_packed else 0)
    row = plain % ROWS
    target = row // PATCHES * 16 + plain // ROWS * PATCHES + row % PATCHES
    return (packed == target).astype(F32).astype(BF)


def backward_kernel(
    tokens_ref, masked_ref, joined_ref, probs_ref, w_qkv_ref, w_out_ref,
    packed_ref,
    grad_ref, head_ref, weight_ref, out_weight_ref, sems,
):
    out_copies = [
        pltpu.make_async_copy(
            w_out_ref.at[pl.ds(chunk * WIDE, WIDE)],
            out_weight_ref.at[pl.ds(chunk * WIDE, WIDE)],
            sems.at[chunk],
        )
        for chunk in range(3)
    ]
    qkv_copies = [
        pltpu.make_async_copy(
            w_qkv_ref.at[pl.ds(chunk * WIDE, WIDE)],
            weight_ref.at[pl.ds(chunk * WIDE, WIDE)],
            sems.at[3 + chunk],
        )
        for chunk in range(3)
    ]
    for copy in out_copies + qkv_copies:
        copy.start()
    masked = masked_ref[...]
    for chunk in range(3):
        columns = slice(chunk * WIDE, (chunk + 1) * WIDE)
        out_copies[chunk].wait()
        head_ref[:, columns] = dot(masked, out_weight_ref[columns, :], NT).astype(BF)
    for head in range(H):
        base, width, inside = window(head)
        queries = only(inside, joined_ref[:, base : base + width])
        keys_in = joined_ref[:, D + base : D + base + width]
        values = joined_ref[:, 2 * D + base : 2 * D + base + width]
        head_grad = only(inside, head_ref[:, base : base + width])
        probs = probs_ref[head]
        prob_grad = dot(head_grad, values, NT)
        inner = jnp.sum(probs * prob_grad, axis=-1, keepdims=True)
        score_grad = (probs * (prob_grad - inner) * SCALE).astype(BF)
        parts = (
            dot(score_grad, keys_in).astype(BF),
            dot(score_grad, queries, TN).astype(BF),
            dot(probs.astype(BF), head_grad, TN).astype(BF),
        )
        for index, part in enumerate(parts):
            at = index * D + base
            if head == 0:
                grad_ref[:, at : at + width] = part
            else:
                grad_ref[:, at : at + width] = jnp.where(inside, part, grad_ref[:, at : at + width])
    pieces = []
    for chunk in range(3):
        qkv_copies[chunk].wait()
        rows = slice(chunk * WIDE, (chunk + 1) * WIDE)
        pieces.append(dot(grad_ref[...], weight_ref[rows, :], NT))
    normed_grad = jnp.concatenate(pieces, axis=1)
    normalized, inverse = row_stats(tokens_ref[...])
    mean_grad = jnp.mean(normed_grad, axis=-1, keepdims=True)
    mean_cross = jnp.mean(normed_grad * normalized, axis=-1, keepdims=True)
    d_tokens = (
        masked.astype(F32) + inverse * (normed_grad - mean_grad - normalized * mean_cross)
    ).astype(BF)
    stacked = jnp.concatenate([d_tokens[:, c * WIDE : (c + 1) * WIDE] for c in range(3)], axis=0)
    packed_ref[...] = dot(spread_rows(True), stacked).astype(BF)


def weight_kernel(own_ref, one_ref, two_ref, three_ref, chosen_ref, after_ref, terms_ref):
    refs = (own_ref, one_ref, two_ref, three_ref)
    attended = jnp.concatenate([ref[:D, :] for ref in refs], axis=1)
    masked = jnp.concatenate(
        [
            jnp.concatenate([ref[D + t * 128 : D + (t + 1) * 128, :] for t in range(3)], axis=1)
            for ref in refs
        ],
        axis=0,
    )
    chosen = dot(chosen_ref[...], attended).astype(BF)
    terms_ref[...] = dot(chosen, masked).astype(terms_ref.dtype)


def merge_kernel(rows_ref, keep_ref, got_ref, merged_ref):
    rows = rows_ref[...].astype(F32).reshape(SLOTS, 16, WIDE)
    terms = (keep_ref[...] + got_ref[...].astype(F32)).reshape(SLOTS, PAD_ROWS, WIDE)
    merged = jnp.concatenate([rows, terms], axis=1).reshape(SLOTS * 40, WIDE)
    merged_ref[...] = merged.astype(BF)


def unpack_kernel(merged_ref, d_tokens_ref, d_w_ref):
    merged = merged_ref[...].astype(F32).reshape(SLOTS, 40, WIDE)
    rows = merged[:, :16].reshape(512, WIDE).astype(BF)
    plain = dot(spread_rows(False), rows).astype(BF)
    for block in range(3):
        d_tokens_ref[:, block * WIDE : (block + 1) * WIDE] = plain[block * ROWS : (block + 1) * ROWS]
    total = jnp.sum(merged[:, 16:], axis=0)
    d_w_ref[...] = total[:OUT_ROWS, :COLS]


def chosen_rows(core):
    at = jnp.arange(SLOTS * PAD_ROWS, dtype=jnp.int32)
    inner = at % PAD_ROWS
    target = at // PAD_ROWS * (2 * OUT_ROWS) + core * OUT_ROWS + inner
    target = jnp.where(inner < OUT_ROWS, target, -1)
    return (target[:, None] == jnp.arange(D, dtype=jnp.int32)[None, :]).astype(BF)


def body(tokens, d_out, frames, frame_order, w_qkv, w_out):
    place = lax.axis_index("dp")
    core = lax.axis_index("core")
    shape = jax.ShapeDtypeStruct
    live = (frame_order[0] < frames[0]).astype(F32)
    live_rows = jnp.repeat(live, PATCHES)
    packed = call(
        pack_kernel,
        shape((256, D), BF),
        (tokens[0], d_out[0]),
        scratch=(pltpu.VMEM((256, D), BF), pltpu.SemaphoreType.DMA((2,))),
        limit=60,
        far=(0, 1),
    )
    arrived = lax.all_to_all(
        packed.reshape(SLOTS, 8, D), ("y", "z"), split_axis=0, concat_axis=0, tiled=True
    ).reshape(256, D)
    kept, masked, joined, probs, own, one, two, three = call(
        forward_kernel,
        (
            shape((ROWS, D), BF),
            shape((ROWS, D), BF),
            shape((ROWS, 3 * D), BF),
            shape((H, ROWS, ROWS), F32),
        )
        + (shape((D + WIDE, ROWS), BF),) * 4,
        (place.reshape(1), arrived, live_rows[:, None], live_rows[None, :], w_qkv),
        scratch=(
            pltpu.VMEM((4, ROWS, WIDE), BF),
            pltpu.VMEM((ROWS, D), F32),
            pltpu.VMEM((D, 3 * D), BF),
            pltpu.SemaphoreType.DMA((9,)),
        ),
        smem=(0,),
        far=(4,),
        limit=47,
        flops=int(2e9),
        data=int(14e6),
    )
    ring = lambda step: [(i, (i + step) % 4) for i in range(4)]
    from_one = lax.ppermute(one, "dp", ring(1))
    from_two = lax.ppermute(two, "dp", ring(2))
    from_three = lax.ppermute(three, "dp", ring(3))
    rows = call(
        backward_kernel,
        shape((512, WIDE), BF),
        (kept, masked, joined, probs, w_qkv, w_out),
        scratch=(
            pltpu.VMEM((ROWS, 3 * D), BF),
            pltpu.VMEM((ROWS, D), BF),
            pltpu.VMEM((D, 3 * D), BF),
            pltpu.VMEM((D, D), BF),
            pltpu.SemaphoreType.DMA((6,)),
        ),
        far=(4, 5),
        limit=47,
        flops=int(3e9),
        data=int(16e6),
    )
    payloads = (own, from_one, from_two, from_three)
    send = call(
        weight_kernel,
        shape((SLOTS * PAD_ROWS, WIDE), BF),
        payloads + (chosen_rows(1 - core), rows),
        far=(5,),
        flops=int(1e9),
        data=int(4e6),
    )
    got = lax.ppermute(send, "core", [(0, 1), (1, 0)])
    keep = call(
        weight_kernel,
        shape((SLOTS * PAD_ROWS, WIDE), F32),
        payloads + (chosen_rows(core), send),
        far=(5,),
        flops=int(1e9),
        data=int(4e6),
    )
    merged = call(merge_kernel, shape((SLOTS * 40, WIDE), BF), (rows, keep, got), limit=16)
    returned = lax.all_to_all(
        merged.reshape(SLOTS, 40, WIDE), ("y", "z"), split_axis=0, concat_axis=0, tiled=True
    ).reshape(SLOTS * 40, WIDE)
    d_tokens, d_w = call(
        unpack_kernel, (shape((ROWS, D), BF), shape((OUT_ROWS, COLS), F32)), (returned,), limit=16
    )
    return d_tokens[None], d_w


def solution(mesh):
    fine = Mesh(mesh.devices.reshape(4, 4, 8, 2), ("dp", "y", "z", "core"))
    seq = ("y", "z", "core")
    placed = (P("dp", seq, None), P("dp", seq, None), P("dp"), P("dp", None), P(), P())
    return jax.shard_map(
        body,
        mesh=fine,
        in_specs=placed,
        out_specs=(P("dp", seq, None), P(seq, "dp")),
        check_vma=False,
    )
```

time: 120 us -> 100 us (0.83)
  waiting for transfers between devices: 60.5 us -> 19.5 us
  blocking collectives: 0 us -> 33.8 us
  starting transfers between devices: 28.6 us -> 17.2 us
  Pallas kernels: 18.9 us -> 26 us
  local copies, waits for them, and re-layouts: 7.02 us -> 0.26 us
  other arithmetic: 3.1 us -> 1.4 us
    all_to_all x0 -> x1, blocking collectives: none -> 33.8 us  [body(): lax.all_to_all(merged.reshape(SLOTS, 40, WIDE), ('y', 'z'), split_axis=0,...]
    all_to_all x2 -> x0, waiting for transfers between devices: 30.6 us -> none  [the longest x1 18 us: body(): lax.all_to_all(partial, ('y', 'z'), split_axis=0, concat_axis=0, tiled=True)]
    all_to_all x2 -> x0, starting transfers between devices: 11.2 us -> none  [the longest x1 6.63 us: body(): lax.all_to_all(d_rows.reshape(SLOTS, PATCHES, D), ('y', 'z'), split_axis=...]
    pallas_call x4 -> x7, Pallas kernels: 18.9 us -> 26 us  [call(): pl.pallas_call(kernel, out_shape=out_shape, in_specs=specs, out_specs=jax...]
    unnamed x14 -> x2, local copies, waits for them, and re-layouts: 5.2 us -> 0.01 us
    ppermute x1, waiting for transfers between devices: 5.2 us -> 0.01 us  [body(): from_one = lax.ppermute(one, 'dp', ring(1))]
    ppermute x1, waiting for transfers between devices: 6.72 us -> 2.36 us  [body(): from_two = lax.ppermute(two, 'dp', ring(2))]
    convert_element_type x2, other arithmetic: 2.35 us -> 0.71 us  [chosen_rows(): (target[:, None] == jnp.arange(D, dtype=jnp.int32)[None, :]).astype(BF)]
  transfers between devices with their start and end apart: 7 -> 5, of which waited for: 5 -> 2; matrix products, arithmetic and copies ran while one was open for 4% -> 2% of each run, Pallas kernels for 7% -> 13%
where the time goes in v2:
time: 100 us; the launch traced here: 99.5 us
  blocking collectives  33.8 us (34%)
  Pallas kernels  26 us (26%)
  waiting for transfers between devices  19.5 us (20%)
  starting transfers between devices  17.2 us (17%)
  other arithmetic  1.4 us (1%)
  between operations  1.38 us (1%)
    all_to_all x1, blocking collectives, body(): lax.all_to_all(merged.reshape(SLOTS, 40, WIDE), ('y', 'z'), split_axis=0,...  33.8 us
    pallas_call x7, Pallas kernels, call(): pl.pallas_call(kernel, out_shape=out_shape, in_specs=specs, out_specs=jax...  26 us
    all_to_all x1, waiting for transfers between devices, body(): lax.all_to_all(packed.reshape(SLOTS, 8, D), ('y', 'z'), split_axis=0, con...  17.1 us
    all_to_all x1, starting transfers between devices, body(): lax.all_to_all(packed.reshape(SLOTS, 8, D), ('y', 'z'), split_axis=0, con...  11.4 us
    ppermute x1, starting transfers between devices, body(): from_two = lax.ppermute(two, 'dp', ring(2))  2.73 us
    ppermute x1, waiting for transfers between devices, body(): from_two = lax.ppermute(two, 'dp', ring(2))  2.36 us
  transfers between devices with their start and end apart: 5, of which 2 were waited for; matrix products, arithmetic and copies ran while one was open for 2% of the time, Pallas kernels for 13%

profile of v2, /device:TPU:32, one launch (start us, length us, event | category | flops | bytes accessed | tf_op | source)
XLA Modules:
  0.0 99.5 jit_solution(1471769922440615811)
XLA Ops:
  0.6 2.2 %shard_map.77 = bf16[256,1152]{1,0:T(8,128)(2,1)} custom-call(bf16[128,1152]{1,0:T(8,128)(2,1)} %bitcast.16, bf16[128,1152]{1,0:T(8,128)(2,1)} %bitcast.17), custom_call_target="tpu_custom_call" | custom-call | tf_op jit(solution)/shard_map/pallas_call | solution.py:43
  2.9 11.4 %all-to-all-start = ((bf16[32,8,1152]{2,1,0:T(8,128)(2,1)}), bf16[32,8,1152]{2,1,0:T(8,128)(2,1)S(1)}, u32[]{:S(2)}, u32[]{:S(2)}) async-start(bf16[32,8,1152]{2,1,0:T(8,128)(2,1)} %bitcast.15), calls=%async_computation | async-start | bytes 1179648 | tf_op jit(solution)/shard_map/all_to_all | solution.py:285
  14.9 0.7 fusion.9
  15.6 0.1 broadcast_in_dim.7
  15.6 0.1 broadcast_in_dim_reshape.8.live_row_ref
  15.7 0.1 broadcast_in_dim_reshape.7.live_col_ref
  15.8 0.4 fusion.1.chosen_ref
  16.2 17.1 %all-to-all-done = bf16[32,8,1152]{2,1,0:T(8,128)(2,1)S(1)} async-done(((bf16[32,8,1152]{2,1,0:T(8,128)(2,1)}), bf16[32,8,1152]{2,1,0:T(8,128)(2,1)S(1)}, u32[]{:S(2)}, u32[]{:S(2)}) %all-to-all-start) | async-done | bytes 589856 | tf_op jit(solution)/shard_map/all_to_all | solution.py:285
  33.3 0.0 copy-start
  33.3 8.4 %shard_map.78 = (bf16[128,1152]{1,0:T(8,128)(2,1)S(1)}, bf16[128,1152]{1,0:T(8,128)(2,1)S(1)}, bf16[128,3456]{1,0:T(8,128)(2,1)S(1)}, f32[16,128,128]{2,1,0:T(8,...) custom-call(s32[1]{0:T(128)} %bitcast.place_ref, ...), custom_call_target="tpu_custom_call" | custom-call | flops 2000000000 | bytes 14000000 | tf_op jit(solution)/shard_map/pallas_call | solution.py:43
  41.7 1.6 %collective-permute-start = (bf16[1536,128]{1,0:T(8,128)(2,1)S(1)}, bf16[1536,128]{1,0:T(8,128)(2,1)S(1)}, u32[]{:S(2)}, u32[]{:S(2)}) collective-permute-start(bf16[1536,128]{1,0:T(8,128)(2,1)S(1)} %get-tuple-element.17), channel_id=1, source_target_pairs={{0,64},{64,128},{128,192},{192,0},{1,65},{65,129},{129,193},{193,1... | collective-permute-start | bytes 1179656 | tf_op jit(solution)/shard_map/ppermute | solution.py:311
  43.2 2.7 %collective-permute-start.1 = (bf16[1536,128]{1,0:T(8,128)(2,1)S(1)}, bf16[1536,128]{1,0:T(8,128)(2,1)S(1)}, u32[]{:S(2)}, u32[]{:S(2)}) collective-permute-start(bf16[1536,128]{1,0:T(8,128)(2,1)S(1)} %get-tuple-element.18), channel_id=1, source_target_pairs={{0,128},{64,192},{128,0},{192,64},{1,129},{65,193},{129,1},{193,65... | collective-permute-start | bytes 1179656 | tf_op jit(solution)/shard_map/ppermute | solution.py:312
  46.0 1.4 %collective-permute-start.2 = (bf16[1536,128]{1,0:T(8,128)(2,1)S(1)}, bf16[1536,128]{1,0:T(8,128)(2,1)S(1)}, u32[]{:S(2)}, u32[]{:S(2)}) collective-permute-start(bf16[1536,128]{1,0:T(8,128)(2,1)S(1)} %get-tuple-element.19), channel_id=1, source_target_pairs={{0,192},{64,0},{128,64},{192,128},{1,193},{65,1},{129,65},{193,129... | collective-permute-start | bytes 1179656 | tf_op jit(solution)/shard_map/ppermute | solution.py:313
  47.4 0.0 copy-done
  47.4 10.9 %shard_map.79.after_ref.rows_ref = bf16[512,384]{1,0:T(8,128)(2,1)S(1)} custom-call(bf16[128,1152]{1,0:T(8,128)(2,1)S(1)} %get-tuple-element.12.tokens_ref, bf16[128,1152]{1,0:T(8,128)(2,1)S(1)} %get-tuple-element.13.masked_ref, bf16[128,3456]{1,0:T(8,128)(2,1)S(1)} %get-tuple-element.14.joined_ref, f32[16,128,128]{2,1,0:T(8,128)S(1)} %get-tuple-element.15.probs_ref, ...), custom_call_target="tpu_custom_call" | custom-call | flops 3000000000 | bytes 16000000 | tf_op jit(solution)/shard_map/pallas_call | solution.py:43
  58.4 0.0 collective-permute-done.one_ref
  58.4 2.4 %collective-permute-done.1.two_ref = bf16[1536,128]{1,0:T(8,128)(2,1)S(1)} collective-permute-done((bf16[1536,128]{1,0:T(8,128)(2,1)S(1)}, bf16[1536,128]{1,0:T(8,128)(2,1)S(1)}, u32[]{:S(2)}, u32[]{:S(2)}) %collective-permute-start.1) | collective-permute-done | bytes 393248 | tf_op jit(solution)/shard_map/ppermute | solution.py:312
  60.7 0.0 collective-permute-done.2.three_ref
  60.7 1.6 %shard_map.80.after_ref = bf16[768,384]{1,0:T(8,128)(2,1)S(1)} custom-call(bf16[1536,128]{1,0:T(8,128)(2,1)S(1)} %get-tuple-element.16.own_ref, bf16[1536,128]{1,0:T(8,128)(2,1)S(1)} %collective-permute-done.one_ref, bf16[1536,128]{1,0:T(8,128)(2,1)S(1)} %collective-permute-done.1.two_ref, bf16[1536,128]{1,0:T(8,128)(2,1)S(1)} %collective-permute-done.2.three_ref, ...), custom_call_target="tpu_custom_call" | custom-call | flops 1000000000 | bytes 4000000 | tf_op jit(solution)/shard_map/pallas_call | solution.py:43
  62.3 0.1 collective-permute-start.3
  62.4 0.4 fusion.chosen_ref
  62.8 1.6 %shard_map.81.keep_ref = f32[768,384]{1,0:T(8,128)S(1)} custom-call(bf16[1536,128]{1,0:T(8,128)(2,1)S(1)} %get-tuple-element.16.own_ref, bf16[1536,128]{1,0:T(8,128)(2,1)S(1)} %collective-permute-done.one_ref, bf16[1536,128]{1,0:T(8,128)(2,1)S(1)} %collective-permute-done.1.two_ref, bf16[1536,128]{1,0:T(8,128)(2,1)S(1)} %collective-permute-done.2.three_ref, ...), custom_call_target="tpu_custom_call" | custom-call | flops 1000000000 | bytes 4000000 | tf_op jit(solution)/shard_map/pallas_call | solution.py:43
  64.4 0.0 collective-permute-done.3.got_ref
  64.4 0.1 shard_map.82
  64.5 33.8 %all_to_all.10 = bf16[32,40,384]{2,1,0:T(8,128)(2,1)S(1)} all-to-all(bf16[32,40,384]{2,1,0:T(8,128)(2,1)S(1)} %bitcast.12), channel_id=1, replica_groups=mesh['dp'=4,'y'=4,'z'=8,'core'=2] {'y','z'}, dimensions={0} | all-to-all | bytes 1966080 | tf_op jit(solution)/shard_map/all_to_all | solution.py:349
  98.3 1.1 %shard_map.83 = (bf16[128,1152]{1,0:T(8,128)(2,1)}, f32[18,288]{1,0:T(8,128)}) custom-call(bf16[1280,384]{1,0:T(8,128)(2,1)S(1)} %bitcast.13), custom_call_target="tpu_custom_call" | custom-call | tf_op jit(solution)/shard_map/pallas_call | solution.py:43
  (2 shorter events, 0.0 us)
Async XLA Ops:
  2.9 30.4 %all-to-all-start = ((bf16[32,8,1152]{2,1,0:T(8,128)(2,1)}), bf16[32,8,1152]{2,1,0:T(8,128)(2,1)S(1)}, u32[]{:S(2)}, u32[]{:S(2)}) async-start(bf16[32,8,1152]{2,1,0:T(8,128)(2,1)} %bitcast.15), calls=%async_computation | async-start | bytes 1179648 | tf_op jit(solution)/shard_map/all_to_all | solution.py:285
  33.3 14.2 %copy-start = (bf16[1152,1152]{1,0:T(8,128)(2,1)S(1)}, bf16[1152,1152]{1,0:T(8,128)(2,1)}, u32[]{:S(2)}) copy-start(bf16[1152,1152]{1,0:T(8,128)(2,1)} %w_out_ref.1) | copy-start | bytes 7962628
  41.7 16.7 %collective-permute-start = (bf16[1536,128]{1,0:T(8,128)(2,1)S(1)}, bf16[1536,128]{1,0:T(8,128)(2,1)S(1)}, u32[]{:S(2)}, u32[]{:S(2)}) collective-permute-start(bf16[1536,128]{1,0:T(8,128)(2,1)S(1)} %get-tuple-element.17), channel_id=1, source_target_pairs={{0,64},{64,128},{128,192},{192,0},{1,65},{65,129},{129,193},{193,1... | collective-permute-start | bytes 1179656 | tf_op jit(solution)/shard_map/ppermute | solution.py:311
  43.2 17.5 %collective-permute-start.1 = (bf16[1536,128]{1,0:T(8,128)(2,1)S(1)}, bf16[1536,128]{1,0:T(8,128)(2,1)S(1)}, u32[]{:S(2)}, u32[]{:S(2)}) collective-permute-start(bf16[1536,128]{1,0:T(8,128)(2,1)S(1)} %get-tuple-element.18), channel_id=1, source_target_pairs={{0,128},{64,192},{128,0},{192,64},{1,129},{65,193},{129,1},{193,65... | collective-permute-start | bytes 1179656 | tf_op jit(solution)/shard_map/ppermute | solution.py:312
  46.0 14.8 %collective-permute-start.2 = (bf16[1536,128]{1,0:T(8,128)(2,1)S(1)}, bf16[1536,128]{1,0:T(8,128)(2,1)S(1)}, u32[]{:S(2)}, u32[]{:S(2)}) collective-permute-start(bf16[1536,128]{1,0:T(8,128)(2,1)S(1)} %get-tuple-element.19), channel_id=1, source_target_pairs={{0,192},{64,0},{128,64},{192,128},{1,193},{65,1},{129,65},{193,129... | collective-permute-start | bytes 1179656 | tf_op jit(solution)/shard_map/ppermute | solution.py:313
  62.3 2.1 %collective-permute-start.3 = (bf16[768,384]{1,0:T(8,128)(2,1)S(1)}, bf16[768,384]{1,0:T(8,128)(2,1)S(1)}, u32[]{:S(2)}, u32[]{:S(2)}) collective-permute-start(bf16[768,384]{1,0:T(8,128)(2,1)S(1)} %shard_map.80.after_ref), channel_id=1, source_target_pairs={{0,1},{1,0},{2,3},{3,2},{4,5},{5,4},{6,7},{7,6},{8,9},{9,8},{10,11... | collective-permute-start | bytes 1769480 | tf_op jit(solution)/shard_map/ppermute | solution.py:339

commit v3 on v2

v3 whole, which is shorter than its diff:
```python
import math

import jax
import jax.numpy as jnp
from jax import lax
from jax.experimental import pallas as pl
from jax.experimental.pallas import tpu as pltpu
from jax.sharding import Mesh, PartitionSpec as P

H = 16
D = 1152
E = D // H
SLOTS = 32
PATCHES = 4
ROWS = SLOTS * PATCHES
SCALE = 1.0 / math.sqrt(E)
BF = jnp.bfloat16
F32 = jnp.float32
MIB = 1024 * 1024
COLS = 288
WIDE = 384
OUT_ROWS = 18
CHUNK = 80
TOKEN_ROWS = 36
PAYLOAD = D + COLS
EXP_SCALE = SCALE * math.log2(math.e)

NN = (((1,), (0,)), ((), ()))
NT = (((1,), (1,)), ((), ()))
TN = (((0,), (0,)), ((), ()))


def dot(a, b, dims=NN):
    return lax.dot_general(a, b, dims, preferred_element_type=F32)


def whole():
    return pl.BlockSpec(memory_space=pltpu.VMEM)


def call(kernel, out_shape, inputs, scratch=(), limit=32, flops=0, data=0, smem=(), far=()):
    spaces = {i: pltpu.SMEM for i in smem} | {i: pl.ANY for i in far}
    specs = [
        pl.BlockSpec(memory_space=spaces.get(i, pltpu.VMEM)) for i in range(len(inputs))
    ]
    return pl.pallas_call(
        kernel,
        out_shape=out_shape,
        in_specs=specs,
        out_specs=jax.tree.map(lambda _: whole(), out_shape),
        scratch_shapes=list(scratch),
        compiler_params=pltpu.CompilerParams(vmem_limit_bytes=limit * MIB),
        cost_estimate=pl.CostEstimate(flops=flops, bytes_accessed=data, transcendentals=0),
    )(*inputs)


def pick(shape, target, along):
    return (lax.broadcasted_iota(jnp.int32, shape, along) == target).astype(F32).astype(BF)


def row_index(rows):
    return lax.broadcasted_iota(jnp.int32, (rows, 1), 0)


def lane_index(lanes):
    return lax.broadcasted_iota(jnp.int32, (1, lanes), 1)


def source_row(packed):
    inner = packed % 8
    return packed // 8 * PATCHES + inner % PATCHES + jnp.where(inner >= PATCHES, ROWS, 0)


def patch_row(packed):
    inner = packed % 8
    return packed // 8 + inner % PATCHES * SLOTS + jnp.where(inner >= PATCHES, ROWS, 0)


def pack_kernel(tokens_ref, d_out_ref, packed_ref, both_ref, sems):
    copies = [
        pltpu.make_async_copy(ref, both_ref.at[pl.ds(i * ROWS, ROWS)], sems.at[i])
        for i, ref in enumerate((tokens_ref, d_out_ref))
    ]
    for copy in copies:
        copy.start()
    chooser = pick((256, 256), source_row(row_index(256)), 1)
    for copy in copies:
        copy.wait()
    packed_ref[...] = dot(chooser, both_ref[...]).astype(BF)


def row_stats(tokens):
    values = tokens.astype(F32)
    center = values - jnp.mean(values, axis=-1, keepdims=True)
    spread = jnp.mean(center * center, axis=-1, keepdims=True)
    inverse = lax.rsqrt(spread + 1e-06)
    return center * inverse, inverse


def window(head):
    low = head * E
    base = low // 128 * 128
    width = 128 if low + E <= base + 128 else 256
    lane = lax.broadcasted_iota(jnp.int32, (ROWS, width), 1)
    inside = (lane >= low - base) & (lane < low - base + E)
    return base, width, inside


def only(inside, array):
    return jnp.where(inside, array, jnp.zeros_like(array))


def lane_patch():
    return lax.broadcasted_iota(jnp.int32, (SLOTS, ROWS), 1) // SLOTS


def diagonal(full, patch):
    packed = full[:SLOTS]
    for p in range(1, PATCHES):
        packed = jnp.where(patch == p, full[p * SLOTS : (p + 1) * SLOTS], packed)
    return packed


def spread(packed, patch):
    blocks = [jnp.where(patch == p, packed, 0.0) for p in range(PATCHES)]
    return jnp.concatenate(blocks, axis=0).astype(BF)


def forward_kernel(
    place_ref, packed_ref, live_ref, w_qkv_ref,
    tokens_ref, masked_ref, joined_ref, probs_ref, own_ref, one_ref, two_ref, three_ref,
    turned_ref, values_ref, attended_ref, weight_ref, sems,
):
    spans = [pl.ds(kind * D + chunk * WIDE, WIDE) for chunk in range(3) for kind in range(3)]
    copies = [
        pltpu.make_async_copy(w_qkv_ref.at[:, span], weight_ref.at[:, span], sems.at[i])
        for i, span in enumerate(spans)
    ]
    for copy in copies:
        copy.start()
    plain = dot(pick((256, 256), patch_row(lane_index(256)), 0), packed_ref[...])
    tokens = plain[:ROWS].astype(BF)
    tokens_ref[...] = tokens
    normalized, _ = row_stats(tokens)
    normed = normalized.astype(BF)
    live = live_ref[...]
    masked = plain[ROWS:] * jnp.concatenate([live] * PATCHES, axis=0)
    masked_ref[...] = masked.astype(BF)
    for block in range(9):
        lanes = slice(block * 128, (block + 1) * 128)
        turned_ref[lanes, :] = masked[:, lanes].T.astype(BF)
    me = place_ref[0]
    sends = (own_ref, one_ref, two_ref, three_ref)
    for step, out_ref in enumerate(sends):
        start = pl.multiple_of((me + step) % 4 * COLS, 16)
        out_ref[D:, :] = turned_ref[pl.ds(start, COLS), :]
    patch = lane_patch()
    done = 0
    for chunk in range(3):
        for kind in range(3):
            copies[chunk * 3 + kind].wait()
            columns = slice(kind * D + chunk * WIDE, kind * D + (chunk + 1) * WIDE)
            product = dot(normed, weight_ref[:, columns])
            joined_ref[:, columns] = product.astype(BF)
            if kind == 2:
                for block in range(3):
                    at = chunk * WIDE + block * 128
                    values_ref[at : at + 128, :] = product[:, block * 128 : (block + 1) * 128].T
        while done < H and window(done)[0] + window(done)[1] <= (chunk + 1) * WIDE:
            head = done
            done += 1
            base, width, inside = window(head)
            queries = only(inside, joined_ref[:, base : base + width])
            keys_in = joined_ref[:, D + base : D + base + width]
            scores = diagonal(dot(keys_in, queries, NT), patch)
            scores = jnp.where(live > 0.5, scores, -1e30)
            top = jnp.max(scores, axis=0, keepdims=True)
            exponent = jnp.exp2((scores - top) * EXP_SCALE)
            probs = exponent / jnp.sum(exponent, axis=0, keepdims=True)
            probs_ref[head] = probs
            rows = slice(head * E, (head + 1) * E)
            attended_ref[rows, :] = dot(values_ref[rows, :].astype(BF), spread(probs, patch))
    attended = attended_ref[...].astype(BF)
    for out_ref in sends:
        out_ref[:D, :] = attended


def backward_kernel(
    tokens_ref, masked_ref, joined_ref, probs_ref, w_qkv_ref, w_out_ref,
    packed_ref, place_ref,
    grad_ref, head_ref, weight_ref, out_weight_ref, sems,
):
    out_copies = [
        pltpu.make_async_copy(
            w_out_ref.at[pl.ds(chunk * WIDE, WIDE)],
            out_weight_ref.at[pl.ds(chunk * WIDE, WIDE)],
            sems.at[chunk],
        )
        for chunk in range(3)
    ]
    qkv_copies = [
        pltpu.make_async_copy(
            w_qkv_ref.at[pl.ds(chunk * WIDE, WIDE)],
            weight_ref.at[pl.ds(chunk * WIDE, WIDE)],
            sems.at[3 + chunk],
        )
        for chunk in range(3)
    ]
    for copy in out_copies + qkv_copies:
        copy.start()
    term = lane_index(3 * 8 * OUT_ROWS)
    kind, inner = term // (8 * OUT_ROWS), term % (8 * OUT_ROWS)
    row = inner % OUT_ROWS
    at = TOKEN_ROWS + kind * OUT_ROWS + jnp.where(kind == 2, row // 4, row)
    place_ref[...] = pick((8 * CHUNK, 3 * 8 * OUT_ROWS), inner // OUT_ROWS * CHUNK + at, 0)
    masked = masked_ref[...]
    for chunk in range(3):
        columns = slice(chunk * WIDE, (chunk + 1) * WIDE)
        out_copies[chunk].wait()
        head_ref[:, columns] = dot(masked, out_weight_ref[columns, :], NT).astype(BF)
    patch = lane_patch()
    for head in range(H):
        base, width, inside = window(head)
        queries = only(inside, joined_ref[:, base : base + width])
        keys_in = joined_ref[:, D + base : D + base + width]
        values = joined_ref[:, 2 * D + base : 2 * D + base + width]
        head_grad = only(inside, head_ref[:, base : base + width])
        probs = probs_ref[head]
        prob_grad = diagonal(dot(values, head_grad, NT), patch)
        inner_sum = jnp.sum(probs * prob_grad, axis=0, keepdims=True)
        score_grad = spread(probs * (prob_grad - inner_sum) * SCALE, patch)
        parts = (
            dot(score_grad, keys_in, TN).astype(BF),
            dot(score_grad, queries).astype(BF),
            dot(spread(probs, patch), head_grad).astype(BF),
        )
        for index, part in enumerate(parts):
            at = index * D + base
            if head == 0:
                grad_ref[:, at : at + width] = part
            else:
                grad_ref[:, at : at + width] = jnp.where(inside, part, grad_ref[:, at : at + width])
    pieces = []
    for chunk in range(3):
        qkv_copies[chunk].wait()
        rows = slice(chunk * WIDE, (chunk + 1) * WIDE)
        pieces.append(dot(grad_ref[...], weight_ref[rows, :], NT))
    normed_grad = jnp.concatenate(pieces, axis=1)
    normalized, inverse = row_stats(tokens_ref[...])
    mean_grad = jnp.mean(normed_grad, axis=-1, keepdims=True)
    mean_cross = jnp.mean(normed_grad * normalized, axis=-1, keepdims=True)
    d_tokens = (
        masked.astype(F32) + inverse * (normed_grad - mean_grad - normalized * mean_cross)
    ).astype(BF)
    piece = lane_index(576)
    target = piece % 16 * CHUNK + piece // 64 * PATCHES + piece % 64 // 16
    chooser = pick((16 * CHUNK, 576), target, 0)
    for half in range(2):
        stacked = jnp.concatenate(
            [
                d_tokens[p * SLOTS + half * 16 : p * SLOTS + half * 16 + 16, c * 128 : (c + 1) * 128]
                for c in range(9)
                for p in range(PATCHES)
            ],
            axis=0,
        )
        packed_ref[half * 16 * CHUNK : (half + 1) * 16 * CHUNK, :] = dot(chooser, stacked).astype(BF)


def weight_kernel(own_ref, one_ref, two_ref, three_ref, chosen_ref, after_ref, terms_ref):
    refs = (own_ref, one_ref, two_ref, three_ref)
    attended = jnp.concatenate([ref[:D, :] for ref in refs], axis=1)
    masked = jnp.concatenate([ref[D:, :] for ref in refs], axis=1)
    masked = jnp.concatenate([masked[:256]] + [masked[256:]] * 4, axis=0)
    chosen = dot(chosen_ref[...], attended).astype(BF)
    terms_ref[...] = dot(chosen, masked, NT).astype(terms_ref.dtype)


def merge_kernel(rows_ref, keep_ref, got_ref, place_ref, merged_ref):
    terms = keep_ref[...] + got_ref[...].astype(F32)
    row = row_index(SLOTS * OUT_ROWS) % OUT_ROWS
    last = jnp.where(row % 4 == lane_index(128) // 32, terms[:, 256:], 0.0)
    blocks = [block.astype(BF) for block in (terms[:, :128], terms[:, 128:256], last)]
    for group in range(4):
        rows = slice(group * 8 * OUT_ROWS, (group + 1) * 8 * OUT_ROWS)
        stacked = jnp.concatenate([block[rows] for block in blocks], axis=0)
        out = slice(group * 8 * CHUNK, (group + 1) * 8 * CHUNK)
        merged_ref[out, :] = (
            dot(place_ref[...], stacked) + rows_ref[out, :].astype(F32)
        ).astype(BF)


def unpack_kernel(merged_ref, d_tokens_ref, d_w_ref, total_ref):
    piece = row_index(288)
    row = piece % 32
    source = row // PATCHES * CHUNK + piece // 32 * PATCHES + row % PATCHES
    chooser = pick((288, 8 * CHUNK), source, 1)
    for group in range(4):
        rows = dot(chooser, merged_ref[group * 8 * CHUNK : (group + 1) * 8 * CHUNK, :]).astype(BF)
        for block in range(9):
            d_tokens_ref[group * 32 : (group + 1) * 32, block * 128 : (block + 1) * 128] = rows[
                block * 32 : (block + 1) * 32
            ]
    merged = merged_ref[...].astype(F32).reshape(SLOTS, CHUNK, 128)
    total_ref[...] = jnp.sum(merged[:, 32:], axis=0)
    first = TOKEN_ROWS - 32
    d_w_ref[:, :128] = total_ref[first : first + OUT_ROWS, :]
    d_w_ref[:, 128:256] = total_ref[first + OUT_ROWS : first + 2 * OUT_ROWS, :]
    for row in range(OUT_ROWS):
        at = first + 2 * OUT_ROWS + row // 4
        lanes = slice(row % 4 * 32, row % 4 * 32 + 32)
        d_w_ref[row : row + 1, 256:] = total_ref[at : at + 1, lanes]


def chosen_rows(core):
    at = jnp.arange(SLOTS * OUT_ROWS, dtype=jnp.int32)
    target = at // OUT_ROWS * (2 * OUT_ROWS) + core * OUT_ROWS + at % OUT_ROWS
    return (target[:, None] == jnp.arange(D, dtype=jnp.int32)[None, :]).astype(BF)


def body(tokens, d_out, frames, frame_order, w_qkv, w_out):
    place = lax.axis_index("dp")
    core = lax.axis_index("core")
    shape = jax.ShapeDtypeStruct
    live = (frame_order[0] < frames[0]).astype(F32)
    packed = call(
        pack_kernel,
        shape((256, D), BF),
        (tokens[0], d_out[0]),
        scratch=(pltpu.VMEM((256, D), BF), pltpu.SemaphoreType.DMA((2,))),
        limit=60,
        far=(0, 1),
    )
    arrived = lax.all_to_all(
        packed.reshape(SLOTS, 8, D), ("y", "z"), split_axis=0, concat_axis=0, tiled=True
    ).reshape(256, D)
    kept, masked, joined, probs, own, one, two, three = call(
        forward_kernel,
        (
            shape((ROWS, D), BF),
            shape((ROWS, D), BF),
            shape((ROWS, 3 * D), BF),
            shape((H, SLOTS, ROWS), F32),
        )
        + (shape((PAYLOAD, ROWS), BF),) * 4,
        (place.reshape(1), arrived, live[:, None], w_qkv),
        scratch=(
            pltpu.VMEM((D, ROWS), BF),
            pltpu.VMEM((D, ROWS), F32),
            pltpu.VMEM((D, ROWS), F32),
            pltpu.VMEM((D, 3 * D), BF),
            pltpu.SemaphoreType.DMA((9,)),
        ),
        smem=(0,),
        far=(3,),
        limit=47,
        flops=int(2e9),
        data=int(14e6),
    )
    ring = lambda step: [(i, (i + step) % 4) for i in range(4)]
    from_one = lax.ppermute(one, "dp", ring(1))
    from_two = lax.ppermute(two, "dp", ring(2))
    from_three = lax.ppermute(three, "dp", ring(3))
    rows, places = call(
        backward_kernel,
        (shape((SLOTS * CHUNK, 128), BF), shape((8 * CHUNK, 3 * 8 * OUT_ROWS), BF)),
        (kept, masked, joined, probs, w_qkv, w_out),
        scratch=(
            pltpu.VMEM((ROWS, 3 * D), BF),
            pltpu.VMEM((ROWS, D), BF),
            pltpu.VMEM((D, 3 * D), BF),
            pltpu.VMEM((D, D), BF),
            pltpu.SemaphoreType.DMA((6,)),
        ),
        far=(4, 5),
        limit=47,
        flops=int(3e9),
        data=int(16e6),
    )
    payloads = (own, from_one, from_two, from_three)
    send = call(
        weight_kernel,
        shape((SLOTS * OUT_ROWS, WIDE), BF),
        payloads + (chosen_rows(1 - core), rows),
        far=(5,),
        flops=int(1e9),
        data=int(4e6),
    )
    got = lax.ppermute(send, "core", [(0, 1), (1, 0)])
    keep = call(
        weight_kernel,
        shape((SLOTS * OUT_ROWS, WIDE), F32),
        payloads + (chosen_rows(core), send),
        far=(5,),
        flops=int(1e9),
        data=int(4e6),
    )
    merged = call(
        merge_kernel, shape((SLOTS * CHUNK, 128), BF), (rows, keep, got, places), limit=16
    )
    returned = lax.all_to_all(
        merged.reshape(SLOTS, CHUNK, 128), ("y", "z"), split_axis=0, concat_axis=0, tiled=True
    ).reshape(SLOTS * CHUNK, 128)
    d_tokens, d_w = call(
        unpack_kernel,
        (shape((ROWS, D), BF), shape((OUT_ROWS, COLS), F32)),
        (returned,),
        scratch=(pltpu.VMEM((CHUNK - 32, 128), F32),),
        limit=16,
    )
    return d_tokens[None], d_w


def solution(mesh):
    fine = Mesh(mesh.devices.reshape(4, 4, 8, 2), ("dp", "y", "z", "core"))
    seq = ("y", "z", "core")
    placed = (P("dp", seq, None), P("dp", seq, None), P("dp"), P("dp", None), P(), P())
    return jax.shard_map(
        body,
        mesh=fine,
        in_specs=placed,
        out_specs=(P("dp", seq, None), P(seq, "dp")),
        check_vma=False,
    )
```

time: 100 us -> 91.3 us (0.913)
  blocking collectives: 33.8 us -> 27.2 us
  Pallas kernels: 26 us -> 24.7 us
    all_to_all x1, blocking collectives: 33.8 us -> 27.2 us  [body(): lax.all_to_all(merged.reshape(SLOTS, CHUNK, 128), ('y', 'z'), split_axis=...]
    pallas_call x7, Pallas kernels: 26 us -> 24.7 us  [call(): pl.pallas_call(kernel, out_shape=out_shape, in_specs=specs, out_specs=jax...]
  transfers between devices with their start and end apart: 5 -> 5, of which waited for: 2 -> 3; matrix products, arithmetic and copies ran while one was open for 2% -> 1% of each run, Pallas kernels for 13% -> 13%
where the time goes in v3:
time: 91.3 us; the launch traced here: 91 us
  blocking collectives  27.2 us (30%)
  Pallas kernels  24.7 us (27%)
  waiting for transfers between devices  19.2 us (21%)
  starting transfers between devices  17.2 us (19%)
  between operations  1.38 us (2%)
  other arithmetic  1.26 us (1%)
    all_to_all x1, blocking collectives, body(): lax.all_to_all(merged.reshape(SLOTS, CHUNK, 128), ('y', 'z'), split_axis=...  27.2 us
    pallas_call x7, Pallas kernels, call(): pl.pallas_call(kernel, out_shape=out_shape, in_specs=specs, out_specs=jax...  24.7 us
    all_to_all x1, waiting for transfers between devices, body(): lax.all_to_all(packed.reshape(SLOTS, 8, D), ('y', 'z'), split_axis=0, con...  17.3 us
    all_to_all x1, starting transfers between devices, body(): lax.all_to_all(packed.reshape(SLOTS, 8, D), ('y', 'z'), split_axis=0, con...  11.4 us
    ppermute x1, starting transfers between devices, body(): from_two = lax.ppermute(two, 'dp', ring(2))  2.72 us
  transfers between devices with their start and end apart: 5, of which 3 were waited for; matrix products, arithmetic and copies ran while one was open for 1% of the time, Pallas kernels for 13%

profile of v3, /device:TPU:32, one launch (start us, length us, event | category | flops | bytes accessed | tf_op | source)
XLA Modules:
  0.0 91.0 jit_solution(444184513354117446)
XLA Ops:
  0.6 2.2 %shard_map.77 = bf16[256,1152]{1,0:T(8,128)(2,1)} custom-call(bf16[128,1152]{1,0:T(8,128)(2,1)} %bitcast.16, bf16[128,1152]{1,0:T(8,128)(2,1)} %bitcast.17), custom_call_target="tpu_custom_call" | custom-call | tf_op jit(solution)/shard_map/pallas_call | solution.py:46
  2.9 11.4 %all-to-all-start = ((bf16[32,8,1152]{2,1,0:T(8,128)(2,1)}), bf16[32,8,1152]{2,1,0:T(8,128)(2,1)S(1)}, u32[]{:S(2)}, u32[]{:S(2)}) async-start(bf16[32,8,1152]{2,1,0:T(8,128)(2,1)} %bitcast.15), calls=%async_computation | async-start | bytes 1179648 | tf_op jit(solution)/shard_map/all_to_all | solution.py:334
  14.9 0.7 fusion.12
  15.6 0.1 copy.8.live_ref
  15.7 0.3 fusion.1.chosen_ref
  16.0 17.3 %all-to-all-done = bf16[32,8,1152]{2,1,0:T(8,128)(2,1)S(1)} async-done(((bf16[32,8,1152]{2,1,0:T(8,128)(2,1)}), bf16[32,8,1152]{2,1,0:T(8,128)(2,1)S(1)}, u32[]{:S(2)}, u32[]{:S(2)}) %all-to-all-start) | async-done | bytes 589856 | tf_op jit(solution)/shard_map/all_to_all | solution.py:334
  33.3 0.0 copy-start
  33.3 7.3 %shard_map.78 = (bf16[128,1152]{1,0:T(8,128)(2,1)S(1)}, bf16[128,1152]{1,0:T(8,128)(2,1)S(1)}, bf16[128,3456]{1,0:T(8,128)(2,1)S(1)}, f32[16,32,128]{2,1,0:T(8,1...) custom-call(s32[1]{0:T(128)} %bitcast.place_ref, ...), custom_call_target="tpu_custom_call" | custom-call | flops 2000000000 | bytes 14000000 | tf_op jit(solution)/shard_map/pallas_call | solution.py:46
  40.6 1.6 %collective-permute-start = (bf16[1440,128]{1,0:T(8,128)(2,1)S(1)}, bf16[1440,128]{1,0:T(8,128)(2,1)S(1)}, u32[]{:S(2)}, u32[]{:S(2)}) collective-permute-start(bf16[1440,128]{1,0:T(8,128)(2,1)S(1)} %get-tuple-element.20), channel_id=1, source_target_pairs={{0,64},{64,128},{128,192},{192,0},{1,65},{65,129},{129,193},{193,1... | collective-permute-start | bytes 1105928 | tf_op jit(solution)/shard_map/ppermute | solution.py:361
  42.1 2.7 %collective-permute-start.1 = (bf16[1440,128]{1,0:T(8,128)(2,1)S(1)}, bf16[1440,128]{1,0:T(8,128)(2,1)S(1)}, u32[]{:S(2)}, u32[]{:S(2)}) collective-permute-start(bf16[1440,128]{1,0:T(8,128)(2,1)S(1)} %get-tuple-element.21), channel_id=1, source_target_pairs={{0,128},{64,192},{128,0},{192,64},{1,129},{65,193},{129,1},{193,65... | collective-permute-start | bytes 1105928 | tf_op jit(solution)/shard_map/ppermute | solution.py:362
  44.9 1.4 %collective-permute-start.2 = (bf16[1440,128]{1,0:T(8,128)(2,1)S(1)}, bf16[1440,128]{1,0:T(8,128)(2,1)S(1)}, u32[]{:S(2)}, u32[]{:S(2)}) collective-permute-start(bf16[1440,128]{1,0:T(8,128)(2,1)S(1)} %get-tuple-element.22), channel_id=1, source_target_pairs={{0,192},{64,0},{128,64},{192,128},{1,193},{65,1},{129,65},{193,129... | collective-permute-start | bytes 1105928 | tf_op jit(solution)/shard_map/ppermute | solution.py:363
  46.3 0.0 copy-done
  46.3 10.5 %shard_map.79 = (bf16[2560,128]{1,0:T(8,128)(2,1)S(1)}, bf16[640,432]{1,0:T(8,128)(2,1)S(1)}) custom-call(bf16[128,1152]{1,0:T(8,128)(2,1)S(1)} %get-tuple-element.14.tokens_ref, bf16[128,1152]{1,0:T(8,128)(2,1)S(1)} %get-tuple-element.15.masked_ref, bf16[128,3456]{1,0:T(8,128)(2,1)S(1)} %get-tuple-element.16.joined_ref, ...), custom_call_target="tpu_custom_call" | custom-call | flops 3000000000 | bytes 16000000 | tf_op jit(solution)/shard_map/pallas_call | solution.py:46
  56.9 0.0 collective-permute-done.one_ref
  56.9 1.7 %collective-permute-done.1.two_ref = bf16[1440,128]{1,0:T(8,128)(2,1)S(1)} collective-permute-done((bf16[1440,128]{1,0:T(8,128)(2,1)S(1)}, bf16[1440,128]{1,0:T(8,128)(2,1)S(1)}, u32[]{:S(2)}, u32[]{:S(2)}) %collective-permute-start.1) | collective-permute-done | bytes 368672 | tf_op jit(solution)/shard_map/ppermute | solution.py:362
  58.6 0.0 collective-permute-done.2.three_ref
  58.6 1.2 %shard_map.80.after_ref = bf16[576,384]{1,0:T(8,128)(2,1)S(1)} custom-call(bf16[1440,128]{1,0:T(8,128)(2,1)S(1)} %get-tuple-element.19.own_ref, bf16[1440,128]{1,0:T(8,128)(2,1)S(1)} %collective-permute-done.one_ref, bf16[1440,128]{1,0:T(8,128)(2,1)S(1)} %collective-permute-done.1.two_ref, bf16[1440,128]{1,0:T(8,128)(2,1)S(1)} %collective-permute-done.2.three_ref, ...), custom_call_target="tpu_custom_call" | custom-call | flops 1000000000 | bytes 4000000 | tf_op jit(solution)/shard_map/pallas_call | solution.py:46
  59.8 0.1 collective-permute-start.3
  59.9 0.3 fusion.chosen_ref
  60.2 1.2 %shard_map.81.keep_ref = f32[576,384]{1,0:T(8,128)S(1)} custom-call(bf16[1440,128]{1,0:T(8,128)(2,1)S(1)} %get-tuple-element.19.own_ref, bf16[1440,128]{1,0:T(8,128)(2,1)S(1)} %collective-permute-done.one_ref, bf16[1440,128]{1,0:T(8,128)(2,1)S(1)} %collective-permute-done.1.two_ref, bf16[1440,128]{1,0:T(8,128)(2,1)S(1)} %collective-permute-done.2.three_ref, ...), custom_call_target="tpu_custom_call" | custom-call | flops 1000000000 | bytes 4000000 | tf_op jit(solution)/shard_map/pallas_call | solution.py:46
  61.5 0.2 collective-permute-done.3.got_ref
  61.7 0.9 shard_map.82
  62.6 27.2 %all_to_all.10 = bf16[32,80,128]{2,1,0:T(8,128)(2,1)S(1)} all-to-all(bf16[32,80,128]{2,1,0:T(8,128)(2,1)S(1)} %bitcast.13), channel_id=1, replica_groups=mesh['dp'=4,'y'=4,'z'=8,'core'=2] {'y','z'}, dimensions={0} | all-to-all | bytes 1310720 | tf_op jit(solution)/shard_map/all_to_all | solution.py:401
  89.7 1.3 %shard_map.83 = (bf16[128,1152]{1,0:T(8,128)(2,1)}, f32[18,288]{1,0:T(8,128)}) custom-call(bf16[2560,128]{1,0:T(8,128)(2,1)S(1)} %bitcast.12), custom_call_target="tpu_custom_call" | custom-call | tf_op jit(solution)/shard_map/pallas_call | solution.py:46
  (2 shorter events, 0.0 us)
Async XLA Ops:
  2.9 30.4 %all-to-all-start = ((bf16[32,8,1152]{2,1,0:T(8,128)(2,1)}), bf16[32,8,1152]{2,1,0:T(8,128)(2,1)S(1)}, u32[]{:S(2)}, u32[]{:S(2)}) async-start(bf16[32,8,1152]{2,1,0:T(8,128)(2,1)} %bitcast.15), calls=%async_computation | async-start | bytes 1179648 | tf_op jit(solution)/shard_map/all_to_all | solution.py:334
  33.3 13.1 %copy-start = (bf16[1152,1152]{1,0:T(8,128)(2,1)S(1)}, bf16[1152,1152]{1,0:T(8,128)(2,1)}, u32[]{:S(2)}) copy-start(bf16[1152,1152]{1,0:T(8,128)(2,1)} %w_out_ref.1) | copy-start | bytes 7962628
  40.6 16.3 %collective-permute-start = (bf16[1440,128]{1,0:T(8,128)(2,1)S(1)}, bf16[1440,128]{1,0:T(8,128)(2,1)S(1)}, u32[]{:S(2)}, u32[]{:S(2)}) collective-permute-start(bf16[1440,128]{1,0:T(8,128)(2,1)S(1)} %get-tuple-element.20), channel_id=1, source_target_pairs={{0,64},{64,128},{128,192},{192,0},{1,65},{65,129},{129,193},{193,1... | collective-permute-start | bytes 1105928 | tf_op jit(solution)/shard_map/ppermute | solution.py:361
  42.1 16.4 %collective-permute-start.1 = (bf16[1440,128]{1,0:T(8,128)(2,1)S(1)}, bf16[1440,128]{1,0:T(8,128)(2,1)S(1)}, u32[]{:S(2)}, u32[]{:S(2)}) collective-permute-start(bf16[1440,128]{1,0:T(8,128)(2,1)S(1)} %get-tuple-element.21), channel_id=1, source_target_pairs={{0,128},{64,192},{128,0},{192,64},{1,129},{65,193},{129,1},{193,65... | collective-permute-start | bytes 1105928 | tf_op jit(solution)/shard_map/ppermute | solution.py:362
  44.9 13.7 %collective-permute-start.2 = (bf16[1440,128]{1,0:T(8,128)(2,1)S(1)}, bf16[1440,128]{1,0:T(8,128)(2,1)S(1)}, u32[]{:S(2)}, u32[]{:S(2)}) collective-permute-start(bf16[1440,128]{1,0:T(8,128)(2,1)S(1)} %get-tuple-element.22), channel_id=1, source_target_pairs={{0,192},{64,0},{128,64},{192,128},{1,193},{65,1},{129,65},{193,129... | collective-permute-start | bytes 1105928 | tf_op jit(solution)/shard_map/ppermute | solution.py:363
  59.8 1.9 %collective-permute-start.3 = (bf16[576,384]{1,0:T(8,128)(2,1)S(1)}, bf16[576,384]{1,0:T(8,128)(2,1)S(1)}, u32[]{:S(2)}, u32[]{:S(2)}) collective-permute-start(bf16[576,384]{1,0:T(8,128)(2,1)S(1)} %shard_map.80.after_ref), channel_id=1, source_target_pairs={{0,1},{1,0},{2,3},{3,2},{4,5},{5,4},{6,7},{7,6},{8,9},{9,8},{10,11... | collective-permute-start | bytes 1327112 | tf_op jit(solution)/shard_map/ppermute | solution.py:389

commit v4 on v3

--- a/solution.py
+++ b/solution.py
@@ -38,7 +38,9 @@
     return pl.BlockSpec(memory_space=pltpu.VMEM)
 
 
-def call(kernel, out_shape, inputs, scratch=(), limit=32, flops=0, data=0, smem=(), far=()):
+def call(
+    kernel, out_shape, inputs, scratch=(), limit=32, flops=0, data=0, smem=(), far=(), smem_out=()
+):
     spaces = {i: pltpu.SMEM for i in smem} | {i: pl.ANY for i in far}
     specs = [
         pl.BlockSpec(memory_space=spaces.get(i, pltpu.VMEM)) for i in range(len(inputs))
@@ -47,7 +49,10 @@
         kernel,
         out_shape=out_shape,
         in_specs=specs,
-        out_specs=jax.tree.map(lambda _: whole(), out_shape),
+        out_specs=[
+            pl.BlockSpec(memory_space=pltpu.SMEM) if i in smem_out else whole()
+            for i in range(len(out_shape))
+        ],
         scratch_shapes=list(scratch),
         compiler_params=pltpu.CompilerParams(vmem_limit_bytes=limit * MIB),
         cost_estimate=pl.CostEstimate(flops=flops, bytes_accessed=data, transcendentals=0),
@@ -76,7 +81,13 @@
     return packed // 8 + inner % PATCHES * SLOTS + jnp.where(inner >= PATCHES, ROWS, 0)
 
 
-def pack_kernel(tokens_ref, d_out_ref, packed_ref, both_ref, sems):
+def pack_kernel(
+    dp_ref, core_ref, frames_ref, order_ref, tokens_ref, d_out_ref,
+    packed_ref, dp_out_ref, core_out_ref, live_ref,
+    both_ref, sems,
+):
+    dp_out_ref[0] = dp_ref[0]
+    core_out_ref[0] = core_ref[0]
     copies = [
         pltpu.make_async_copy(ref, both_ref.at[pl.ds(i * ROWS, ROWS)], sems.at[i])
         for i, ref in enumerate((tokens_ref, d_out_ref))
@@ -84,6 +95,9 @@
     for copy in copies:
         copy.start()
     chooser = pick((256, 256), source_row(row_index(256)), 1)
+    live = (order_ref[...] < frames_ref[0]).astype(F32)
+    live = jnp.where(row_index(SLOTS) == lane_index(SLOTS), live, 0.0)
+    live_ref[...] = jnp.sum(live, axis=1, keepdims=True)
     for copy in copies:
         copy.wait()
     packed_ref[...] = dot(chooser, both_ref[...]).astype(BF)
@@ -186,8 +200,8 @@
 
 
 def backward_kernel(
-    tokens_ref, masked_ref, joined_ref, probs_ref, w_qkv_ref, w_out_ref,
-    packed_ref, place_ref,
+    core_ref, tokens_ref, masked_ref, joined_ref, probs_ref, w_qkv_ref, w_out_ref,
+    packed_ref, place_ref, mine_ref, theirs_ref,
     grad_ref, head_ref, weight_ref, out_weight_ref, sems,
 ):
     out_copies = [
@@ -213,6 +227,11 @@
     row = inner % OUT_ROWS
     at = TOKEN_ROWS + kind * OUT_ROWS + jnp.where(kind == 2, row // 4, row)
     place_ref[...] = pick((8 * CHUNK, 3 * 8 * OUT_ROWS), inner // OUT_ROWS * CHUNK + at, 0)
+    row = row_index(SLOTS * OUT_ROWS)
+    start = row // OUT_ROWS * (2 * OUT_ROWS) + row % OUT_ROWS
+    core = core_ref[0]
+    mine_ref[...] = pick((SLOTS * OUT_ROWS, D), start + core * OUT_ROWS, 1)
+    theirs_ref[...] = pick((SLOTS * OUT_ROWS, D), start + (1 - core) * OUT_ROWS, 1)
     masked = masked_ref[...]
     for chunk in range(3):
         columns = slice(chunk * WIDE, (chunk + 1) * WIDE)
@@ -267,7 +286,8 @@
         packed_ref[half * 16 * CHUNK : (half + 1) * 16 * CHUNK, :] = dot(chooser, stacked).astype(BF)
 
 
-def weight_kernel(own_ref, one_ref, two_ref, three_ref, chosen_ref, after_ref, terms_ref):
+def weight_kernel(own_ref, one_ref, two_ref, three_ref, chosen_ref, *after_and_out):
+    terms_ref = after_and_out[-1]
     refs = (own_ref, one_ref, two_ref, three_ref)
     attended = jnp.concatenate([ref[:D, :] for ref in refs], axis=1)
     masked = jnp.concatenate([ref[D:, :] for ref in refs], axis=1)
@@ -312,24 +332,25 @@
         d_w_ref[row : row + 1, 256:] = total_ref[at : at + 1, lanes]
 
 
-def chosen_rows(core):
-    at = jnp.arange(SLOTS * OUT_ROWS, dtype=jnp.int32)
-    target = at // OUT_ROWS * (2 * OUT_ROWS) + core * OUT_ROWS + at % OUT_ROWS
-    return (target[:, None] == jnp.arange(D, dtype=jnp.int32)[None, :]).astype(BF)
-
-
 def body(tokens, d_out, frames, frame_order, w_qkv, w_out):
-    place = lax.axis_index("dp")
-    core = lax.axis_index("core")
     shape = jax.ShapeDtypeStruct
-    live = (frame_order[0] < frames[0]).astype(F32)
-    packed = call(
+    one_int = shape((1,), jnp.int32)
+    packed, place, core, live = call(
         pack_kernel,
-        shape((256, D), BF),
-        (tokens[0], d_out[0]),
+        (shape((256, D), BF), one_int, one_int, shape((SLOTS, 1), F32)),
+        (
+            lax.axis_index("dp").reshape(1),
+            lax.axis_index("core").reshape(1),
+            frames,
+            frame_order,
+            tokens[0],
+            d_out[0],
+        ),
         scratch=(pltpu.VMEM((256, D), BF), pltpu.SemaphoreType.DMA((2,))),
         limit=60,
-        far=(0, 1),
+        smem=(0, 1, 2),
+        far=(4, 5),
+        smem_out=(1, 2),
     )
     arrived = lax.all_to_all(
         packed.reshape(SLOTS, 8, D), ("y", "z"), split_axis=0, concat_axis=0, tiled=True
@@ -343,7 +364,7 @@
             shape((H, SLOTS, ROWS), F32),
         )
         + (shape((PAYLOAD, ROWS), BF),) * 4,
-        (place.reshape(1), arrived, live[:, None], w_qkv),
+        (place, arrived, live, w_qkv),
         scratch=(
             pltpu.VMEM((D, ROWS), BF),
             pltpu.VMEM((D, ROWS), F32),
@@ -361,10 +382,11 @@
     from_one = lax.ppermute(one, "dp", ring(1))
     from_two = lax.ppermute(two, "dp", ring(2))
     from_three = lax.ppermute(three, "dp", ring(3))
-    rows, places = call(
+    chosen = shape((SLOTS * OUT_ROWS, D), BF)
+    rows, places, mine, theirs = call(
         backward_kernel,
-        (shape((SLOTS * CHUNK, 128), BF), shape((8 * CHUNK, 3 * 8 * OUT_ROWS), BF)),
-        (kept, masked, joined, probs, w_qkv, w_out),
+        (shape((SLOTS * CHUNK, 128), BF), shape((8 * CHUNK, 3 * 8 * OUT_ROWS), BF), chosen, chosen),
+        (core, kept, masked, joined, probs, w_qkv, w_out),
         scratch=(
             pltpu.VMEM((ROWS, 3 * D), BF),
             pltpu.VMEM((ROWS, D), BF),
@@ -372,31 +394,31 @@
             pltpu.VMEM((D, D), BF),
             pltpu.SemaphoreType.DMA((6,)),
         ),
-        far=(4, 5),
+        smem=(0,),
+        far=(5, 6),
         limit=47,
         flops=int(3e9),
         data=int(16e6),
     )
     payloads = (own, from_one, from_two, from_three)
-    send = call(
+    (send,) = call(
         weight_kernel,
-        shape((SLOTS * OUT_ROWS, WIDE), BF),
-        payloads + (chosen_rows(1 - core), rows),
+        (shape((SLOTS * OUT_ROWS, WIDE), BF),),
+        payloads + (theirs,),
+        flops=int(1e9),
+        data=int(4e6),
+    )
+    got = lax.ppermute(send, "core", [(0, 1), (1, 0)])
+    (keep,) = call(
+        weight_kernel,
+        (shape((SLOTS * OUT_ROWS, WIDE), F32),),
+        payloads + (mine, send),
         far=(5,),
         flops=int(1e9),
         data=int(4e6),
     )
-    got = lax.ppermute(send, "core", [(0, 1), (1, 0)])
-    keep = call(
-        weight_kernel,
-        shape((SLOTS * OUT_ROWS, WIDE), F32),
-        payloads + (chosen_rows(core), send),
-        far=(5,),
-        flops=int(1e9),
-        data=int(4e6),
-    )
-    merged = call(
-        merge_kernel, shape((SLOTS * CHUNK, 128), BF), (rows, keep, got, places), limit=16
+    (merged,) = call(
+        merge_kernel, (shape((SLOTS * CHUNK, 128), BF),), (rows, keep, got, places), limit=16
     )
     returned = lax.all_to_all(
         merged.reshape(SLOTS, CHUNK, 128), ("y", "z"), split_axis=0, concat_axis=0, tiled=True

time: 91.3 us -> 93.8 us (1.027)
  blocking collectives: 27.2 us -> 57.4 us
  waiting for transfers between devices: 19.2 us -> 1.27 us
  starting transfers between devices: 17.2 us -> 5.82 us
  Pallas kernels: 24.7 us -> 26.9 us
  other arithmetic: 1.26 us -> 0 us
    all_to_all x0 -> x1, blocking collectives: none -> 30.4 us  [body(): lax.all_to_all(packed.reshape(SLOTS, 8, D), ('y', 'z'), split_axis=0, con...]
    all_to_all x1 -> x0, waiting for transfers between devices: 17.3 us -> none  [body(): lax.all_to_all(packed.reshape(SLOTS, 8, D), ('y', 'z'), split_axis=0, con...]
    all_to_all x1 -> x0, starting transfers between devices: 11.4 us -> none  [body(): lax.all_to_all(packed.reshape(SLOTS, 8, D), ('y', 'z'), split_axis=0, con...]
    pallas_call x7, Pallas kernels: 24.7 us -> 26.9 us  [call(): pl.pallas_call(kernel, out_shape=out_shape, in_specs=specs, out_specs=[pl...]
    convert_element_type x3 -> x0, other arithmetic: 1.23 us -> none  [the longest x1 0.66 us: body(): live = (frame_order[0] < frames[0]).astype(F32)]
    ppermute x1, waiting for transfers between devices: 1.69 us -> 0.72 us  [body(): from_two = lax.ppermute(two, 'dp', ring(2))]
  transfers between devices with their start and end apart: 5 -> 4, of which waited for: 3 -> 2; matrix products, arithmetic and copies ran while one was open for 1% -> 0% of each run, Pallas kernels for 13% -> 14%
where the time goes in v4:
time: 93.8 us; the launch traced here: 93.5 us
  blocking collectives  57.4 us (61%)
  Pallas kernels  26.9 us (29%)
  starting transfers between devices  5.82 us (6%)
  between operations  1.34 us (1%)
  waiting for transfers between devices  1.27 us (1%)
    all_to_all x1, blocking collectives, body(): lax.all_to_all(packed.reshape(SLOTS, 8, D), ('y', 'z'), split_axis=0, con...  30.4 us
    all_to_all x1, blocking collectives, body(): lax.all_to_all(merged.reshape(SLOTS, CHUNK, 128), ('y', 'z'), split_axis=...  27 us
    pallas_call x7, Pallas kernels, call(): pl.pallas_call(kernel, out_shape=out_shape, in_specs=specs, out_specs=[pl...  26.9 us
    ppermute x1, starting transfers between devices, body(): from_two = lax.ppermute(two, 'dp', ring(2))  2.73 us
  transfers between devices with their start and end apart: 4, of which 2 were waited for; matrix products, arithmetic and copies ran while one was open for 0% of the time, Pallas kernels for 14%

profile of v4, /device:TPU:32, one launch (start us, length us, event | category | flops | bytes accessed | tf_op | source)
XLA Modules:
  0.0 93.5 jit_solution(10807004459955429413)
XLA Ops:
  1.3 3.0 %shard_map.77 = (bf16[256,1152]{1,0:T(8,128)(2,1)}, s32[1]{0:T(128)}, s32[1]{0:T(128)}, f32[32,1]{1,0:T(8,128)}) custom-call(s32[1]{0:T(128)} %bitcast.dp_ref, s32[1]{0:T(128)} %bitcast.1.core_ref, s32[1]{0:T(128)S(6)} %copy.8.frames_ref, s32[1,32]{1,0:T(1,128)} %order_ref.1, bf16[128,1152]{1,0:T(8,128)(2,1)} %bitcast.13, bf16[128,1152]{1,0:T(8,128)(2,1)} %bitcast.14), custom_call_target="tpu_custom_call" | custom-call | tf_op jit(solution)/shard_map/pallas_call | solution.py:48
  4.2 30.4 %all_to_all.10 = bf16[32,8,1152]{2,1,0:T(8,128)(2,1)S(1)} all-to-all(bf16[32,8,1152]{2,1,0:T(8,128)(2,1)} %bitcast.12), channel_id=1, replica_groups=mesh['dp'=4,'y'=4,'z'=8,'core'=2] {'y','z'}, dimensions={0} | all-to-all | bytes 1179648 | tf_op jit(solution)/shard_map/all_to_all | solution.py:355
  34.6 0.0 copy-start
  34.6 0.7 copy-done
  35.3 7.8 %shard_map.78 = (bf16[128,1152]{1,0:T(8,128)(2,1)S(1)}, bf16[128,1152]{1,0:T(8,128)(2,1)S(1)}, bf16[128,3456]{1,0:T(8,128)(2,1)S(1)}, f32[16,32,128]{2,1,0:T(8,1...) custom-call(s32[1]{0:T(128)} %get-tuple-element.21.place_ref, ...), custom_call_target="tpu_custom_call" | custom-call | flops 2000000000 | bytes 14000000 | tf_op jit(solution)/shard_map/pallas_call | solution.py:48
  43.1 1.6 %collective-permute-start = (bf16[1440,128]{1,0:T(8,128)(2,1)S(1)}, bf16[1440,128]{1,0:T(8,128)(2,1)S(1)}, u32[]{:S(2)}, u32[]{:S(2)}) collective-permute-start(bf16[1440,128]{1,0:T(8,128)(2,1)S(1)} %get-tuple-element.30), channel_id=1, source_target_pairs={{0,64},{64,128},{128,192},{192,0},{1,65},{65,129},{129,193},{193,1... | collective-permute-start | bytes 1105928 | tf_op jit(solution)/shard_map/ppermute | solution.py:382
  44.7 2.7 %collective-permute-start.1 = (bf16[1440,128]{1,0:T(8,128)(2,1)S(1)}, bf16[1440,128]{1,0:T(8,128)(2,1)S(1)}, u32[]{:S(2)}, u32[]{:S(2)}) collective-permute-start(bf16[1440,128]{1,0:T(8,128)(2,1)S(1)} %get-tuple-element.31), channel_id=1, source_target_pairs={{0,128},{64,192},{128,0},{192,64},{1,129},{65,193},{129,1},{193,65... | collective-permute-start | bytes 1105928 | tf_op jit(solution)/shard_map/ppermute | solution.py:383
  47.4 1.4 %collective-permute-start.2 = (bf16[1440,128]{1,0:T(8,128)(2,1)S(1)}, bf16[1440,128]{1,0:T(8,128)(2,1)S(1)}, u32[]{:S(2)}, u32[]{:S(2)}) collective-permute-start(bf16[1440,128]{1,0:T(8,128)(2,1)S(1)} %get-tuple-element.32), channel_id=1, source_target_pairs={{0,192},{64,0},{128,64},{192,128},{1,193},{65,1},{129,65},{193,129... | collective-permute-start | bytes 1105928 | tf_op jit(solution)/shard_map/ppermute | solution.py:384
  48.9 11.5 %shard_map.79 = (bf16[2560,128]{1,0:T(8,128)(2,1)S(1)}, bf16[640,432]{1,0:T(8,128)(2,1)S(1)}, bf16[576,1152]{1,0:T(8,128)(2,1)S(1)}, bf16[576,1152]{1,0:T(8,128)(2,1)S(1)}) custom-call(s32[1]{0:T(128)} %get-tuple-element.20.core_ref, bf16[128,1152]{1,0:T(8,128)(2,1)S(1)} %get-tuple-element.24.tokens_ref, bf16[128,1152]{1,0:T(8,128)(2,1)S(1)} %get-tuple-element.25.masked_ref, ...), custom_call_target="tpu_custom_call" | custom-call | flops 3000000000 | bytes 16000000 | tf_op jit(solution)/shard_map/pallas_call | solution.py:48
  60.4 0.0 collective-permute-done.one_ref
  60.4 0.7 collective-permute-done.1.two_ref
  61.1 0.0 collective-permute-done.2.three_ref
  61.1 1.2 %shard_map.80.after_and_out_0_ = bf16[576,384]{1,0:T(8,128)(2,1)S(1)} custom-call(bf16[1440,128]{1,0:T(8,128)(2,1)S(1)} %get-tuple-element.29.own_ref, bf16[1440,128]{1,0:T(8,128)(2,1)S(1)} %collective-permute-done.one_ref, bf16[1440,128]{1,0:T(8,128)(2,1)S(1)} %collective-permute-done.1.two_ref, bf16[1440,128]{1,0:T(8,128)(2,1)S(1)} %collective-permute-done.2.three_ref, ...), custom_call_target="tpu_custom_call" | custom-call | flops 1000000000 | bytes 4000000 | tf_op jit(solution)/shard_map/pallas_call | solution.py:48
  62.4 0.1 collective-permute-start.3
  62.5 1.2 %shard_map.81.keep_ref = f32[576,384]{1,0:T(8,128)S(1)} custom-call(bf16[1440,128]{1,0:T(8,128)(2,1)S(1)} %get-tuple-element.29.own_ref, bf16[1440,128]{1,0:T(8,128)(2,1)S(1)} %collective-permute-done.one_ref, bf16[1440,128]{1,0:T(8,128)(2,1)S(1)} %collective-permute-done.1.two_ref, bf16[1440,128]{1,0:T(8,128)(2,1)S(1)} %collective-permute-done.2.three_ref, ...), custom_call_target="tpu_custom_call" | custom-call | flops 1000000000 | bytes 4000000 | tf_op jit(solution)/shard_map/pallas_call | solution.py:48
  63.7 0.5 collective-permute-done.3.got_ref
  64.3 0.9 shard_map.82
  65.2 27.0 %all_to_all.11 = bf16[32,80,128]{2,1,0:T(8,128)(2,1)S(1)} all-to-all(bf16[32,80,128]{2,1,0:T(8,128)(2,1)S(1)} %bitcast.10), channel_id=1, replica_groups=mesh['dp'=4,'y'=4,'z'=8,'core'=2] {'y','z'}, dimensions={0} | all-to-all | bytes 1310720 | tf_op jit(solution)/shard_map/all_to_all | solution.py:423
  92.2 1.3 %shard_map.83 = (bf16[128,1152]{1,0:T(8,128)(2,1)}, f32[18,288]{1,0:T(8,128)}) custom-call(bf16[2560,128]{1,0:T(8,128)(2,1)S(1)} %bitcast.9), custom_call_target="tpu_custom_call" | custom-call | tf_op jit(solution)/shard_map/pallas_call | solution.py:48
Async XLA Ops:
  34.6 0.7 copy-start
  43.1 17.3 %collective-permute-start = (bf16[1440,128]{1,0:T(8,128)(2,1)S(1)}, bf16[1440,128]{1,0:T(8,128)(2,1)S(1)}, u32[]{:S(2)}, u32[]{:S(2)}) collective-permute-start(bf16[1440,128]{1,0:T(8,128)(2,1)S(1)} %get-tuple-element.30), channel_id=1, source_target_pairs={{0,64},{64,128},{128,192},{192,0},{1,65},{65,129},{129,193},{193,1... | collective-permute-start | bytes 1105928 | tf_op jit(solution)/shard_map/ppermute | solution.py:382
  44.7 16.4 %collective-permute-start.1 = (bf16[1440,128]{1,0:T(8,128)(2,1)S(1)}, bf16[1440,128]{1,0:T(8,128)(2,1)S(1)}, u32[]{:S(2)}, u32[]{:S(2)}) collective-permute-start(bf16[1440,128]{1,0:T(8,128)(2,1)S(1)} %get-tuple-element.31), channel_id=1, source_target_pairs={{0,128},{64,192},{128,0},{192,64},{1,129},{65,193},{129,1},{193,65... | collective-permute-start | bytes 1105928 | tf_op jit(solution)/shard_map/ppermute | solution.py:383
  47.4 13.7 %collective-permute-start.2 = (bf16[1440,128]{1,0:T(8,128)(2,1)S(1)}, bf16[1440,128]{1,0:T(8,128)(2,1)S(1)}, u32[]{:S(2)}, u32[]{:S(2)}) collective-permute-start(bf16[1440,128]{1,0:T(8,128)(2,1)S(1)} %get-tuple-element.32), channel_id=1, source_target_pairs={{0,192},{64,0},{128,64},{192,128},{1,193},{65,1},{129,65},{193,129... | collective-permute-start | bytes 1105928 | tf_op jit(solution)/shard_map/ppermute | solution.py:384
  62.4 1.9 %collective-permute-start.3 = (bf16[576,384]{1,0:T(8,128)(2,1)S(1)}, bf16[576,384]{1,0:T(8,128)(2,1)S(1)}, u32[]{:S(2)}, u32[]{:S(2)}) collective-permute-start(bf16[576,384]{1,0:T(8,128)(2,1)S(1)} %shard_map.80.after_and_out_0_), channel_id=1, source_target_pairs={{0,1},{1,0},{2,3},{3,2},{4,5},{5,4},{6,7},{7,6},{8,9},{9,8},{10,11... | collective-permute-start | bytes 1327112 | tf_op jit(solution)/shard_map/ppermute | solution.py:411

commit v5 on v3

--- a/solution.py
+++ b/solution.py
@@ -1,3 +1,4 @@
+import functools
 import math
 
 import jax
@@ -23,6 +24,7 @@
 CHUNK = 80
 TOKEN_ROWS = 36
 PAYLOAD = D + COLS
+HALF = D // 2
 EXP_SCALE = SCALE * math.log2(math.e)
 
 NN = (((1,), (0,)), ((), ()))
@@ -127,11 +129,11 @@
 
 
 def forward_kernel(
-    place_ref, packed_ref, live_ref, w_qkv_ref,
+    place_ref, core_ref, packed_ref, live_ref, first_q_ref, first_k_ref, first_v_ref, w_qkv_ref,
     tokens_ref, masked_ref, joined_ref, probs_ref, own_ref, one_ref, two_ref, three_ref,
     turned_ref, values_ref, attended_ref, weight_ref, sems,
 ):
-    spans = [pl.ds(kind * D + chunk * WIDE, WIDE) for chunk in range(3) for kind in range(3)]
+    spans = [pl.ds(kind * D + chunk * WIDE, WIDE) for chunk in (1, 2) for kind in range(3)]
     copies = [
         pltpu.make_async_copy(w_qkv_ref.at[:, span], weight_ref.at[:, span], sems.at[i])
         for i, span in enumerate(spans)
@@ -157,10 +159,16 @@
     patch = lane_patch()
     done = 0
     for chunk in range(3):
+        if chunk > 0:
+            for copy in copies[chunk * 3 - 3 : chunk * 3]:
+                copy.wait()
         for kind in range(3):
-            copies[chunk * 3 + kind].wait()
             columns = slice(kind * D + chunk * WIDE, kind * D + (chunk + 1) * WIDE)
-            product = dot(normed, weight_ref[:, columns])
+            if chunk == 0:
+                weight = (first_q_ref, first_k_ref, first_v_ref)[kind][...]
+            else:
+                weight = weight_ref[:, columns]
+            product = dot(normed, weight)
             joined_ref[:, columns] = product.astype(BF)
             if kind == 2:
                 for block in range(3):
@@ -179,7 +187,10 @@
             probs = exponent / jnp.sum(exponent, axis=0, keepdims=True)
             probs_ref[head] = probs
             rows = slice(head * E, (head + 1) * E)
-            attended_ref[rows, :] = dot(values_ref[rows, :].astype(BF), spread(probs, patch))
+            attended = dot(values_ref[rows, :].astype(BF), spread(probs, patch))
+            for group in range(4):
+                at = group % 2 * HALF + head * 2 * OUT_ROWS + group // 2 * OUT_ROWS
+                attended_ref[at : at + OUT_ROWS, :] = attended[group * OUT_ROWS : (group + 1) * OUT_ROWS]
     attended = attended_ref[...].astype(BF)
     for out_ref in sends:
         out_ref[:D, :] = attended
@@ -214,9 +225,10 @@
     at = TOKEN_ROWS + kind * OUT_ROWS + jnp.where(kind == 2, row // 4, row)
     place_ref[...] = pick((8 * CHUNK, 3 * 8 * OUT_ROWS), inner // OUT_ROWS * CHUNK + at, 0)
     masked = masked_ref[...]
+    for copy in out_copies:
+        copy.wait()
     for chunk in range(3):
         columns = slice(chunk * WIDE, (chunk + 1) * WIDE)
-        out_copies[chunk].wait()
         head_ref[:, columns] = dot(masked, out_weight_ref[columns, :], NT).astype(BF)
     patch = lane_patch()
     for head in range(H):
@@ -241,8 +253,9 @@
             else:
                 grad_ref[:, at : at + width] = jnp.where(inside, part, grad_ref[:, at : at + width])
     pieces = []
+    for copy in qkv_copies:
+        copy.wait()
     for chunk in range(3):
-        qkv_copies[chunk].wait()
         rows = slice(chunk * WIDE, (chunk + 1) * WIDE)
         pieces.append(dot(grad_ref[...], weight_ref[rows, :], NT))
     normed_grad = jnp.concatenate(pieces, axis=1)
@@ -267,13 +280,14 @@
         packed_ref[half * 16 * CHUNK : (half + 1) * 16 * CHUNK, :] = dot(chooser, stacked).astype(BF)
 
 
-def weight_kernel(own_ref, one_ref, two_ref, three_ref, chosen_ref, after_ref, terms_ref):
+def weight_kernel(other, core_ref, own_ref, one_ref, two_ref, three_ref, after_ref, terms_ref):
     refs = (own_ref, one_ref, two_ref, three_ref)
-    attended = jnp.concatenate([ref[:D, :] for ref in refs], axis=1)
+    core = 1 - core_ref[0] if other else core_ref[0]
+    start = pl.multiple_of(core * HALF, HALF)
+    attended = jnp.concatenate([ref[pl.ds(start, HALF), :] for ref in refs], axis=1)
     masked = jnp.concatenate([ref[D:, :] for ref in refs], axis=1)
     masked = jnp.concatenate([masked[:256]] + [masked[256:]] * 4, axis=0)
-    chosen = dot(chosen_ref[...], attended).astype(BF)
-    terms_ref[...] = dot(chosen, masked, NT).astype(terms_ref.dtype)
+    terms_ref[...] = dot(attended, masked, NT).astype(terms_ref.dtype)
 
 
 def merge_kernel(rows_ref, keep_ref, got_ref, place_ref, merged_ref):
@@ -312,12 +326,6 @@
         d_w_ref[row : row + 1, 256:] = total_ref[at : at + 1, lanes]
 
 
-def chosen_rows(core):
-    at = jnp.arange(SLOTS * OUT_ROWS, dtype=jnp.int32)
-    target = at // OUT_ROWS * (2 * OUT_ROWS) + core * OUT_ROWS + at % OUT_ROWS
-    return (target[:, None] == jnp.arange(D, dtype=jnp.int32)[None, :]).astype(BF)
-
-
 def body(tokens, d_out, frames, frame_order, w_qkv, w_out):
     place = lax.axis_index("dp")
     core = lax.axis_index("core")
@@ -334,6 +342,7 @@
     arrived = lax.all_to_all(
         packed.reshape(SLOTS, 8, D), ("y", "z"), split_axis=0, concat_axis=0, tiled=True
     ).reshape(256, D)
+    firsts = tuple(w_qkv[:, kind * D : kind * D + WIDE] for kind in range(3))
     kept, masked, joined, probs, own, one, two, three = call(
         forward_kernel,
         (
@@ -343,16 +352,16 @@
             shape((H, SLOTS, ROWS), F32),
         )
         + (shape((PAYLOAD, ROWS), BF),) * 4,
-        (place.reshape(1), arrived, live[:, None], w_qkv),
+        (place.reshape(1), core.reshape(1), arrived, live[:, None]) + firsts + (w_qkv,),
         scratch=(
             pltpu.VMEM((D, ROWS), BF),
             pltpu.VMEM((D, ROWS), F32),
             pltpu.VMEM((D, ROWS), F32),
             pltpu.VMEM((D, 3 * D), BF),
-            pltpu.SemaphoreType.DMA((9,)),
+            pltpu.SemaphoreType.DMA((6,)),
         ),
-        smem=(0,),
-        far=(3,),
+        smem=(0, 1),
+        far=(7,),
         limit=47,
         flops=int(2e9),
         data=int(14e6),
@@ -379,18 +388,20 @@
     )
     payloads = (own, from_one, from_two, from_three)
     send = call(
-        weight_kernel,
+        functools.partial(weight_kernel, True),
         shape((SLOTS * OUT_ROWS, WIDE), BF),
-        payloads + (chosen_rows(1 - core), rows),
+        (core.reshape(1),) + payloads + (rows,),
+        smem=(0,),
         far=(5,),
         flops=int(1e9),
         data=int(4e6),
     )
     got = lax.ppermute(send, "core", [(0, 1), (1, 0)])
     keep = call(
-        weight_kernel,
+        functools.partial(weight_kernel, False),
         shape((SLOTS * OUT_ROWS, WIDE), F32),
-        payloads + (chosen_rows(core), send),
+        (core.reshape(1),) + payloads + (send,),
+        smem=(0,),
         far=(5,),
         flops=int(1e9),
         data=int(4e6),

time: 91.3 us -> 89.8 us (0.984)
  Pallas kernels: 24.7 us -> 21.4 us
  local copies, waits for them, and re-layouts: 0.09 us -> 2.08 us
    pallas_call x7, Pallas kernels: 24.7 us -> 21.4 us  [call(): pl.pallas_call(kernel, out_shape=out_shape, in_specs=specs, out_specs=jax...]
    slice x0 -> x1, local copies, waits for them, and re-layouts: none -> 1.98 us  [body(): firsts = tuple((w_qkv[:, kind * D:kind * D + WIDE] for kind in range(3)))]
    all_to_all x1, waiting for transfers between devices: 17.3 us -> 15.6 us  [body(): lax.all_to_all(packed.reshape(SLOTS, 8, D), ('y', 'z'), split_axis=0, con...]
    ppermute x1, waiting for transfers between devices: 1.69 us -> 2.84 us  [body(): from_two = lax.ppermute(two, 'dp', ring(2))]
    ppermute x1, waiting for transfers between devices: 0.25 us -> 1.28 us  [body(): got = lax.ppermute(send, 'core', [(0, 1), (1, 0)])]
  transfers between devices with their start and end apart: 5 -> 5, of which waited for: 3 -> 3; matrix products, arithmetic and copies ran while one was open for 1% -> 3% of each run, Pallas kernels for 13% -> 11%
where the time goes in v5:
time: 89.8 us; the launch traced here: 89.5 us
  blocking collectives  27 us (30%)
  Pallas kernels  21.4 us (24%)
  waiting for transfers between devices  19.7 us (22%)
  starting transfers between devices  17.2 us (19%)
  local copies, waits for them, and re-layouts  2.08 us (2%)
  between operations  1.36 us (2%)
    all_to_all x1, blocking collectives, body(): lax.all_to_all(merged.reshape(SLOTS, CHUNK, 128), ('y', 'z'), split_axis=...  27 us
    pallas_call x7, Pallas kernels, call(): pl.pallas_call(kernel, out_shape=out_shape, in_specs=specs, out_specs=jax...  21.4 us
    all_to_all x1, waiting for transfers between devices, body(): lax.all_to_all(packed.reshape(SLOTS, 8, D), ('y', 'z'), split_axis=0, con...  15.6 us
    all_to_all x1, starting transfers between devices, body(): lax.all_to_all(packed.reshape(SLOTS, 8, D), ('y', 'z'), split_axis=0, con...  11.4 us
    ppermute x1, waiting for transfers between devices, body(): from_two = lax.ppermute(two, 'dp', ring(2))  2.84 us
    ppermute x1, starting transfers between devices, body(): from_two = lax.ppermute(two, 'dp', ring(2))  2.73 us
    slice x1, local copies, waits for them, and re-layouts, body(): firsts = tuple((w_qkv[:, kind * D:kind * D + WIDE] for kind in range(3)))  1.98 us
  transfers between devices with their start and end apart: 5, of which 3 were waited for; matrix products, arithmetic and copies ran while one was open for 3% of the time, Pallas kernels for 11%

profile of v5, /device:TPU:32, one launch (start us, length us, event | category | flops | bytes accessed | tf_op | source)
XLA Modules:
  0.0 89.5 jit_solution(10459234343100170469)
XLA Ops:
  0.6 2.2 %shard_map.77 = bf16[256,1152]{1,0:T(8,128)(2,1)} custom-call(bf16[128,1152]{1,0:T(8,128)(2,1)} %bitcast.17, bf16[128,1152]{1,0:T(8,128)(2,1)} %bitcast.18), custom_call_target="tpu_custom_call" | custom-call | tf_op jit(solution)/shard_map/pallas_call | solution.py:48
  2.9 11.4 %all-to-all-start = ((bf16[32,8,1152]{2,1,0:T(8,128)(2,1)}), bf16[32,8,1152]{2,1,0:T(8,128)(2,1)S(1)}, u32[]{:S(2)}, u32[]{:S(2)}) async-start(bf16[32,8,1152]{2,1,0:T(8,128)(2,1)} %bitcast.16), calls=%async_computation | async-start | bytes 1179648 | tf_op jit(solution)/shard_map/all_to_all | solution.py:342
  14.9 0.7 fusion
  15.6 0.1 copy.8.live_ref
  15.6 2.0 %fusion.1 = (bf16[1152,384]{1,0:T(8,128)(2,1)S(1)}, bf16[1152,384]{1,0:T(8,128)(2,1)S(1)}, bf16[1152,384]{1,0:T(8,128)(2,1)S(1)}) fusion(bf16[1152,3456]{1,0:T(8,128)(2,1)} %w_qkv_ref.3), kind=kLoop, calls=%fused_computation.2 | loop fusion | bytes 5308416 | tf_op jit(solution)/shard_map/slice | solution.py:345
  17.6 15.6 %all-to-all-done = bf16[32,8,1152]{2,1,0:T(8,128)(2,1)S(1)} async-done(((bf16[32,8,1152]{2,1,0:T(8,128)(2,1)}), bf16[32,8,1152]{2,1,0:T(8,128)(2,1)S(1)}, u32[]{:S(2)}, u32[]{:S(2)}) %all-to-all-start) | async-done | bytes 589856 | tf_op jit(solution)/shard_map/all_to_all | solution.py:342
  33.2 0.0 copy-start
  33.2 6.6 %shard_map.78 = (bf16[128,1152]{1,0:T(8,128)(2,1)S(1)}, bf16[128,1152]{1,0:T(8,128)(2,1)S(1)}, bf16[128,3456]{1,0:T(8,128)(2,1)S(1)}, f32[16,32,128]{2,1,0:T(8,1...) custom-call(s32[1]{0:T(128)} %bitcast.place_ref, ...), custom_call_target="tpu_custom_call" | custom-call | flops 2000000000 | bytes 14000000 | tf_op jit(solution)/shard_map/pallas_call | solution.py:48
  39.9 1.6 %collective-permute-start = (bf16[1440,128]{1,0:T(8,128)(2,1)S(1)}, bf16[1440,128]{1,0:T(8,128)(2,1)S(1)}, u32[]{:S(2)}, u32[]{:S(2)}) collective-permute-start(bf16[1440,128]{1,0:T(8,128)(2,1)S(1)} %get-tuple-element.20), channel_id=1, source_target_pairs={{0,64},{64,128},{128,192},{192,0},{1,65},{65,129},{129,193},{193,1... | collective-permute-start | bytes 1105928 | tf_op jit(solution)/shard_map/ppermute | solution.py:370
  41.4 2.7 %collective-permute-start.1 = (bf16[1440,128]{1,0:T(8,128)(2,1)S(1)}, bf16[1440,128]{1,0:T(8,128)(2,1)S(1)}, u32[]{:S(2)}, u32[]{:S(2)}) collective-permute-start(bf16[1440,128]{1,0:T(8,128)(2,1)S(1)} %get-tuple-element.21), channel_id=1, source_target_pairs={{0,128},{64,192},{128,0},{192,64},{1,129},{65,193},{129,1},{193,65... | collective-permute-start | bytes 1105928 | tf_op jit(solution)/shard_map/ppermute | solution.py:371
  44.2 1.4 %collective-permute-start.2 = (bf16[1440,128]{1,0:T(8,128)(2,1)S(1)}, bf16[1440,128]{1,0:T(8,128)(2,1)S(1)}, u32[]{:S(2)}, u32[]{:S(2)}) collective-permute-start(bf16[1440,128]{1,0:T(8,128)(2,1)S(1)} %get-tuple-element.22), channel_id=1, source_target_pairs={{0,192},{64,0},{128,64},{192,128},{1,193},{65,1},{129,65},{193,129... | collective-permute-start | bytes 1105928 | tf_op jit(solution)/shard_map/ppermute | solution.py:372
  45.6 0.0 copy-done
  45.6 9.4 %shard_map.79 = (bf16[2560,128]{1,0:T(8,128)(2,1)S(1)}, bf16[640,432]{1,0:T(8,128)(2,1)S(1)}) custom-call(bf16[128,1152]{1,0:T(8,128)(2,1)S(1)} %get-tuple-element.14.tokens_ref, bf16[128,1152]{1,0:T(8,128)(2,1)S(1)} %get-tuple-element.15.masked_ref, bf16[128,3456]{1,0:T(8,128)(2,1)S(1)} %get-tuple-element.16.joined_ref, ...), custom_call_target="tpu_custom_call" | custom-call | flops 3000000000 | bytes 16000000 | tf_op jit(solution)/shard_map/pallas_call | solution.py:48
  55.0 0.0 collective-permute-done.one_ref
  55.0 2.8 %collective-permute-done.1.two_ref = bf16[1440,128]{1,0:T(8,128)(2,1)S(1)} collective-permute-done((bf16[1440,128]{1,0:T(8,128)(2,1)S(1)}, bf16[1440,128]{1,0:T(8,128)(2,1)S(1)}, u32[]{:S(2)}, u32[]{:S(2)}) %collective-permute-start.1) | collective-permute-done | bytes 368672 | tf_op jit(solution)/shard_map/ppermute | solution.py:371
  57.9 0.0 collective-permute-done.2.three_ref
  57.9 0.5 shard_map.80.after_ref
  58.4 0.1 collective-permute-start.3
  58.5 0.5 shard_map.81.keep_ref
  59.0 1.3 %collective-permute-done.3.got_ref = bf16[576,384]{1,0:T(8,128)(2,1)S(1)} collective-permute-done((bf16[576,384]{1,0:T(8,128)(2,1)S(1)}, bf16[576,384]{1,0:T(8,128)(2,1)S(1)}, u32[]{:S(2)}, u32[]{:S(2)}) %collective-permute-start.3) | collective-permute-done | bytes 442400 | tf_op jit(solution)/shard_map/ppermute | solution.py:399
  60.3 0.9 shard_map.82
  61.2 27.0 %all_to_all.10 = bf16[32,80,128]{2,1,0:T(8,128)(2,1)S(1)} all-to-all(bf16[32,80,128]{2,1,0:T(8,128)(2,1)S(1)} %bitcast.14), channel_id=1, replica_groups=mesh['dp'=4,'y'=4,'z'=8,'core'=2] {'y','z'}, dimensions={0} | all-to-all | bytes 1310720 | tf_op jit(solution)/shard_map/all_to_all | solution.py:412
  88.2 1.3 %shard_map.83 = (bf16[128,1152]{1,0:T(8,128)(2,1)}, f32[18,288]{1,0:T(8,128)}) custom-call(bf16[2560,128]{1,0:T(8,128)(2,1)S(1)} %bitcast.13), custom_call_target="tpu_custom_call" | custom-call | tf_op jit(solution)/shard_map/pallas_call | solution.py:48
Async XLA Ops:
  2.9 30.4 %all-to-all-start = ((bf16[32,8,1152]{2,1,0:T(8,128)(2,1)}), bf16[32,8,1152]{2,1,0:T(8,128)(2,1)S(1)}, u32[]{:S(2)}, u32[]{:S(2)}) async-start(bf16[32,8,1152]{2,1,0:T(8,128)(2,1)} %bitcast.16), calls=%async_computation | async-start | bytes 1179648 | tf_op jit(solution)/shard_map/all_to_all | solution.py:342
  33.2 12.4 %copy-start = (bf16[1152,1152]{1,0:T(8,128)(2,1)S(1)}, bf16[1152,1152]{1,0:T(8,128)(2,1)}, u32[]{:S(2)}) copy-start(bf16[1152,1152]{1,0:T(8,128)(2,1)} %w_out_ref.1) | copy-start | bytes 7962628
  39.9 15.2 %collective-permute-start = (bf16[1440,128]{1,0:T(8,128)(2,1)S(1)}, bf16[1440,128]{1,0:T(8,128)(2,1)S(1)}, u32[]{:S(2)}, u32[]{:S(2)}) collective-permute-start(bf16[1440,128]{1,0:T(8,128)(2,1)S(1)} %get-tuple-element.20), channel_id=1, source_target_pairs={{0,64},{64,128},{128,192},{192,0},{1,65},{65,129},{129,193},{193,1... | collective-permute-start | bytes 1105928 | tf_op jit(solution)/shard_map/ppermute | solution.py:370
  41.4 16.4 %collective-permute-start.1 = (bf16[1440,128]{1,0:T(8,128)(2,1)S(1)}, bf16[1440,128]{1,0:T(8,128)(2,1)S(1)}, u32[]{:S(2)}, u32[]{:S(2)}) collective-permute-start(bf16[1440,128]{1,0:T(8,128)(2,1)S(1)} %get-tuple-element.21), channel_id=1, source_target_pairs={{0,128},{64,192},{128,0},{192,64},{1,129},{65,193},{129,1},{193,65... | collective-permute-start | bytes 1105928 | tf_op jit(solution)/shard_map/ppermute | solution.py:371
  44.2 13.7 %collective-permute-start.2 = (bf16[1440,128]{1,0:T(8,128)(2,1)S(1)}, bf16[1440,128]{1,0:T(8,128)(2,1)S(1)}, u32[]{:S(2)}, u32[]{:S(2)}) collective-permute-start(bf16[1440,128]{1,0:T(8,128)(2,1)S(1)} %get-tuple-element.22), channel_id=1, source_target_pairs={{0,192},{64,0},{128,64},{192,128},{1,193},{65,1},{129,65},{193,129... | collective-permute-start | bytes 1105928 | tf_op jit(solution)/shard_map/ppermute | solution.py:372
  58.4 1.9 %collective-permute-start.3 = (bf16[576,384]{1,0:T(8,128)(2,1)S(1)}, bf16[576,384]{1,0:T(8,128)(2,1)S(1)}, u32[]{:S(2)}, u32[]{:S(2)}) collective-permute-start(bf16[576,384]{1,0:T(8,128)(2,1)S(1)} %shard_map.80.after_ref), channel_id=1, source_target_pairs={{0,1},{1,0},{2,3},{3,2},{4,5},{5,4},{6,7},{7,6},{8,9},{9,8},{10,11... | collective-permute-start | bytes 1327112 | tf_op jit(solution)/shard_map/ppermute | solution.py:399

commit v6 on v5

--- a/solution.py
+++ b/solution.py
@@ -36,24 +36,27 @@
     return lax.dot_general(a, b, dims, preferred_element_type=F32)
 
 
-def whole():
-    return pl.BlockSpec(memory_space=pltpu.VMEM)
-
-
-def call(kernel, out_shape, inputs, scratch=(), limit=32, flops=0, data=0, smem=(), far=()):
+def call(
+    kernel, out_shape, inputs, scratch=(), limit=32, flops=0, data=0, smem=(), far=(), far_out=()
+):
     spaces = {i: pltpu.SMEM for i in smem} | {i: pl.ANY for i in far}
-    specs = [
-        pl.BlockSpec(memory_space=spaces.get(i, pltpu.VMEM)) for i in range(len(inputs))
-    ]
-    return pl.pallas_call(
+    single = isinstance(out_shape, jax.ShapeDtypeStruct)
+    shapes = (out_shape,) if single else tuple(out_shape)
+    outs = pl.pallas_call(
         kernel,
-        out_shape=out_shape,
-        in_specs=specs,
-        out_specs=jax.tree.map(lambda _: whole(), out_shape),
+        out_shape=shapes,
+        in_specs=[
+            pl.BlockSpec(memory_space=spaces.get(i, pltpu.VMEM)) for i in range(len(inputs))
+        ],
+        out_specs=tuple(
+            pl.BlockSpec(memory_space=pl.ANY if i in far_out else pltpu.VMEM)
+            for i in range(len(shapes))
+        ),
         scratch_shapes=list(scratch),
         compiler_params=pltpu.CompilerParams(vmem_limit_bytes=limit * MIB),
         cost_estimate=pl.CostEstimate(flops=flops, bytes_accessed=data, transcendentals=0),
     )(*inputs)
+    return outs[0] if single else outs
 
 
 def pick(shape, target, along):
@@ -129,9 +132,9 @@
 
 
 def forward_kernel(
-    place_ref, core_ref, packed_ref, live_ref, first_q_ref, first_k_ref, first_v_ref, w_qkv_ref,
-    tokens_ref, masked_ref, joined_ref, probs_ref, own_ref, one_ref, two_ref, three_ref,
-    turned_ref, values_ref, attended_ref, weight_ref, sems,
+    core_ref, packed_ref, live_ref, first_q_ref, first_k_ref, first_v_ref, w_qkv_ref,
+    tokens_ref, masked_ref, joined_ref, probs_ref, sends_ref,
+    turned_ref, values_ref, attended_ref, rounded_ref, weight_ref, sems, send_sems,
 ):
     spans = [pl.ds(kind * D + chunk * WIDE, WIDE) for chunk in (1, 2) for kind in range(3)]
     copies = [
@@ -151,11 +154,14 @@
     for block in range(9):
         lanes = slice(block * 128, (block + 1) * 128)
         turned_ref[lanes, :] = masked[:, lanes].T.astype(BF)
-    me = place_ref[0]
-    sends = (own_ref, one_ref, two_ref, three_ref)
-    for step, out_ref in enumerate(sends):
-        start = pl.multiple_of((me + step) % 4 * COLS, 16)
-        out_ref[D:, :] = turned_ref[pl.ds(start, COLS), :]
+    slices = [
+        pltpu.make_async_copy(
+            turned_ref.at[pl.ds(part * COLS, COLS)], sends_ref.at[part, pl.ds(D, COLS)], send_sems.at[part]
+        )
+        for part in range(4)
+    ]
+    for copy in slices:
+        copy.start()
     patch = lane_patch()
     done = 0
     for chunk in range(3):
@@ -191,9 +197,15 @@
             for group in range(4):
                 at = group % 2 * HALF + head * 2 * OUT_ROWS + group // 2 * OUT_ROWS
                 attended_ref[at : at + OUT_ROWS, :] = attended[group * OUT_ROWS : (group + 1) * OUT_ROWS]
-    attended = attended_ref[...].astype(BF)
-    for out_ref in sends:
-        out_ref[:D, :] = attended
+    rounded_ref[...] = attended_ref[...].astype(BF)
+    wholes = [
+        pltpu.make_async_copy(rounded_ref, sends_ref.at[part, pl.ds(0, D)], send_sems.at[4 + part])
+        for part in range(4)
+    ]
+    for copy in wholes:
+        copy.start()
+    for copy in slices + wholes:
+        copy.wait()
 
 
 def backward_kernel(
@@ -280,12 +292,11 @@
         packed_ref[half * 16 * CHUNK : (half + 1) * 16 * CHUNK, :] = dot(chooser, stacked).astype(BF)
 
 
-def weight_kernel(other, core_ref, own_ref, one_ref, two_ref, three_ref, after_ref, terms_ref):
-    refs = (own_ref, one_ref, two_ref, three_ref)
+def weight_kernel(other, core_ref, gathered_ref, after_ref, terms_ref):
     core = 1 - core_ref[0] if other else core_ref[0]
     start = pl.multiple_of(core * HALF, HALF)
-    attended = jnp.concatenate([ref[pl.ds(start, HALF), :] for ref in refs], axis=1)
-    masked = jnp.concatenate([ref[D:, :] for ref in refs], axis=1)
+    attended = jnp.concatenate([gathered_ref[i, pl.ds(start, HALF), :] for i in range(4)], axis=1)
+    masked = jnp.concatenate([gathered_ref[i, D:, :] for i in range(4)], axis=1)
     masked = jnp.concatenate([masked[:256]] + [masked[256:]] * 4, axis=0)
     terms_ref[...] = dot(attended, masked, NT).astype(terms_ref.dtype)
 
@@ -327,7 +338,6 @@
 
 
 def body(tokens, d_out, frames, frame_order, w_qkv, w_out):
-    place = lax.axis_index("dp")
     core = lax.axis_index("core")
     shape = jax.ShapeDtypeStruct
     live = (frame_order[0] < frames[0]).astype(F32)
@@ -343,33 +353,33 @@
         packed.reshape(SLOTS, 8, D), ("y", "z"), split_axis=0, concat_axis=0, tiled=True
     ).reshape(256, D)
     firsts = tuple(w_qkv[:, kind * D : kind * D + WIDE] for kind in range(3))
-    kept, masked, joined, probs, own, one, two, three = call(
+    kept, masked, joined, probs, sends = call(
         forward_kernel,
         (
             shape((ROWS, D), BF),
             shape((ROWS, D), BF),
             shape((ROWS, 3 * D), BF),
             shape((H, SLOTS, ROWS), F32),
-        )
-        + (shape((PAYLOAD, ROWS), BF),) * 4,
-        (place.reshape(1), core.reshape(1), arrived, live[:, None]) + firsts + (w_qkv,),
+            shape((4, PAYLOAD, ROWS), BF),
+        ),
+        (core.reshape(1), arrived, live[:, None]) + firsts + (w_qkv,),
         scratch=(
             pltpu.VMEM((D, ROWS), BF),
             pltpu.VMEM((D, ROWS), F32),
             pltpu.VMEM((D, ROWS), F32),
+            pltpu.VMEM((D, ROWS), BF),
             pltpu.VMEM((D, 3 * D), BF),
             pltpu.SemaphoreType.DMA((6,)),
+            pltpu.SemaphoreType.DMA((8,)),
         ),
-        smem=(0, 1),
-        far=(7,),
-        limit=47,
+        smem=(0,),
+        far=(6,),
+        far_out=(4,),
+        limit=52,
         flops=int(2e9),
         data=int(14e6),
     )
-    ring = lambda step: [(i, (i + step) % 4) for i in range(4)]
-    from_one = lax.ppermute(one, "dp", ring(1))
-    from_two = lax.ppermute(two, "dp", ring(2))
-    from_three = lax.ppermute(three, "dp", ring(3))
+    gathered = lax.all_to_all(sends, "dp", split_axis=0, concat_axis=0, tiled=True)
     rows, places = call(
         backward_kernel,
         (shape((SLOTS * CHUNK, 128), BF), shape((8 * CHUNK, 3 * 8 * OUT_ROWS), BF)),
@@ -382,17 +392,16 @@
             pltpu.SemaphoreType.DMA((6,)),
         ),
         far=(4, 5),
-        limit=47,
+        limit=52,
         flops=int(3e9),
         data=int(16e6),
     )
-    payloads = (own, from_one, from_two, from_three)
     send = call(
         functools.partial(weight_kernel, True),
         shape((SLOTS * OUT_ROWS, WIDE), BF),
-        (core.reshape(1),) + payloads + (rows,),
+        (core.reshape(1), gathered, rows),
         smem=(0,),
-        far=(5,),
+        far=(2,),
         flops=int(1e9),
         data=int(4e6),
     )
@@ -400,9 +409,9 @@
     keep = call(
         functools.partial(weight_kernel, False),
         shape((SLOTS * OUT_ROWS, WIDE), F32),
-        (core.reshape(1),) + payloads + (send,),
+        (core.reshape(1), gathered, send),
         smem=(0,),
-        far=(5,),
+        far=(2,),
         flops=int(1e9),
         data=int(4e6),
     )

time: 89.8 us -> 96.3 us (1.072)
  Pallas kernels: 21.4 us -> 26.5 us
  waiting for transfers between devices: 19.7 us -> 21.2 us
  starting transfers between devices: 17.2 us -> 15.8 us
  local copies, waits for them, and re-layouts: 2.08 us -> 3.4 us
    ppermute x3 -> x0, starting transfers between devices: 5.73 us -> none  [the longest x1 2.73 us: body(): from_two = lax.ppermute(two, 'dp', ring(2))]
    all_to_all x0 -> x1, waiting for transfers between devices: none -> 5.59 us  [body(): lax.all_to_all(sends, 'dp', split_axis=0, concat_axis=0, tiled=True)]
    pallas_call x7, Pallas kernels: 21.4 us -> 26.5 us  [call(): pl.pallas_call(kernel, out_shape=shapes, in_specs=[pl.BlockSpec(memory_sp...]
    all_to_all x0 -> x1, starting transfers between devices: none -> 4.3 us  [body(): lax.all_to_all(sends, 'dp', split_axis=0, concat_axis=0, tiled=True)]
    ppermute x3 -> x0, waiting for transfers between devices: 2.85 us -> none  [the longest x1 2.84 us: body(): from_two = lax.ppermute(two, 'dp', ring(2))]
    slice x1, local copies, waits for them, and re-layouts: 1.98 us -> 3.3 us  [body(): firsts = tuple((w_qkv[:, kind * D:kind * D + WIDE] for kind in range(3)))]
    all_to_all x1, waiting for transfers between devices: 15.6 us -> 14.3 us  [body(): lax.all_to_all(packed.reshape(SLOTS, 8, D), ('y', 'z'), split_axis=0, con...]
  transfers between devices with their start and end apart: 5 -> 3, of which waited for: 3 -> 3; matrix products, arithmetic and copies ran while one was open for 3% -> 4% of each run, Pallas kernels for 11% -> 13%
where the time goes in v6:
time: 96.3 us; the launch traced here: 95.9 us
  blocking collectives  27 us (28%)
  Pallas kernels  26.5 us (28%)
  waiting for transfers between devices  21.2 us (22%)
  starting transfers between devices  15.8 us (16%)
  local copies, waits for them, and re-layouts  3.4 us (4%)
  between operations  1.35 us (1%)
    all_to_all x1, blocking collectives, body(): lax.all_to_all(merged.reshape(SLOTS, CHUNK, 128), ('y', 'z'), split_axis=...  27 us
    pallas_call x7, Pallas kernels, call(): pl.pallas_call(kernel, out_shape=shapes, in_specs=[pl.BlockSpec(memory_sp...  26.5 us
    all_to_all x1, waiting for transfers between devices, body(): lax.all_to_all(packed.reshape(SLOTS, 8, D), ('y', 'z'), split_axis=0, con...  14.3 us
    all_to_all x1, starting transfers between devices, body(): lax.all_to_all(packed.reshape(SLOTS, 8, D), ('y', 'z'), split_axis=0, con...  11.4 us
    all_to_all x1, waiting for transfers between devices, body(): lax.all_to_all(sends, 'dp', split_axis=0, concat_axis=0, tiled=True)  5.59 us
    all_to_all x1, starting transfers between devices, body(): lax.all_to_all(sends, 'dp', split_axis=0, concat_axis=0, tiled=True)  4.3 us
    slice x1, local copies, waits for them, and re-layouts, body(): firsts = tuple((w_qkv[:, kind * D:kind * D + WIDE] for kind in range(3)))  3.3 us
  transfers between devices with their start and end apart: 3, of which 3 were waited for; matrix products, arithmetic and copies ran while one was open for 4% of the time, Pallas kernels for 13%

profile of v6, /device:TPU:32, one launch (start us, length us, event | category | flops | bytes accessed | tf_op | source)
XLA Modules:
  0.0 95.9 jit_solution(1268467863793767380)
XLA Ops:
  0.6 2.2 %shard_map.77 = bf16[256,1152]{1,0:T(8,128)(2,1)} custom-call(bf16[128,1152]{1,0:T(8,128)(2,1)} %bitcast.16, bf16[128,1152]{1,0:T(8,128)(2,1)} %bitcast.17), custom_call_target="tpu_custom_call" | custom-call | tf_op jit(solution)/shard_map/pallas_call | solution.py:45
  2.9 11.4 %all-to-all-start = ((bf16[32,8,1152]{2,1,0:T(8,128)(2,1)}), bf16[32,8,1152]{2,1,0:T(8,128)(2,1)S(1)}, u32[]{:S(2)}, u32[]{:S(2)}) async-start(bf16[32,8,1152]{2,1,0:T(8,128)(2,1)} %bitcast.15), calls=%async_computation | async-start | bytes 1179648 | tf_op jit(solution)/shard_map/all_to_all | solution.py:352
  14.9 0.7 fusion
  15.6 0.1 copy.8.live_ref
  15.6 3.3 %fusion.1 = (bf16[1152,384]{1,0:T(8,128)(2,1)}, bf16[1152,384]{1,0:T(8,128)(2,1)}, bf16[1152,384]{1,0:T(8,128)(2,1)}) fusion(bf16[1152,3456]{1,0:T(8,128)(2,1)} %w_qkv_ref.3), kind=kLoop, calls=%fused_computation.2 | loop fusion | bytes 5308416 | tf_op jit(solution)/shard_map/slice | solution.py:355
  18.9 14.3 %all-to-all-done = bf16[32,8,1152]{2,1,0:T(8,128)(2,1)S(1)} async-done(((bf16[32,8,1152]{2,1,0:T(8,128)(2,1)}), bf16[32,8,1152]{2,1,0:T(8,128)(2,1)S(1)}, u32[]{:S(2)}, u32[]{:S(2)}) %all-to-all-start) | async-done | bytes 589856 | tf_op jit(solution)/shard_map/all_to_all | solution.py:352
  33.3 9.6 %shard_map.78 = (bf16[128,1152]{1,0:T(8,128)(2,1)S(1)}, bf16[128,1152]{1,0:T(8,128)(2,1)S(1)}, bf16[128,3456]{1,0:T(8,128)(2,1)}, f32[16,32,128]{2,1,0:T(8,128)S(1)}, bf16[4,1440,128]{2,1,0:T(8,128)(2,1)}) custom-call(s32[1]{0:T(128)} %bitcast.core_ref, bf16[256,1152]{1,0:T(8,128)(2,1)S(1)} %bitcast.14, f32[32,1]{1,0:T(8,128)S(1)} %copy.8.live_ref, ...), custom_call_target="tpu_custom_call" | custom-call | flops 2000000000 | bytes 14000000 | tf_op jit(solution)/shard_map/pallas_call | solution.py:45
  42.8 4.3 %all-to-all-start.1 = ((bf16[4,1440,128]{2,1,0:T(8,128)(2,1)}), bf16[4,1440,128]{2,1,0:T(8,128)(2,1)S(1)}, u32[]{:S(2)}, u32[]{:S(2)}) async-start(bf16[4,1440,128]{2,1,0:T(8,128)(2,1)} %get-tuple-element.16), calls=%async_computation.1 | async-start | bytes 2949120 | tf_op jit(solution)/shard_map/all_to_all | solution.py:382
  47.1 11.6 %shard_map.79 = (bf16[2560,128]{1,0:T(8,128)(2,1)S(1)}, bf16[640,432]{1,0:T(8,128)(2,1)}) custom-call(bf16[128,1152]{1,0:T(8,128)(2,1)S(1)} %get-tuple-element.11.tokens_ref, bf16[128,1152]{1,0:T(8,128)(2,1)S(1)} %get-tuple-element.12.masked_ref, bf16[128,3456]{1,0:T(8,128)(2,1)} %get-tuple-element.13.joined_ref, ...), custom_call_target="tpu_custom_call" | custom-call | flops 3000000000 | bytes 16000000 | tf_op jit(solution)/shard_map/pallas_call | solution.py:45
  58.7 5.6 %all-to-all-done.1.gathered_ref = bf16[4,1440,128]{2,1,0:T(8,128)(2,1)S(1)} async-done(((bf16[4,1440,128]{2,1,0:T(8,128)(2,1)}), bf16[4,1440,128]{2,1,0:T(8,128)(2,1)S(1)}, u32[]{:S(2)}, u32[]{:S(2)}) %all-to-all-start.1) | async-done | bytes 1474592 | tf_op jit(solution)/shard_map/all_to_all | solution.py:382
  64.3 0.5 shard_map.80.after_ref
  64.8 0.0 copy-start
  64.8 0.1 collective-permute-start
  64.9 0.5 shard_map.81.keep_ref
  65.4 1.3 %collective-permute-done.got_ref = bf16[576,384]{1,0:T(8,128)(2,1)S(1)} collective-permute-done((bf16[576,384]{1,0:T(8,128)(2,1)S(1)}, bf16[576,384]{1,0:T(8,128)(2,1)S(1)}, u32[]{:S(2)}, u32[]{:S(2)}) %collective-permute-start) | collective-permute-done | bytes 442400 | tf_op jit(solution)/shard_map/ppermute | solution.py:408
  66.7 0.0 copy-done
  66.7 0.9 shard_map.82
  67.6 27.0 %all_to_all.15 = bf16[32,80,128]{2,1,0:T(8,128)(2,1)S(1)} all-to-all(bf16[32,80,128]{2,1,0:T(8,128)(2,1)S(1)} %bitcast.13), channel_id=1, replica_groups=mesh['dp'=4,'y'=4,'z'=8,'core'=2] {'y','z'}, dimensions={0} | all-to-all | bytes 1310720 | tf_op jit(solution)/shard_map/all_to_all | solution.py:421
  94.6 1.3 %shard_map.83 = (bf16[128,1152]{1,0:T(8,128)(2,1)}, f32[18,288]{1,0:T(8,128)}) custom-call(bf16[2560,128]{1,0:T(8,128)(2,1)S(1)} %bitcast.12), custom_call_target="tpu_custom_call" | custom-call | tf_op jit(solution)/shard_map/pallas_call | solution.py:45
Async XLA Ops:
  2.9 30.4 %all-to-all-start = ((bf16[32,8,1152]{2,1,0:T(8,128)(2,1)}), bf16[32,8,1152]{2,1,0:T(8,128)(2,1)S(1)}, u32[]{:S(2)}, u32[]{:S(2)}) async-start(bf16[32,8,1152]{2,1,0:T(8,128)(2,1)} %bitcast.15), calls=%async_computation | async-start | bytes 1179648 | tf_op jit(solution)/shard_map/all_to_all | solution.py:352
  42.8 21.5 %all-to-all-start.1 = ((bf16[4,1440,128]{2,1,0:T(8,128)(2,1)}), bf16[4,1440,128]{2,1,0:T(8,128)(2,1)S(1)}, u32[]{:S(2)}, u32[]{:S(2)}) async-start(bf16[4,1440,128]{2,1,0:T(8,128)(2,1)} %get-tuple-element.16), calls=%async_computation.1 | async-start | bytes 2949120 | tf_op jit(solution)/shard_map/all_to_all | solution.py:382
  64.8 1.9 %copy-start = (bf16[640,432]{1,0:T(8,128)(2,1)S(1)}, bf16[640,432]{1,0:T(8,128)(2,1)}, u32[]{:S(2)}) copy-start(bf16[640,432]{1,0:T(8,128)(2,1)} %get-tuple-element.17.place_ref) | copy-start | bytes 1658884
  64.8 1.9 %collective-permute-start = (bf16[576,384]{1,0:T(8,128)(2,1)S(1)}, bf16[576,384]{1,0:T(8,128)(2,1)S(1)}, u32[]{:S(2)}, u32[]{:S(2)}) collective-permute-start(bf16[576,384]{1,0:T(8,128)(2,1)S(1)} %shard_map.80.after_ref), channel_id=1, source_target_pairs={{0,1},{1,0},{2,3},{3,2},{4,5},{5,4},{6,7},{7,6},{8,9},{9,8},{10,11... | collective-permute-start | bytes 1327112 | tf_op jit(solution)/shard_map/ppermute | solution.py:408

commit v7 on v5

--- a/solution.py
+++ b/solution.py
@@ -130,7 +130,8 @@
 
 def forward_kernel(
     place_ref, core_ref, packed_ref, live_ref, first_q_ref, first_k_ref, first_v_ref, w_qkv_ref,
-    tokens_ref, masked_ref, joined_ref, probs_ref, own_ref, one_ref, two_ref, three_ref,
+    tokens_ref, masked_ref, joined_ref, probs_ref,
+    own_ref, right_far_ref, left_far_ref, right_ref, left_ref,
     turned_ref, values_ref, attended_ref, weight_ref, sems,
 ):
     spans = [pl.ds(kind * D + chunk * WIDE, WIDE) for chunk in (1, 2) for kind in range(3)]
@@ -152,10 +153,16 @@
         lanes = slice(block * 128, (block + 1) * 128)
         turned_ref[lanes, :] = masked[:, lanes].T.astype(BF)
     me = place_ref[0]
-    sends = (own_ref, one_ref, two_ref, three_ref)
-    for step, out_ref in enumerate(sends):
-        start = pl.multiple_of((me + step) % 4 * COLS, 16)
-        out_ref[D:, :] = turned_ref[pl.ds(start, COLS), :]
+
+    def slice_for(step, first, size):
+        start = pl.multiple_of((me + step) % 4 * COLS, 16) + first
+        return turned_ref[pl.ds(pl.multiple_of(start, 16), size), :]
+
+    own_ref[D:, :] = slice_for(0, 0, COLS)
+    right_ref[HALF:, :] = slice_for(1, 0, COLS)
+    left_ref[HALF:, :] = slice_for(3, 0, COLS)
+    right_far_ref[HALF:, :] = slice_for(2, 0, COLS // 2)
+    left_far_ref[HALF:, :] = slice_for(2, COLS // 2, COLS // 2)
     patch = lane_patch()
     done = 0
     for chunk in range(3):
@@ -192,44 +199,18 @@
                 at = group % 2 * HALF + head * 2 * OUT_ROWS + group // 2 * OUT_ROWS
                 attended_ref[at : at + OUT_ROWS, :] = attended[group * OUT_ROWS : (group + 1) * OUT_ROWS]
     attended = attended_ref[...].astype(BF)
-    for out_ref in sends:
-        out_ref[:D, :] = attended
-
-
-def backward_kernel(
-    tokens_ref, masked_ref, joined_ref, probs_ref, w_qkv_ref, w_out_ref,
-    packed_ref, place_ref,
-    grad_ref, head_ref, weight_ref, out_weight_ref, sems,
-):
-    out_copies = [
-        pltpu.make_async_copy(
-            w_out_ref.at[pl.ds(chunk * WIDE, WIDE)],
-            out_weight_ref.at[pl.ds(chunk * WIDE, WIDE)],
-            sems.at[chunk],
-        )
-        for chunk in range(3)
-    ]
-    qkv_copies = [
-        pltpu.make_async_copy(
-            w_qkv_ref.at[pl.ds(chunk * WIDE, WIDE)],
-            weight_ref.at[pl.ds(chunk * WIDE, WIDE)],
-            sems.at[3 + chunk],
-        )
-        for chunk in range(3)
-    ]
-    for copy in out_copies + qkv_copies:
-        copy.start()
-    term = lane_index(3 * 8 * OUT_ROWS)
-    kind, inner = term // (8 * OUT_ROWS), term % (8 * OUT_ROWS)
-    row = inner % OUT_ROWS
-    at = TOKEN_ROWS + kind * OUT_ROWS + jnp.where(kind == 2, row // 4, row)
-    place_ref[...] = pick((8 * CHUNK, 3 * 8 * OUT_ROWS), inner // OUT_ROWS * CHUNK + at, 0)
+    own_ref[:D, :] = attended
+    right_far_ref[:HALF, :] = attended[:HALF]
+    left_far_ref[:HALF, :] = attended[HALF:]
+    right_ref[:HALF, :] = attended[HALF:]
+    left_ref[:HALF, :] = attended[:HALF]
+
+
+def attention_grad_kernel(masked_ref, joined_ref, probs_ref, w_out_ref, grad_ref, head_ref):
     masked = masked_ref[...]
-    for copy in out_copies:
-        copy.wait()
     for chunk in range(3):
         columns = slice(chunk * WIDE, (chunk + 1) * WIDE)
-        head_ref[:, columns] = dot(masked, out_weight_ref[columns, :], NT).astype(BF)
+        head_ref[:, columns] = dot(masked, w_out_ref[columns, :], NT).astype(BF)
     patch = lane_patch()
     for head in range(H):
         base, width, inside = window(head)
@@ -252,12 +233,21 @@
                 grad_ref[:, at : at + width] = part
             else:
                 grad_ref[:, at : at + width] = jnp.where(inside, part, grad_ref[:, at : at + width])
+
+
+def token_grad_kernel(
+    tokens_ref, masked_ref, grad_ref, w_qkv_ref, after_ref, also_after_ref, packed_ref, place_ref
+):
+    term = lane_index(3 * 8 * OUT_ROWS)
+    kind, inner = term // (8 * OUT_ROWS), term % (8 * OUT_ROWS)
+    row = inner % OUT_ROWS
+    at = TOKEN_ROWS + kind * OUT_ROWS + jnp.where(kind == 2, row // 4, row)
+    place_ref[...] = pick((8 * CHUNK, 3 * 8 * OUT_ROWS), inner // OUT_ROWS * CHUNK + at, 0)
+    masked = masked_ref[...]
     pieces = []
-    for copy in qkv_copies:
-        copy.wait()
     for chunk in range(3):
         rows = slice(chunk * WIDE, (chunk + 1) * WIDE)
-        pieces.append(dot(grad_ref[...], weight_ref[rows, :], NT))
+        pieces.append(dot(grad_ref[...], w_qkv_ref[rows, :], NT))
     normed_grad = jnp.concatenate(pieces, axis=1)
     normalized, inverse = row_stats(tokens_ref[...])
     mean_grad = jnp.mean(normed_grad, axis=-1, keepdims=True)
@@ -280,12 +270,22 @@
         packed_ref[half * 16 * CHUNK : (half + 1) * 16 * CHUNK, :] = dot(chooser, stacked).astype(BF)
 
 
-def weight_kernel(other, core_ref, own_ref, one_ref, two_ref, three_ref, after_ref, terms_ref):
-    refs = (own_ref, one_ref, two_ref, three_ref)
+def weight_kernel(
+    other, core_ref, own_ref, left_a_ref, left_b_ref, right_a_ref, right_b_ref, far_a_ref, far_b_ref,
+    after_ref, terms_ref,
+):
     core = 1 - core_ref[0] if other else core_ref[0]
     start = pl.multiple_of(core * HALF, HALF)
-    attended = jnp.concatenate([ref[pl.ds(start, HALF), :] for ref in refs], axis=1)
-    masked = jnp.concatenate([ref[D:, :] for ref in refs], axis=1)
+    pairs = ((left_a_ref, left_b_ref), (right_b_ref, right_a_ref), (far_a_ref, far_b_ref))
+    attended = jnp.concatenate(
+        [own_ref[pl.ds(start, HALF), :]]
+        + [jnp.where(core == 0, first[:HALF, :], second[:HALF, :]) for first, second in pairs],
+        axis=1,
+    )
+    far = jnp.concatenate([far_a_ref[HALF:, :], far_b_ref[HALF:, :]], axis=0)
+    masked = jnp.concatenate(
+        [own_ref[D:, :], left_b_ref[HALF:, :], right_b_ref[HALF:, :], far], axis=1
+    )
     masked = jnp.concatenate([masked[:256]] + [masked[256:]] * 4, axis=0)
     terms_ref[...] = dot(attended, masked, NT).astype(terms_ref.dtype)
 
@@ -343,15 +343,17 @@
         packed.reshape(SLOTS, 8, D), ("y", "z"), split_axis=0, concat_axis=0, tiled=True
     ).reshape(256, D)
     firsts = tuple(w_qkv[:, kind * D : kind * D + WIDE] for kind in range(3))
-    kept, masked, joined, probs, own, one, two, three = call(
+    kept, masked, joined, probs, own, right_far, left_far, right, left = call(
         forward_kernel,
         (
             shape((ROWS, D), BF),
             shape((ROWS, D), BF),
             shape((ROWS, 3 * D), BF),
             shape((H, SLOTS, ROWS), F32),
+            shape((PAYLOAD, ROWS), BF),
         )
-        + (shape((PAYLOAD, ROWS), BF),) * 4,
+        + (shape((HALF + COLS // 2, ROWS), BF),) * 2
+        + (shape((HALF + COLS, ROWS), BF),) * 2,
         (place.reshape(1), core.reshape(1), arrived, live[:, None]) + firsts + (w_qkv,),
         scratch=(
             pltpu.VMEM((D, ROWS), BF),
@@ -366,33 +368,39 @@
         flops=int(2e9),
         data=int(14e6),
     )
-    ring = lambda step: [(i, (i + step) % 4) for i in range(4)]
-    from_one = lax.ppermute(one, "dp", ring(1))
-    from_two = lax.ppermute(two, "dp", ring(2))
-    from_three = lax.ppermute(three, "dp", ring(3))
-    rows, places = call(
-        backward_kernel,
-        (shape((SLOTS * CHUNK, 128), BF), shape((8 * CHUNK, 3 * 8 * OUT_ROWS), BF)),
-        (kept, masked, joined, probs, w_qkv, w_out),
-        scratch=(
-            pltpu.VMEM((ROWS, 3 * D), BF),
-            pltpu.VMEM((ROWS, D), BF),
-            pltpu.VMEM((D, 3 * D), BF),
-            pltpu.VMEM((D, D), BF),
-            pltpu.SemaphoreType.DMA((6,)),
-        ),
-        far=(4, 5),
-        limit=47,
+    up = [(i, (i + 1) % 4) for i in range(4)]
+    down = [(i, (i + 3) % 4) for i in range(4)]
+    left_a = lax.ppermute(right_far, "dp", up)
+    right_a = lax.ppermute(left_far, "dp", down)
+    left_b = lax.ppermute(right, "dp", up)
+    right_b = lax.ppermute(left, "dp", down)
+    grads = call(
+        attention_grad_kernel,
+        shape((ROWS, 3 * D), BF),
+        (masked, joined, probs, w_out),
+        scratch=(pltpu.VMEM((ROWS, D), BF),),
+        limit=24,
         flops=int(3e9),
         data=int(16e6),
     )
-    payloads = (own, from_one, from_two, from_three)
+    far_a = lax.ppermute(left_a, "dp", up)
+    far_b = lax.ppermute(right_a, "dp", down)
+    rows, places = call(
+        token_grad_kernel,
+        (shape((SLOTS * CHUNK, 128), BF), shape((8 * CHUNK, 3 * 8 * OUT_ROWS), BF)),
+        (kept, masked, grads, w_qkv, left_a, right_a),
+        far=(4, 5),
+        limit=24,
+        flops=int(3e9),
+        data=int(16e6),
+    )
+    payloads = (own, left_a, left_b, right_a, right_b, far_a, far_b)
     send = call(
         functools.partial(weight_kernel, True),
         shape((SLOTS * OUT_ROWS, WIDE), BF),
         (core.reshape(1),) + payloads + (rows,),
         smem=(0,),
-        far=(5,),
+        far=(8,),
         flops=int(1e9),
         data=int(4e6),
     )
@@ -402,7 +410,7 @@
         shape((SLOTS * OUT_ROWS, WIDE), F32),
         (core.reshape(1),) + payloads + (send,),
         smem=(0,),
-        far=(5,),
+        far=(8,),
         flops=int(1e9),
         data=int(4e6),
     )

time: 89.8 us -> 88.9 us (0.990)
  starting transfers between devices: 17.2 us -> 21.3 us
  waiting for transfers between devices: 19.7 us -> 16.9 us
  blocking collectives: 27 us -> 25.3 us
    ppermute x3 -> x6, starting transfers between devices: 5.73 us -> 9.85 us  [the longest x1 3.22 us: body(): far_b = lax.ppermute(right_a, 'dp', down)]
    ppermute x3 -> x6, waiting for transfers between devices: 2.85 us -> 0.02 us  [the longest x1 0.01 us: body(): left_a = lax.ppermute(right_far, 'dp', up)]
    all_to_all x1, blocking collectives: 27 us -> 25.3 us  [body(): lax.all_to_all(merged.reshape(SLOTS, CHUNK, 128), ('y', 'z'), split_axis=...]
    pallas_call x7 -> x8, Pallas kernels: 21.4 us -> 20.9 us  [call(): pl.pallas_call(kernel, out_shape=out_shape, in_specs=specs, out_specs=jax...]
  transfers between devices with their start and end apart: 5 -> 8, of which waited for: 3 -> 2; matrix products, arithmetic and copies ran while one was open for 3% -> 3% of each run, Pallas kernels for 11% -> 10%
where the time goes in v7:
time: 88.9 us; the launch traced here: 88.6 us
  blocking collectives  25.3 us (28%)
  starting transfers between devices  21.3 us (24%)
  Pallas kernels  20.9 us (24%)
  waiting for transfers between devices  16.9 us (19%)
  local copies, waits for them, and re-layouts  2.09 us (2%)
  between operations  1.42 us (2%)
    all_to_all x1, blocking collectives, body(): lax.all_to_all(merged.reshape(SLOTS, CHUNK, 128), ('y', 'z'), split_axis=...  25.3 us
    pallas_call x8, Pallas kernels, call(): pl.pallas_call(kernel, out_shape=out_shape, in_specs=specs, out_specs=jax...  20.9 us
    all_to_all x1, waiting for transfers between devices, body(): lax.all_to_all(packed.reshape(SLOTS, 8, D), ('y', 'z'), split_axis=0, con...  15.6 us
    all_to_all x1, starting transfers between devices, body(): lax.all_to_all(packed.reshape(SLOTS, 8, D), ('y', 'z'), split_axis=0, con...  11.4 us
    ppermute x1, starting transfers between devices, body(): far_b = lax.ppermute(right_a, 'dp', down)  3.22 us
    ppermute x1, starting transfers between devices, body(): right_b = lax.ppermute(left, 'dp', down)  2.96 us
    slice x1, local copies, waits for them, and re-layouts, body(): firsts = tuple((w_qkv[:, kind * D:kind * D + WIDE] for kind in range(3)))  1.98 us
  transfers between devices with their start and end apart: 8, of which 2 were waited for; matrix products, arithmetic and copies ran while one was open for 3% of the time, Pallas kernels for 10%

profile of v7, /device:TPU:32, one launch (start us, length us, event | category | flops | bytes accessed | tf_op | source)
XLA Modules:
  0.0 88.6 jit_solution(7074030323973237447)
XLA Ops:
  0.6 2.2 %shard_map.77 = bf16[256,1152]{1,0:T(8,128)(2,1)} custom-call(bf16[128,1152]{1,0:T(8,128)(2,1)} %bitcast.19, bf16[128,1152]{1,0:T(8,128)(2,1)} %bitcast.20), custom_call_target="tpu_custom_call" | custom-call | tf_op jit(solution)/shard_map/pallas_call | solution.py:48
  2.9 11.4 %all-to-all-start = ((bf16[32,8,1152]{2,1,0:T(8,128)(2,1)}), bf16[32,8,1152]{2,1,0:T(8,128)(2,1)S(1)}, u32[]{:S(2)}, u32[]{:S(2)}) async-start(bf16[32,8,1152]{2,1,0:T(8,128)(2,1)} %bitcast.18), calls=%async_computation | async-start | bytes 1179648 | tf_op jit(solution)/shard_map/all_to_all | solution.py:342
  14.9 0.7 fusion
  15.6 0.1 copy.8.live_ref
  15.7 2.0 %fusion.1 = (bf16[1152,384]{1,0:T(8,128)(2,1)S(1)}, bf16[1152,384]{1,0:T(8,128)(2,1)S(1)}, bf16[1152,384]{1,0:T(8,128)(2,1)S(1)}) fusion(bf16[1152,3456]{1,0:T(8,128)(2,1)} %w_qkv_ref.3), kind=kLoop, calls=%fused_computation.2 | loop fusion | bytes 5308416 | tf_op jit(solution)/shard_map/slice | solution.py:345
  17.6 15.6 %all-to-all-done = bf16[32,8,1152]{2,1,0:T(8,128)(2,1)S(1)} async-done(((bf16[32,8,1152]{2,1,0:T(8,128)(2,1)}), bf16[32,8,1152]{2,1,0:T(8,128)(2,1)S(1)}, u32[]{:S(2)}, u32[]{:S(2)}) %all-to-all-start) | async-done | bytes 589856 | tf_op jit(solution)/shard_map/all_to_all | solution.py:342
  33.3 0.0 copy-start
  33.3 0.0 slice-start
  33.3 0.0 slice-start.1
  33.3 6.8 %shard_map.78 = (bf16[128,1152]{1,0:T(8,128)(2,1)S(1)}, bf16[128,1152]{1,0:T(8,128)(2,1)S(1)}, bf16[128,3456]{1,0:T(8,128)(2,1)S(1)}, f32[16,32,128]{2,1,0:T(8,1...) custom-call(s32[1]{0:T(128)} %bitcast.place_ref, ...), custom_call_target="tpu_custom_call" | custom-call | flops 2000000000 | bytes 14000000 | tf_op jit(solution)/shard_map/pallas_call | solution.py:48
  40.0 1.6 %collective-permute-start = (bf16[720,128]{1,0:T(8,128)(2,1)S(1)}, bf16[720,128]{1,0:T(8,128)(2,1)S(1)}, u32[]{:S(2)}, u32[]{:S(2)}) collective-permute-start(bf16[720,128]{1,0:T(8,128)(2,1)S(1)} %get-tuple-element.19), channel_id=1, source_target_pairs={{0,64},{64,128},{128,192},{192,0},{1,65},{65,129},{129,193},{193,1... | collective-permute-start | bytes 552968 | tf_op jit(solution)/shard_map/ppermute | solution.py:373
  41.6 1.7 %collective-permute-start.1 = (bf16[720,128]{1,0:T(8,128)(2,1)S(1)}, bf16[720,128]{1,0:T(8,128)(2,1)S(1)}, u32[]{:S(2)}, u32[]{:S(2)}) collective-permute-start(bf16[720,128]{1,0:T(8,128)(2,1)S(1)} %get-tuple-element.20), channel_id=1, source_target_pairs={{0,192},{64,0},{128,64},{192,128},{1,193},{65,1},{129,65},{193,129... | collective-permute-start | bytes 552968 | tf_op jit(solution)/shard_map/ppermute | solution.py:374
  43.4 0.3 collective-permute-start.2
  43.6 3.0 %collective-permute-start.3 = (bf16[864,128]{1,0:T(8,128)(2,1)S(1)}, bf16[864,128]{1,0:T(8,128)(2,1)S(1)}, u32[]{:S(2)}, u32[]{:S(2)}) collective-permute-start(bf16[864,128]{1,0:T(8,128)(2,1)S(1)} %get-tuple-element.24), channel_id=1, source_target_pairs={{0,192},{64,0},{128,64},{192,128},{1,193},{65,1},{129,65},{193,129... | collective-permute-start | bytes 663560 | tf_op jit(solution)/shard_map/ppermute | solution.py:376
  46.6 0.0 copy-done
  46.6 4.6 %shard_map.79.grad_ref = bf16[128,3456]{1,0:T(8,128)(2,1)S(1)} custom-call(bf16[128,1152]{1,0:T(8,128)(2,1)S(1)} %get-tuple-element.16.masked_ref, bf16[128,3456]{1,0:T(8,128)(2,1)S(1)} %get-tuple-element.17.joined_ref, f32[16,32,128]{2,1,0:T(8,128)S(1)} %get-tuple-element.18.probs_ref, bf16[1152,1152]{1,0:T(8,128)(2,1)S(1)} %copy-done), custom_call_target="tpu_custom_call" | custom-call | flops 3000000000 | bytes 16000000 | tf_op jit(solution)/shard_map/pallas_call | solution.py:48
  51.2 0.0 collective-permute-done.after_ref.left_a_ref
  51.2 0.1 collective-permute-start.4
  51.3 0.0 collective-permute-done.1.also_after_ref.right_a_ref
  51.3 3.2 %collective-permute-start.5 = (bf16[720,128]{1,0:T(8,128)(2,1)S(1)}, bf16[720,128]{1,0:T(8,128)(2,1)S(1)}, u32[]{:S(2)}, u32[]{:S(2)}) collective-permute-start(bf16[720,128]{1,0:T(8,128)(2,1)S(1)} %collective-permute-done.1.also_after_ref.right_a_ref), channel_id=1, source_target_pairs={{0,192},{64,0},{128,64},{192,128},{1,193},{65,1},{129,65},{193,129... | collective-permute-start | bytes 552968 | tf_op jit(solution)/shard_map/ppermute | solution.py:387
  54.5 0.0 slice-done
  54.5 0.0 slice-done.1
  54.5 4.2 %shard_map.80 = (bf16[2560,128]{1,0:T(8,128)(2,1)S(1)}, bf16[640,432]{1,0:T(8,128)(2,1)S(1)}) custom-call(bf16[128,1152]{1,0:T(8,128)(2,1)S(1)} %get-tuple-element.15.tokens_ref, bf16[128,1152]{1,0:T(8,128)(2,1)S(1)} %get-tuple-element.16.masked_ref, bf16[128,3456]{1,0:T(8,128)(2,1)S(1)} %shard_map.79.grad_ref, bf16[1152,3456]{1,0:T(8,128)(2,1)S(1)} %bitcast.14, ...), custom_call_target="tpu_custom_call" | custom-call | flops 3000000000 | bytes 16000000 | tf_op jit(solution)/shard_map/pallas_call | solution.py:48
  58.8 0.0 collective-permute-done.2.left_b_ref
  58.8 0.0 collective-permute-done.3.right_b_ref
  58.8 0.0 collective-permute-done.4.far_a_ref
  58.8 0.0 collective-permute-done.5.far_b_ref
  58.8 0.5 shard_map.81.after_ref
  59.3 0.1 collective-permute-start.6
  59.4 0.5 shard_map.82.keep_ref
  59.9 1.3 %collective-permute-done.6.got_ref = bf16[576,384]{1,0:T(8,128)(2,1)S(1)} collective-permute-done((bf16[576,384]{1,0:T(8,128)(2,1)S(1)}, bf16[576,384]{1,0:T(8,128)(2,1)S(1)}, u32[]{:S(2)}, u32[]{:S(2)}) %collective-permute-start.6) | collective-permute-done | bytes 442400 | tf_op jit(solution)/shard_map/ppermute | solution.py:407
  61.2 0.9 shard_map.83
  62.1 25.3 %all_to_all.10 = bf16[32,80,128]{2,1,0:T(8,128)(2,1)S(1)} all-to-all(bf16[32,80,128]{2,1,0:T(8,128)(2,1)S(1)} %bitcast.16), channel_id=1, replica_groups=mesh['dp'=4,'y'=4,'z'=8,'core'=2] {'y','z'}, dimensions={0} | all-to-all | bytes 1310720 | tf_op jit(solution)/shard_map/all_to_all | solution.py:420
  87.3 1.3 %shard_map.84 = (bf16[128,1152]{1,0:T(8,128)(2,1)}, f32[18,288]{1,0:T(8,128)}) custom-call(bf16[2560,128]{1,0:T(8,128)(2,1)S(1)} %bitcast.15), custom_call_target="tpu_custom_call" | custom-call | tf_op jit(solution)/shard_map/pallas_call | solution.py:48
  (1 shorter events, 0.0 us)
Async XLA Ops:
  2.9 30.4 %all-to-all-start = ((bf16[32,8,1152]{2,1,0:T(8,128)(2,1)}), bf16[32,8,1152]{2,1,0:T(8,128)(2,1)S(1)}, u32[]{:S(2)}, u32[]{:S(2)}) async-start(bf16[32,8,1152]{2,1,0:T(8,128)(2,1)} %bitcast.18), calls=%async_computation | async-start | bytes 1179648 | tf_op jit(solution)/shard_map/all_to_all | solution.py:342
  33.3 13.3 %copy-start = (bf16[1152,1152]{1,0:T(8,128)(2,1)S(1)}, bf16[1152,1152]{1,0:T(8,128)(2,1)}, u32[]{:S(2)}) copy-start(bf16[1152,1152]{1,0:T(8,128)(2,1)} %w_out_ref.1) | copy-start | bytes 7962628
  33.3 21.2 %slice-start = ((s8[7962624]{0:T(1024)(128)(4,1)}), s8[4194304]{0:T(1024)(128)(4,1)S(1)}, s32[]{:S(2)}) async-start(s8[7962624]{0:T(1024)(128)(4,1)} %bitcast.13), calls=%async_computation.2 | async-start | bytes 8388608
  33.3 21.2 %slice-start.1 = ((s8[7962624]{0:T(1024)(128)(4,1)}), s8[3768320]{0:T(1024)(128)(4,1)S(1)}, s32[]{:S(2)}) async-start(s8[7962624]{0:T(1024)(128)(4,1)} %bitcast.13), calls=%async_computation.3 | async-start | bytes 7536640
  40.0 11.1 %collective-permute-start = (bf16[720,128]{1,0:T(8,128)(2,1)S(1)}, bf16[720,128]{1,0:T(8,128)(2,1)S(1)}, u32[]{:S(2)}, u32[]{:S(2)}) collective-permute-start(bf16[720,128]{1,0:T(8,128)(2,1)S(1)} %get-tuple-element.19), channel_id=1, source_target_pairs={{0,64},{64,128},{128,192},{192,0},{1,65},{65,129},{129,193},{193,1... | collective-permute-start | bytes 552968 | tf_op jit(solution)/shard_map/ppermute | solution.py:373
  41.6 9.7 %collective-permute-start.1 = (bf16[720,128]{1,0:T(8,128)(2,1)S(1)}, bf16[720,128]{1,0:T(8,128)(2,1)S(1)}, u32[]{:S(2)}, u32[]{:S(2)}) collective-permute-start(bf16[720,128]{1,0:T(8,128)(2,1)S(1)} %get-tuple-element.20), channel_id=1, source_target_pairs={{0,192},{64,0},{128,64},{192,128},{1,193},{65,1},{129,65},{193,129... | collective-permute-start | bytes 552968 | tf_op jit(solution)/shard_map/ppermute | solution.py:374
  43.4 15.4 %collective-permute-start.2 = (bf16[864,128]{1,0:T(8,128)(2,1)S(1)}, bf16[864,128]{1,0:T(8,128)(2,1)S(1)}, u32[]{:S(2)}, u32[]{:S(2)}) collective-permute-start(bf16[864,128]{1,0:T(8,128)(2,1)S(1)} %get-tuple-element.23), channel_id=1, source_target_pairs={{0,64},{64,128},{128,192},{192,0},{1,65},{65,129},{129,193},{193,1... | collective-permute-start | bytes 663560 | tf_op jit(solution)/shard_map/ppermute | solution.py:375
  43.6 15.1 %collective-permute-start.3 = (bf16[864,128]{1,0:T(8,128)(2,1)S(1)}, bf16[864,128]{1,0:T(8,128)(2,1)S(1)}, u32[]{:S(2)}, u32[]{:S(2)}) collective-permute-start(bf16[864,128]{1,0:T(8,128)(2,1)S(1)} %get-tuple-element.24), channel_id=1, source_target_pairs={{0,192},{64,0},{128,64},{192,128},{1,193},{65,1},{129,65},{193,129... | collective-permute-start | bytes 663560 | tf_op jit(solution)/shard_map/ppermute | solution.py:376
  51.2 7.6 %collective-permute-start.4 = (bf16[720,128]{1,0:T(8,128)(2,1)S(1)}, bf16[720,128]{1,0:T(8,128)(2,1)S(1)}, u32[]{:S(2)}, u32[]{:S(2)}) collective-permute-start(bf16[720,128]{1,0:T(8,128)(2,1)S(1)} %collective-permute-done.after_ref.left_a_ref), channel_id=1, source_target_pairs={{0,64},{64,128},{128,192},{192,0},{1,65},{65,129},{129,193},{193,1... | collective-permute-start | bytes 552968 | tf_op jit(solution)/shard_map/ppermute | solution.py:386
  51.3 7.5 %collective-permute-start.5 = (bf16[720,128]{1,0:T(8,128)(2,1)S(1)}, bf16[720,128]{1,0:T(8,128)(2,1)S(1)}, u32[]{:S(2)}, u32[]{:S(2)}) collective-permute-start(bf16[720,128]{1,0:T(8,128)(2,1)S(1)} %collective-permute-done.1.also_after_ref.right_a_ref), channel_id=1, source_target_pairs={{0,192},{64,0},{128,64},{192,128},{1,193},{65,1},{129,65},{193,129... | collective-permute-start | bytes 552968 | tf_op jit(solution)/shard_map/ppermute | solution.py:387
  59.3 1.9 %collective-permute-start.6 = (bf16[576,384]{1,0:T(8,128)(2,1)S(1)}, bf16[576,384]{1,0:T(8,128)(2,1)S(1)}, u32[]{:S(2)}, u32[]{:S(2)}) collective-permute-start(bf16[576,384]{1,0:T(8,128)(2,1)S(1)} %shard_map.81.after_ref), channel_id=1, source_target_pairs={{0,1},{1,0},{2,3},{3,2},{4,5},{5,4},{6,7},{7,6},{8,9},{9,8},{10,11... | collective-permute-start | bytes 1327112 | tf_op jit(solution)/shard_map/ppermute | solution.py:407

commit v8 on v7

--- a/solution.py
+++ b/solution.py
@@ -36,24 +36,27 @@
     return lax.dot_general(a, b, dims, preferred_element_type=F32)
 
 
-def whole():
-    return pl.BlockSpec(memory_space=pltpu.VMEM)
-
-
-def call(kernel, out_shape, inputs, scratch=(), limit=32, flops=0, data=0, smem=(), far=()):
+def call(
+    kernel, out_shape, inputs, scratch=(), limit=32, flops=0, data=0, smem=(), far=(), far_out=()
+):
     spaces = {i: pltpu.SMEM for i in smem} | {i: pl.ANY for i in far}
-    specs = [
-        pl.BlockSpec(memory_space=spaces.get(i, pltpu.VMEM)) for i in range(len(inputs))
-    ]
-    return pl.pallas_call(
+    single = isinstance(out_shape, jax.ShapeDtypeStruct)
+    shapes = (out_shape,) if single else tuple(out_shape)
+    outs = pl.pallas_call(
         kernel,
-        out_shape=out_shape,
-        in_specs=specs,
-        out_specs=jax.tree.map(lambda _: whole(), out_shape),
+        out_shape=shapes,
+        in_specs=[
+            pl.BlockSpec(memory_space=spaces.get(i, pltpu.VMEM)) for i in range(len(inputs))
+        ],
+        out_specs=tuple(
+            pl.BlockSpec(memory_space=pl.ANY if i in far_out else pltpu.VMEM)
+            for i in range(len(shapes))
+        ),
         scratch_shapes=list(scratch),
         compiler_params=pltpu.CompilerParams(vmem_limit_bytes=limit * MIB),
         cost_estimate=pl.CostEstimate(flops=flops, bytes_accessed=data, transcendentals=0),
     )(*inputs)
+    return outs[0] if single else outs
 
 
 def pick(shape, target, along):
@@ -70,7 +73,7 @@
 
 def source_row(packed):
     inner = packed % 8
-    return packed // 8 * PATCHES + inner % PATCHES + jnp.where(inner >= PATCHES, ROWS, 0)
+    return packed // 8 * PATCHES + inner % PATCHES + jnp.where(inner >= PATCHES, ROWS // 2, 0)
 
 
 def patch_row(packed):
@@ -78,17 +81,32 @@
     return packed // 8 + inner % PATCHES * SLOTS + jnp.where(inner >= PATCHES, ROWS, 0)
 
 
-def pack_kernel(tokens_ref, d_out_ref, packed_ref, both_ref, sems):
+def pack_kernel(tokens_ref, d_out_ref, packed_ref, both_ref, out_ref, sems, out_sems):
+    part = ROWS // 2
     copies = [
-        pltpu.make_async_copy(ref, both_ref.at[pl.ds(i * ROWS, ROWS)], sems.at[i])
+        pltpu.make_async_copy(
+            ref.at[pl.ds(half * part, part)],
+            both_ref.at[pl.ds(half * ROWS + i * part, part)],
+            sems.at[half * 2 + i],
+        )
+        for half in range(2)
         for i, ref in enumerate((tokens_ref, d_out_ref))
     ]
     for copy in copies:
         copy.start()
-    chooser = pick((256, 256), source_row(row_index(256)), 1)
-    for copy in copies:
-        copy.wait()
-    packed_ref[...] = dot(chooser, both_ref[...]).astype(BF)
+    chooser = pick((ROWS, ROWS), source_row(row_index(ROWS)), 1)
+    outs = []
+    for half in range(2):
+        for copy in copies[half * 2 : half * 2 + 2]:
+            copy.wait()
+        rows = slice(half * ROWS, (half + 1) * ROWS)
+        out_ref[rows, :] = dot(chooser, both_ref[rows, :]).astype(BF)
+        span = pl.ds(half * ROWS, ROWS)
+        out = pltpu.make_async_copy(out_ref.at[span], packed_ref.at[span], out_sems.at[half])
+        out.start()
+        outs.append(out)
+    for out in outs:
+        out.wait()
 
 
 def row_stats(tokens):
@@ -236,13 +254,8 @@
 
 
 def token_grad_kernel(
-    tokens_ref, masked_ref, grad_ref, w_qkv_ref, after_ref, also_after_ref, packed_ref, place_ref
+    tokens_ref, masked_ref, grad_ref, w_qkv_ref, after_ref, also_after_ref, d_tokens_ref
 ):
-    term = lane_index(3 * 8 * OUT_ROWS)
-    kind, inner = term // (8 * OUT_ROWS), term % (8 * OUT_ROWS)
-    row = inner % OUT_ROWS
-    at = TOKEN_ROWS + kind * OUT_ROWS + jnp.where(kind == 2, row // 4, row)
-    place_ref[...] = pick((8 * CHUNK, 3 * 8 * OUT_ROWS), inner // OUT_ROWS * CHUNK + at, 0)
     masked = masked_ref[...]
     pieces = []
     for chunk in range(3):
@@ -252,42 +265,55 @@
     normalized, inverse = row_stats(tokens_ref[...])
     mean_grad = jnp.mean(normed_grad, axis=-1, keepdims=True)
     mean_cross = jnp.mean(normed_grad * normalized, axis=-1, keepdims=True)
-    d_tokens = (
+    d_tokens_ref[...] = (
         masked.astype(F32) + inverse * (normed_grad - mean_grad - normalized * mean_cross)
     ).astype(BF)
+
+
+def weight_terms(core, payloads):
+    own_ref, left_a_ref, right_a_ref, left_b_ref, right_b_ref, far_a_ref, far_b_ref = payloads
+    start = pl.multiple_of(core * HALF, HALF)
+    pairs = ((left_a_ref, left_b_ref), (right_b_ref, right_a_ref), (far_a_ref, far_b_ref))
+    attended = jnp.concatenate(
+        [own_ref[pl.ds(start, HALF), :]]
+        + [jnp.where(core == 0, first[:HALF, :], second[:HALF, :]) for first, second in pairs],
+        axis=1,
+    )
+    far = jnp.concatenate([far_a_ref[HALF:, :], far_b_ref[HALF:, :]], axis=0)
+    masked = jnp.concatenate(
+        [own_ref[D:, :], left_b_ref[HALF:, :], right_b_ref[HALF:, :], far], axis=1
+    )
+    masked = jnp.concatenate([masked[:256]] + [masked[256:]] * 4, axis=0)
+    return dot(attended, masked, NT)
+
+
+def send_kernel(core_ref, *refs):
+    refs[-1][...] = weight_terms(1 - core_ref[0], refs[:7]).astype(BF)
+
+
+def keep_kernel(core_ref, *refs):
+    d_tokens_ref, _, terms_ref, packed_ref, place_ref = refs[7:]
+    terms_ref[...] = weight_terms(core_ref[0], refs[:7])
+    term = lane_index(3 * 8 * OUT_ROWS)
+    kind, inner = term // (8 * OUT_ROWS), term % (8 * OUT_ROWS)
+    row = inner % OUT_ROWS
+    at = TOKEN_ROWS + kind * OUT_ROWS + jnp.where(kind == 2, row // 4, row)
+    place_ref[...] = pick((8 * CHUNK, 3 * 8 * OUT_ROWS), inner // OUT_ROWS * CHUNK + at, 0)
     piece = lane_index(576)
     target = piece % 16 * CHUNK + piece // 64 * PATCHES + piece % 64 // 16
     chooser = pick((16 * CHUNK, 576), target, 0)
     for half in range(2):
         stacked = jnp.concatenate(
             [
-                d_tokens[p * SLOTS + half * 16 : p * SLOTS + half * 16 + 16, c * 128 : (c + 1) * 128]
+                d_tokens_ref[
+                    p * SLOTS + half * 16 : p * SLOTS + half * 16 + 16, c * 128 : (c + 1) * 128
+                ]
                 for c in range(9)
                 for p in range(PATCHES)
             ],
             axis=0,
         )
         packed_ref[half * 16 * CHUNK : (half + 1) * 16 * CHUNK, :] = dot(chooser, stacked).astype(BF)
-
-
-def weight_kernel(
-    other, core_ref, own_ref, left_a_ref, left_b_ref, right_a_ref, right_b_ref, far_a_ref, far_b_ref,
-    after_ref, terms_ref,
-):
-    core = 1 - core_ref[0] if other else core_ref[0]
-    start = pl.multiple_of(core * HALF, HALF)
-    pairs = ((left_a_ref, left_b_ref), (right_b_ref, right_a_ref), (far_a_ref, far_b_ref))
-    attended = jnp.concatenate(
-        [own_ref[pl.ds(start, HALF), :]]
-        + [jnp.where(core == 0, first[:HALF, :], second[:HALF, :]) for first, second in pairs],
-        axis=1,
-    )
-    far = jnp.concatenate([far_a_ref[HALF:, :], far_b_ref[HALF:, :]], axis=0)
-    masked = jnp.concatenate(
-        [own_ref[D:, :], left_b_ref[HALF:, :], right_b_ref[HALF:, :], far], axis=1
-    )
-    masked = jnp.concatenate([masked[:256]] + [masked[256:]] * 4, axis=0)
-    terms_ref[...] = dot(attended, masked, NT).astype(terms_ref.dtype)
 
 
 def merge_kernel(rows_ref, keep_ref, got_ref, place_ref, merged_ref):
@@ -304,17 +330,22 @@
         ).astype(BF)
 
 
-def unpack_kernel(merged_ref, d_tokens_ref, d_w_ref, total_ref):
+def unpack_kernel(merged_ref, d_tokens_ref, d_w_ref, rows_ref, total_ref, sems):
     piece = row_index(288)
     row = piece % 32
     source = row // PATCHES * CHUNK + piece // 32 * PATCHES + row % PATCHES
     chooser = pick((288, 8 * CHUNK), source, 1)
+    copies = []
     for group in range(4):
         rows = dot(chooser, merged_ref[group * 8 * CHUNK : (group + 1) * 8 * CHUNK, :]).astype(BF)
         for block in range(9):
-            d_tokens_ref[group * 32 : (group + 1) * 32, block * 128 : (block + 1) * 128] = rows[
+            rows_ref[group * 32 : (group + 1) * 32, block * 128 : (block + 1) * 128] = rows[
                 block * 32 : (block + 1) * 32
             ]
+        span = pl.ds(group * 32, 32)
+        copy = pltpu.make_async_copy(rows_ref.at[span], d_tokens_ref.at[span], sems.at[group])
+        copy.start()
+        copies.append(copy)
     merged = merged_ref[...].astype(F32).reshape(SLOTS, CHUNK, 128)
     total_ref[...] = jnp.sum(merged[:, 32:], axis=0)
     first = TOKEN_ROWS - 32
@@ -324,6 +355,8 @@
         at = first + 2 * OUT_ROWS + row // 4
         lanes = slice(row % 4 * 32, row % 4 * 32 + 32)
         d_w_ref[row : row + 1, 256:] = total_ref[at : at + 1, lanes]
+    for copy in copies:
+        copy.wait()
 
 
 def body(tokens, d_out, frames, frame_order, w_qkv, w_out):
@@ -335,9 +368,15 @@
         pack_kernel,
         shape((256, D), BF),
         (tokens[0], d_out[0]),
-        scratch=(pltpu.VMEM((256, D), BF), pltpu.SemaphoreType.DMA((2,))),
+        scratch=(
+            pltpu.VMEM((256, D), BF),
+            pltpu.VMEM((256, D), BF),
+            pltpu.SemaphoreType.DMA((4,)),
+            pltpu.SemaphoreType.DMA((2,)),
+        ),
         limit=60,
         far=(0, 1),
+        far_out=(0,),
     )
     arrived = lax.all_to_all(
         packed.reshape(SLOTS, 8, D), ("y", "z"), split_axis=0, concat_axis=0, tiled=True
@@ -385,32 +424,36 @@
     )
     far_a = lax.ppermute(left_a, "dp", up)
     far_b = lax.ppermute(right_a, "dp", down)
-    rows, places = call(
+    d_rows = call(
         token_grad_kernel,
-        (shape((SLOTS * CHUNK, 128), BF), shape((8 * CHUNK, 3 * 8 * OUT_ROWS), BF)),
+        shape((ROWS, D), BF),
         (kept, masked, grads, w_qkv, left_a, right_a),
         far=(4, 5),
         limit=24,
         flops=int(3e9),
         data=int(16e6),
     )
-    payloads = (own, left_a, left_b, right_a, right_b, far_a, far_b)
+    payloads = (core.reshape(1), own, left_a, right_a, left_b, right_b, far_a, far_b)
     send = call(
-        functools.partial(weight_kernel, True),
+        send_kernel,
         shape((SLOTS * OUT_ROWS, WIDE), BF),
-        (core.reshape(1),) + payloads + (rows,),
+        payloads + (d_rows,),
         smem=(0,),
         far=(8,),
         flops=int(1e9),
         data=int(4e6),
     )
     got = lax.ppermute(send, "core", [(0, 1), (1, 0)])
-    keep = call(
-        functools.partial(weight_kernel, False),
-        shape((SLOTS * OUT_ROWS, WIDE), F32),
-        (core.reshape(1),) + payloads + (send,),
+    keep, rows, places = call(
+        keep_kernel,
+        (
+            shape((SLOTS * OUT_ROWS, WIDE), F32),
+            shape((SLOTS * CHUNK, 128), BF),
+            shape((8 * CHUNK, 3 * 8 * OUT_ROWS), BF),
+        ),
+        payloads + (d_rows, send),
         smem=(0,),
-        far=(8,),
+        far=(9,),
         flops=int(1e9),
         data=int(4e6),
     )
@@ -424,8 +467,13 @@
         unpack_kernel,
         (shape((ROWS, D), BF), shape((OUT_ROWS, COLS), F32)),
         (returned,),
-        scratch=(pltpu.VMEM((CHUNK - 32, 128), F32),),
+        scratch=(
+            pltpu.VMEM((ROWS, D), BF),
+            pltpu.VMEM((CHUNK - 32, 128), F32),
+            pltpu.SemaphoreType.DMA((4,)),
+        ),
         limit=16,
+        far_out=(0,),
     )
     return d_tokens[None], d_w
 

time: 88.9 us -> 89.3 us (level)
    ppermute x1, waiting for transfers between devices: 1.28 us -> 0.32 us  [body(): got = lax.ppermute(send, 'core', [(0, 1), (1, 0)])]
    ppermute x1, waiting for transfers between devices: 0.01 us -> 0.9 us  [body(): far_a = lax.ppermute(left_a, 'dp', up)]
  transfers between devices with their start and end apart: 8 -> 8, of which waited for: 2 -> 3; matrix products, arithmetic and copies ran while one was open for 3% -> 3% of each run, Pallas kernels for 10% -> 10%
where the time goes in v8:
time: 89.3 us; the launch traced here: 88.6 us
  blocking collectives  25.3 us (28%)
  starting transfers between devices  21.3 us (24%)
  Pallas kernels  20.8 us (23%)
  waiting for transfers between devices  16.9 us (19%)
  local copies, waits for them, and re-layouts  2.09 us (2%)
  between operations  1.56 us (2%)
    all_to_all x1, blocking collectives, body(): lax.all_to_all(merged.reshape(SLOTS, CHUNK, 128), ('y', 'z'), split_axis=...  25.3 us
    pallas_call x8, Pallas kernels, call(): pl.pallas_call(kernel, out_shape=shapes, in_specs=[pl.BlockSpec(memory_sp...  20.8 us
    all_to_all x1, waiting for transfers between devices, body(): lax.all_to_all(packed.reshape(SLOTS, 8, D), ('y', 'z'), split_axis=0, con...  15.6 us
    all_to_all x1, starting transfers between devices, body(): lax.all_to_all(packed.reshape(SLOTS, 8, D), ('y', 'z'), split_axis=0, con...  11.4 us
    ppermute x1, starting transfers between devices, body(): far_b = lax.ppermute(right_a, 'dp', down)  3.22 us
    ppermute x1, starting transfers between devices, body(): right_b = lax.ppermute(left, 'dp', down)  2.97 us
    slice x1, local copies, waits for them, and re-layouts, body(): firsts = tuple((w_qkv[:, kind * D:kind * D + WIDE] for kind in range(3)))  1.98 us
  transfers between devices with their start and end apart: 8, of which 3 were waited for; matrix products, arithmetic and copies ran while one was open for 3% of the time, Pallas kernels for 10%

profile of v8, /device:TPU:32, one launch (start us, length us, event | category | flops | bytes accessed | tf_op | source)
XLA Modules:
  0.0 88.6 jit_solution(13037042656441269139)
XLA Ops:
  0.6 2.2 %shard_map.77 = bf16[256,1152]{1,0:T(8,128)(2,1)} custom-call(bf16[128,1152]{1,0:T(8,128)(2,1)} %bitcast.19, bf16[128,1152]{1,0:T(8,128)(2,1)} %bitcast.20), custom_call_target="tpu_custom_call" | custom-call | tf_op jit(solution)/shard_map/pallas_call | solution.py:45
  2.8 11.4 %all-to-all-start = ((bf16[32,8,1152]{2,1,0:T(8,128)(2,1)}), bf16[32,8,1152]{2,1,0:T(8,128)(2,1)S(1)}, u32[]{:S(2)}, u32[]{:S(2)}) async-start(bf16[32,8,1152]{2,1,0:T(8,128)(2,1)} %bitcast.18), calls=%async_computation | async-start | bytes 1179648 | tf_op jit(solution)/shard_map/all_to_all | solution.py:381
  14.9 0.7 fusion
  15.5 0.1 copy.8.live_ref
  15.6 2.0 %fusion.1 = (bf16[1152,384]{1,0:T(8,128)(2,1)S(1)}, bf16[1152,384]{1,0:T(8,128)(2,1)S(1)}, bf16[1152,384]{1,0:T(8,128)(2,1)S(1)}) fusion(bf16[1152,3456]{1,0:T(8,128)(2,1)} %w_qkv_ref.3), kind=kLoop, calls=%fused_computation.2 | loop fusion | bytes 5308416 | tf_op jit(solution)/shard_map/slice | solution.py:384
  17.6 15.6 %all-to-all-done = bf16[32,8,1152]{2,1,0:T(8,128)(2,1)S(1)} async-done(((bf16[32,8,1152]{2,1,0:T(8,128)(2,1)}), bf16[32,8,1152]{2,1,0:T(8,128)(2,1)S(1)}, u32[]{:S(2)}, u32[]{:S(2)}) %all-to-all-start) | async-done | bytes 589856 | tf_op jit(solution)/shard_map/all_to_all | solution.py:381
  33.2 0.0 copy-start
  33.2 0.0 slice-start
  33.2 0.0 slice-start.1
  33.3 6.8 %shard_map.78 = (bf16[128,1152]{1,0:T(8,128)(2,1)S(1)}, bf16[128,1152]{1,0:T(8,128)(2,1)S(1)}, bf16[128,3456]{1,0:T(8,128)(2,1)S(1)}, f32[16,32,128]{2,1,0:T(8,1...) custom-call(s32[1]{0:T(128)} %bitcast.1.place_ref, ...), custom_call_target="tpu_custom_call" | custom-call | flops 2000000000 | bytes 14000000 | tf_op jit(solution)/shard_map/pallas_call | solution.py:45
  40.0 1.6 %collective-permute-start = (bf16[720,128]{1,0:T(8,128)(2,1)S(1)}, bf16[720,128]{1,0:T(8,128)(2,1)S(1)}, u32[]{:S(2)}, u32[]{:S(2)}) collective-permute-start(bf16[720,128]{1,0:T(8,128)(2,1)S(1)} %get-tuple-element.17), channel_id=1, source_target_pairs={{0,64},{64,128},{128,192},{192,0},{1,65},{65,129},{129,193},{193,1... | collective-permute-start | bytes 552968 | tf_op jit(solution)/shard_map/ppermute | solution.py:412
  41.6 1.8 %collective-permute-start.1 = (bf16[720,128]{1,0:T(8,128)(2,1)S(1)}, bf16[720,128]{1,0:T(8,128)(2,1)S(1)}, u32[]{:S(2)}, u32[]{:S(2)}) collective-permute-start(bf16[720,128]{1,0:T(8,128)(2,1)S(1)} %get-tuple-element.18), channel_id=1, source_target_pairs={{0,192},{64,0},{128,64},{192,128},{1,193},{65,1},{129,65},{193,129... | collective-permute-start | bytes 552968 | tf_op jit(solution)/shard_map/ppermute | solution.py:413
  43.3 0.3 collective-permute-start.2
  43.6 3.0 %collective-permute-start.3 = (bf16[864,128]{1,0:T(8,128)(2,1)S(1)}, bf16[864,128]{1,0:T(8,128)(2,1)S(1)}, u32[]{:S(2)}, u32[]{:S(2)}) collective-permute-start(bf16[864,128]{1,0:T(8,128)(2,1)S(1)} %get-tuple-element.20), channel_id=1, source_target_pairs={{0,192},{64,0},{128,64},{192,128},{1,193},{65,1},{129,65},{193,129... | collective-permute-start | bytes 663560 | tf_op jit(solution)/shard_map/ppermute | solution.py:415
  46.6 0.0 copy-done
  46.6 4.6 %shard_map.79.grad_ref = bf16[128,3456]{1,0:T(8,128)(2,1)S(1)} custom-call(bf16[128,1152]{1,0:T(8,128)(2,1)S(1)} %get-tuple-element.22.masked_ref, bf16[128,3456]{1,0:T(8,128)(2,1)S(1)} %get-tuple-element.23.joined_ref, f32[16,32,128]{2,1,0:T(8,128)S(1)} %get-tuple-element.24.probs_ref, bf16[1152,1152]{1,0:T(8,128)(2,1)S(1)} %copy-done), custom_call_target="tpu_custom_call" | custom-call | flops 3000000000 | bytes 16000000 | tf_op jit(solution)/shard_map/pallas_call | solution.py:45
  51.2 0.0 collective-permute-done.after_ref.refs_1_
  51.2 0.1 collective-permute-start.4
  51.3 0.0 collective-permute-done.1.also_after_ref.refs_2_
  51.3 3.2 %collective-permute-start.5 = (bf16[720,128]{1,0:T(8,128)(2,1)S(1)}, bf16[720,128]{1,0:T(8,128)(2,1)S(1)}, u32[]{:S(2)}, u32[]{:S(2)}) collective-permute-start(bf16[720,128]{1,0:T(8,128)(2,1)S(1)} %collective-permute-done.1.also_after_ref.refs_2_), channel_id=1, source_target_pairs={{0,192},{64,0},{128,64},{192,128},{1,193},{65,1},{129,65},{193,129... | collective-permute-start | bytes 552968 | tf_op jit(solution)/shard_map/ppermute | solution.py:426
  54.5 0.0 slice-done
  54.5 0.0 slice-done.1
  54.5 2.6 %shard_map.80.refs_7_ = bf16[128,1152]{1,0:T(8,128)(2,1)S(1)} custom-call(bf16[128,1152]{1,0:T(8,128)(2,1)S(1)} %get-tuple-element.21.tokens_ref, bf16[128,1152]{1,0:T(8,128)(2,1)S(1)} %get-tuple-element.22.masked_ref, bf16[128,3456]{1,0:T(8,128)(2,1)S(1)} %shard_map.79.grad_ref, bf16[1152,3456]{1,0:T(8,128)(2,1)S(1)} %bitcast.14, ...), custom_call_target="tpu_custom_call" | custom-call | flops 3000000000 | bytes 16000000 | tf_op jit(solution)/shard_map/pallas_call | solution.py:45
  57.1 0.0 collective-permute-done.2.refs_3_
  57.1 0.0 collective-permute-done.3.refs_4_
  57.1 0.9 %collective-permute-done.4.refs_5_ = bf16[720,128]{1,0:T(8,128)(2,1)S(1)} collective-permute-done((bf16[720,128]{1,0:T(8,128)(2,1)S(1)}, bf16[720,128]{1,0:T(8,128)(2,1)S(1)}, u32[]{:S(2)}, u32[]{:S(2)}) %collective-permute-start.4) | collective-permute-done | bytes 184352 | tf_op jit(solution)/shard_map/ppermute | solution.py:425
  58.0 0.0 collective-permute-done.5.refs_6_
  58.0 0.5 shard_map.81.refs_8_
  58.5 0.1 collective-permute-start.6
  58.6 1.5 %shard_map.82 = (f32[576,384]{1,0:T(8,128)S(1)}, bf16[2560,128]{1,0:T(8,128)(2,1)S(1)}, bf16[640,432]{1,0:T(8,128)(2,1)S(1)}) custom-call(s32[1]{0:T(128)} %bitcast.core_ref, bf16[1440,128]{1,0:T(8,128)(2,1)S(1)} %get-tuple-element.16.refs_0_, bf16[720,128]{1,0:T(8,128)(2,1)S(1)} %collective-permute-done.after_ref.refs_1_, ...), custom_call_target="tpu_custom_call" | custom-call | flops 1000000000 | bytes 4000000 | tf_op jit(solution)/shard_map/pallas_call | solution.py:45
  60.1 0.3 collective-permute-done.6.got_ref
  60.4 0.9 shard_map.83
  61.2 25.3 %all_to_all.10 = bf16[32,80,128]{2,1,0:T(8,128)(2,1)S(1)} all-to-all(bf16[32,80,128]{2,1,0:T(8,128)(2,1)S(1)} %bitcast.16), channel_id=1, replica_groups=mesh['dp'=4,'y'=4,'z'=8,'core'=2] {'y','z'}, dimensions={0} | all-to-all | bytes 1310720 | tf_op jit(solution)/shard_map/all_to_all | solution.py:463
  86.6 1.8 %shard_map.84 = (bf16[128,1152]{1,0:T(8,128)(2,1)}, f32[18,288]{1,0:T(8,128)}) custom-call(bf16[2560,128]{1,0:T(8,128)(2,1)S(1)} %bitcast.15), custom_call_target="tpu_custom_call" | custom-call | tf_op jit(solution)/shard_map/pallas_call | solution.py:45
  (1 shorter events, 0.0 us)
Async XLA Ops:
  2.8 30.4 %all-to-all-start = ((bf16[32,8,1152]{2,1,0:T(8,128)(2,1)}), bf16[32,8,1152]{2,1,0:T(8,128)(2,1)S(1)}, u32[]{:S(2)}, u32[]{:S(2)}) async-start(bf16[32,8,1152]{2,1,0:T(8,128)(2,1)} %bitcast.18), calls=%async_computation | async-start | bytes 1179648 | tf_op jit(solution)/shard_map/all_to_all | solution.py:381
  33.2 13.3 %copy-start = (bf16[1152,1152]{1,0:T(8,128)(2,1)S(1)}, bf16[1152,1152]{1,0:T(8,128)(2,1)}, u32[]{:S(2)}) copy-start(bf16[1152,1152]{1,0:T(8,128)(2,1)} %w_out_ref.1) | copy-start | bytes 7962628
  33.2 21.2 %slice-start = ((s8[7962624]{0:T(1024)(128)(4,1)}), s8[4194304]{0:T(1024)(128)(4,1)S(1)}, s32[]{:S(2)}) async-start(s8[7962624]{0:T(1024)(128)(4,1)} %bitcast.13), calls=%async_computation.2 | async-start | bytes 8388608
  33.2 21.2 %slice-start.1 = ((s8[7962624]{0:T(1024)(128)(4,1)}), s8[3768320]{0:T(1024)(128)(4,1)S(1)}, s32[]{:S(2)}) async-start(s8[7962624]{0:T(1024)(128)(4,1)} %bitcast.13), calls=%async_computation.3 | async-start | bytes 7536640
  40.0 11.1 %collective-permute-start = (bf16[720,128]{1,0:T(8,128)(2,1)S(1)}, bf16[720,128]{1,0:T(8,128)(2,1)S(1)}, u32[]{:S(2)}, u32[]{:S(2)}) collective-permute-start(bf16[720,128]{1,0:T(8,128)(2,1)S(1)} %get-tuple-element.17), channel_id=1, source_target_pairs={{0,64},{64,128},{128,192},{192,0},{1,65},{65,129},{129,193},{193,1... | collective-permute-start | bytes 552968 | tf_op jit(solution)/shard_map/ppermute | solution.py:412
  41.6 9.7 %collective-permute-start.1 = (bf16[720,128]{1,0:T(8,128)(2,1)S(1)}, bf16[720,128]{1,0:T(8,128)(2,1)S(1)}, u32[]{:S(2)}, u32[]{:S(2)}) collective-permute-start(bf16[720,128]{1,0:T(8,128)(2,1)S(1)} %get-tuple-element.18), channel_id=1, source_target_pairs={{0,192},{64,0},{128,64},{192,128},{1,193},{65,1},{129,65},{193,129... | collective-permute-start | bytes 552968 | tf_op jit(solution)/shard_map/ppermute | solution.py:413
  43.3 13.7 %collective-permute-start.2 = (bf16[864,128]{1,0:T(8,128)(2,1)S(1)}, bf16[864,128]{1,0:T(8,128)(2,1)S(1)}, u32[]{:S(2)}, u32[]{:S(2)}) collective-permute-start(bf16[864,128]{1,0:T(8,128)(2,1)S(1)} %get-tuple-element.19), channel_id=1, source_target_pairs={{0,64},{64,128},{128,192},{192,0},{1,65},{65,129},{129,193},{193,1... | collective-permute-start | bytes 663560 | tf_op jit(solution)/shard_map/ppermute | solution.py:414
  43.6 13.5 %collective-permute-start.3 = (bf16[864,128]{1,0:T(8,128)(2,1)S(1)}, bf16[864,128]{1,0:T(8,128)(2,1)S(1)}, u32[]{:S(2)}, u32[]{:S(2)}) collective-permute-start(bf16[864,128]{1,0:T(8,128)(2,1)S(1)} %get-tuple-element.20), channel_id=1, source_target_pairs={{0,192},{64,0},{128,64},{192,128},{1,193},{65,1},{129,65},{193,129... | collective-permute-start | bytes 663560 | tf_op jit(solution)/shard_map/ppermute | solution.py:415
  51.2 6.8 %collective-permute-start.4 = (bf16[720,128]{1,0:T(8,128)(2,1)S(1)}, bf16[720,128]{1,0:T(8,128)(2,1)S(1)}, u32[]{:S(2)}, u32[]{:S(2)}) collective-permute-start(bf16[720,128]{1,0:T(8,128)(2,1)S(1)} %collective-permute-done.after_ref.refs_1_), channel_id=1, source_target_pairs={{0,64},{64,128},{128,192},{192,0},{1,65},{65,129},{129,193},{193,1... | collective-permute-start | bytes 552968 | tf_op jit(solution)/shard_map/ppermute | solution.py:425
  51.3 6.7 %collective-permute-start.5 = (bf16[720,128]{1,0:T(8,128)(2,1)S(1)}, bf16[720,128]{1,0:T(8,128)(2,1)S(1)}, u32[]{:S(2)}, u32[]{:S(2)}) collective-permute-start(bf16[720,128]{1,0:T(8,128)(2,1)S(1)} %collective-permute-done.1.also_after_ref.refs_2_), channel_id=1, source_target_pairs={{0,192},{64,0},{128,64},{192,128},{1,193},{65,1},{129,65},{193,129... | collective-permute-start | bytes 552968 | tf_op jit(solution)/shard_map/ppermute | solution.py:426
  58.5 1.9 %collective-permute-start.6 = (bf16[576,384]{1,0:T(8,128)(2,1)S(1)}, bf16[576,384]{1,0:T(8,128)(2,1)S(1)}, u32[]{:S(2)}, u32[]{:S(2)}) collective-permute-start(bf16[576,384]{1,0:T(8,128)(2,1)S(1)} %shard_map.81.refs_8_), channel_id=1, source_target_pairs={{0,1},{1,0},{2,3},{3,2},{4,5},{5,4},{6,7},{7,6},{8,9},{9,8},{10,11... | collective-permute-start | bytes 1327112 | tf_op jit(solution)/shard_map/ppermute | solution.py:446

commit v9 on v8

--- a/solution.py
+++ b/solution.py
@@ -330,22 +330,17 @@
         ).astype(BF)
 
 
-def unpack_kernel(merged_ref, d_tokens_ref, d_w_ref, rows_ref, total_ref, sems):
+def unpack_kernel(merged_ref, d_tokens_ref, d_w_ref, total_ref):
     piece = row_index(288)
     row = piece % 32
     source = row // PATCHES * CHUNK + piece // 32 * PATCHES + row % PATCHES
     chooser = pick((288, 8 * CHUNK), source, 1)
-    copies = []
     for group in range(4):
         rows = dot(chooser, merged_ref[group * 8 * CHUNK : (group + 1) * 8 * CHUNK, :]).astype(BF)
         for block in range(9):
-            rows_ref[group * 32 : (group + 1) * 32, block * 128 : (block + 1) * 128] = rows[
+            d_tokens_ref[group * 32 : (group + 1) * 32, block * 128 : (block + 1) * 128] = rows[
                 block * 32 : (block + 1) * 32
             ]
-        span = pl.ds(group * 32, 32)
-        copy = pltpu.make_async_copy(rows_ref.at[span], d_tokens_ref.at[span], sems.at[group])
-        copy.start()
-        copies.append(copy)
     merged = merged_ref[...].astype(F32).reshape(SLOTS, CHUNK, 128)
     total_ref[...] = jnp.sum(merged[:, 32:], axis=0)
     first = TOKEN_ROWS - 32
@@ -355,8 +350,6 @@
         at = first + 2 * OUT_ROWS + row // 4
         lanes = slice(row % 4 * 32, row % 4 * 32 + 32)
         d_w_ref[row : row + 1, 256:] = total_ref[at : at + 1, lanes]
-    for copy in copies:
-        copy.wait()
 
 
 def body(tokens, d_out, frames, frame_order, w_qkv, w_out):
@@ -467,13 +460,8 @@
         unpack_kernel,
         (shape((ROWS, D), BF), shape((OUT_ROWS, COLS), F32)),
         (returned,),
-        scratch=(
-            pltpu.VMEM((ROWS, D), BF),
-            pltpu.VMEM((CHUNK - 32, 128), F32),
-            pltpu.SemaphoreType.DMA((4,)),
-        ),
+        scratch=(pltpu.VMEM((CHUNK - 32, 128), F32),),
         limit=16,
-        far_out=(0,),
     )
     return d_tokens[None], d_w
 

time: 89.3 us -> 88.6 us (level)
  no operation moved by 1% of the time
where the time goes in v9:
time: 88.6 us; the launch traced here: 87.8 us
  blocking collectives  25.3 us (29%)
  starting transfers between devices  21.3 us (24%)
  Pallas kernels  20.2 us (23%)
  waiting for transfers between devices  16.9 us (19%)
  local copies, waits for them, and re-layouts  2.09 us (2%)
  between operations  1.4 us (2%)
    all_to_all x1, blocking collectives, body(): lax.all_to_all(merged.reshape(SLOTS, CHUNK, 128), ('y', 'z'), split_axis=...  25.3 us
    pallas_call x8, Pallas kernels, call(): pl.pallas_call(kernel, out_shape=shapes, in_specs=[pl.BlockSpec(memory_sp...  20.2 us
    all_to_all x1, waiting for transfers between devices, body(): lax.all_to_all(packed.reshape(SLOTS, 8, D), ('y', 'z'), split_axis=0, con...  15.6 us
    all_to_all x1, starting transfers between devices, body(): lax.all_to_all(packed.reshape(SLOTS, 8, D), ('y', 'z'), split_axis=0, con...  11.4 us
    ppermute x1, starting transfers between devices, body(): far_b = lax.ppermute(right_a, 'dp', down)  3.22 us
    ppermute x1, starting transfers between devices, body(): right_b = lax.ppermute(left, 'dp', down)  2.97 us
    slice x1, local copies, waits for them, and re-layouts, body(): firsts = tuple((w_qkv[:, kind * D:kind * D + WIDE] for kind in range(3)))  1.98 us
  transfers between devices with their start and end apart: 8, of which 3 were waited for; matrix products, arithmetic and copies ran while one was open for 3% of the time, Pallas kernels for 10%

profile of v9, /device:TPU:32, one launch (start us, length us, event | category | flops | bytes accessed | tf_op | source)
XLA Modules:
  0.0 87.8 jit_solution(8484125652739088498)
XLA Ops:
  0.6 2.2 %shard_map.77 = bf16[256,1152]{1,0:T(8,128)(2,1)} custom-call(bf16[128,1152]{1,0:T(8,128)(2,1)} %bitcast.19, bf16[128,1152]{1,0:T(8,128)(2,1)} %bitcast.20), custom_call_target="tpu_custom_call" | custom-call | tf_op jit(solution)/shard_map/pallas_call | solution.py:45
  2.8 11.4 %all-to-all-start = ((bf16[32,8,1152]{2,1,0:T(8,128)(2,1)}), bf16[32,8,1152]{2,1,0:T(8,128)(2,1)S(1)}, u32[]{:S(2)}, u32[]{:S(2)}) async-start(bf16[32,8,1152]{2,1,0:T(8,128)(2,1)} %bitcast.18), calls=%async_computation | async-start | bytes 1179648 | tf_op jit(solution)/shard_map/all_to_all | solution.py:374
  14.9 0.7 fusion
  15.5 0.1 copy.8.live_ref
  15.6 2.0 %fusion.1 = (bf16[1152,384]{1,0:T(8,128)(2,1)S(1)}, bf16[1152,384]{1,0:T(8,128)(2,1)S(1)}, bf16[1152,384]{1,0:T(8,128)(2,1)S(1)}) fusion(bf16[1152,3456]{1,0:T(8,128)(2,1)} %w_qkv_ref.3), kind=kLoop, calls=%fused_computation.2 | loop fusion | bytes 5308416 | tf_op jit(solution)/shard_map/slice | solution.py:377
  17.6 15.6 %all-to-all-done = bf16[32,8,1152]{2,1,0:T(8,128)(2,1)S(1)} async-done(((bf16[32,8,1152]{2,1,0:T(8,128)(2,1)}), bf16[32,8,1152]{2,1,0:T(8,128)(2,1)S(1)}, u32[]{:S(2)}, u32[]{:S(2)}) %all-to-all-start) | async-done | bytes 589856 | tf_op jit(solution)/shard_map/all_to_all | solution.py:374
  33.2 0.0 copy-start
  33.2 0.0 slice-start
  33.2 0.0 slice-start.1
  33.3 6.8 %shard_map.78 = (bf16[128,1152]{1,0:T(8,128)(2,1)S(1)}, bf16[128,1152]{1,0:T(8,128)(2,1)S(1)}, bf16[128,3456]{1,0:T(8,128)(2,1)S(1)}, f32[16,32,128]{2,1,0:T(8,1...) custom-call(s32[1]{0:T(128)} %bitcast.1.place_ref, ...), custom_call_target="tpu_custom_call" | custom-call | flops 2000000000 | bytes 14000000 | tf_op jit(solution)/shard_map/pallas_call | solution.py:45
  40.0 1.6 %collective-permute-start = (bf16[720,128]{1,0:T(8,128)(2,1)S(1)}, bf16[720,128]{1,0:T(8,128)(2,1)S(1)}, u32[]{:S(2)}, u32[]{:S(2)}) collective-permute-start(bf16[720,128]{1,0:T(8,128)(2,1)S(1)} %get-tuple-element.17), channel_id=1, source_target_pairs={{0,64},{64,128},{128,192},{192,0},{1,65},{65,129},{129,193},{193,1... | collective-permute-start | bytes 552968 | tf_op jit(solution)/shard_map/ppermute | solution.py:405
  41.6 1.8 %collective-permute-start.1 = (bf16[720,128]{1,0:T(8,128)(2,1)S(1)}, bf16[720,128]{1,0:T(8,128)(2,1)S(1)}, u32[]{:S(2)}, u32[]{:S(2)}) collective-permute-start(bf16[720,128]{1,0:T(8,128)(2,1)S(1)} %get-tuple-element.18), channel_id=1, source_target_pairs={{0,192},{64,0},{128,64},{192,128},{1,193},{65,1},{129,65},{193,129... | collective-permute-start | bytes 552968 | tf_op jit(solution)/shard_map/ppermute | solution.py:406
  43.3 0.3 collective-permute-start.2
  43.6 3.0 %collective-permute-start.3 = (bf16[864,128]{1,0:T(8,128)(2,1)S(1)}, bf16[864,128]{1,0:T(8,128)(2,1)S(1)}, u32[]{:S(2)}, u32[]{:S(2)}) collective-permute-start(bf16[864,128]{1,0:T(8,128)(2,1)S(1)} %get-tuple-element.20), channel_id=1, source_target_pairs={{0,192},{64,0},{128,64},{192,128},{1,193},{65,1},{129,65},{193,129... | collective-permute-start | bytes 663560 | tf_op jit(solution)/shard_map/ppermute | solution.py:408
  46.6 0.0 copy-done
  46.6 4.6 %shard_map.79.grad_ref = bf16[128,3456]{1,0:T(8,128)(2,1)S(1)} custom-call(bf16[128,1152]{1,0:T(8,128)(2,1)S(1)} %get-tuple-element.22.masked_ref, bf16[128,3456]{1,0:T(8,128)(2,1)S(1)} %get-tuple-element.23.joined_ref, f32[16,32,128]{2,1,0:T(8,128)S(1)} %get-tuple-element.24.probs_ref, bf16[1152,1152]{1,0:T(8,128)(2,1)S(1)} %copy-done), custom_call_target="tpu_custom_call" | custom-call | flops 3000000000 | bytes 16000000 | tf_op jit(solution)/shard_map/pallas_call | solution.py:45
  51.2 0.0 collective-permute-done.after_ref.refs_1_
  51.2 0.1 collective-permute-start.4
  51.3 0.0 collective-permute-done.1.also_after_ref.refs_2_
  51.3 3.2 %collective-permute-start.5 = (bf16[720,128]{1,0:T(8,128)(2,1)S(1)}, bf16[720,128]{1,0:T(8,128)(2,1)S(1)}, u32[]{:S(2)}, u32[]{:S(2)}) collective-permute-start(bf16[720,128]{1,0:T(8,128)(2,1)S(1)} %collective-permute-done.1.also_after_ref.refs_2_), channel_id=1, source_target_pairs={{0,192},{64,0},{128,64},{192,128},{1,193},{65,1},{129,65},{193,129... | collective-permute-start | bytes 552968 | tf_op jit(solution)/shard_map/ppermute | solution.py:419
  54.5 0.0 slice-done
  54.5 0.0 slice-done.1
  54.5 2.6 %shard_map.80.refs_7_ = bf16[128,1152]{1,0:T(8,128)(2,1)S(1)} custom-call(bf16[128,1152]{1,0:T(8,128)(2,1)S(1)} %get-tuple-element.21.tokens_ref, bf16[128,1152]{1,0:T(8,128)(2,1)S(1)} %get-tuple-element.22.masked_ref, bf16[128,3456]{1,0:T(8,128)(2,1)S(1)} %shard_map.79.grad_ref, bf16[1152,3456]{1,0:T(8,128)(2,1)S(1)} %bitcast.14, ...), custom_call_target="tpu_custom_call" | custom-call | flops 3000000000 | bytes 16000000 | tf_op jit(solution)/shard_map/pallas_call | solution.py:45
  57.1 0.0 collective-permute-done.2.refs_3_
  57.1 0.0 collective-permute-done.3.refs_4_
  57.1 0.9 %collective-permute-done.4.refs_5_ = bf16[720,128]{1,0:T(8,128)(2,1)S(1)} collective-permute-done((bf16[720,128]{1,0:T(8,128)(2,1)S(1)}, bf16[720,128]{1,0:T(8,128)(2,1)S(1)}, u32[]{:S(2)}, u32[]{:S(2)}) %collective-permute-start.4) | collective-permute-done | bytes 184352 | tf_op jit(solution)/shard_map/ppermute | solution.py:418
  58.0 0.0 collective-permute-done.5.refs_6_
  58.0 0.5 shard_map.81.refs_8_
  58.5 0.1 collective-permute-start.6
  58.6 1.5 %shard_map.82 = (f32[576,384]{1,0:T(8,128)S(1)}, bf16[2560,128]{1,0:T(8,128)(2,1)S(1)}, bf16[640,432]{1,0:T(8,128)(2,1)S(1)}) custom-call(s32[1]{0:T(128)} %bitcast.core_ref, bf16[1440,128]{1,0:T(8,128)(2,1)S(1)} %get-tuple-element.16.refs_0_, bf16[720,128]{1,0:T(8,128)(2,1)S(1)} %collective-permute-done.after_ref.refs_1_, ...), custom_call_target="tpu_custom_call" | custom-call | flops 1000000000 | bytes 4000000 | tf_op jit(solution)/shard_map/pallas_call | solution.py:45
  60.1 0.3 collective-permute-done.6.got_ref
  60.4 0.9 shard_map.83
  61.2 25.3 %all_to_all.10 = bf16[32,80,128]{2,1,0:T(8,128)(2,1)S(1)} all-to-all(bf16[32,80,128]{2,1,0:T(8,128)(2,1)S(1)} %bitcast.16), channel_id=1, replica_groups=mesh['dp'=4,'y'=4,'z'=8,'core'=2] {'y','z'}, dimensions={0} | all-to-all | bytes 1310720 | tf_op jit(solution)/shard_map/all_to_all | solution.py:456
  86.6 1.3 %shard_map.84 = (bf16[128,1152]{1,0:T(8,128)(2,1)}, f32[18,288]{1,0:T(8,128)}) custom-call(bf16[2560,128]{1,0:T(8,128)(2,1)S(1)} %bitcast.15), custom_call_target="tpu_custom_call" | custom-call | tf_op jit(solution)/shard_map/pallas_call | solution.py:45
  (1 shorter events, 0.0 us)
Async XLA Ops:
  2.8 30.4 %all-to-all-start = ((bf16[32,8,1152]{2,1,0:T(8,128)(2,1)}), bf16[32,8,1152]{2,1,0:T(8,128)(2,1)S(1)}, u32[]{:S(2)}, u32[]{:S(2)}) async-start(bf16[32,8,1152]{2,1,0:T(8,128)(2,1)} %bitcast.18), calls=%async_computation | async-start | bytes 1179648 | tf_op jit(solution)/shard_map/all_to_all | solution.py:374
  33.2 13.3 %copy-start = (bf16[1152,1152]{1,0:T(8,128)(2,1)S(1)}, bf16[1152,1152]{1,0:T(8,128)(2,1)}, u32[]{:S(2)}) copy-start(bf16[1152,1152]{1,0:T(8,128)(2,1)} %w_out_ref.1) | copy-start | bytes 7962628
  33.2 21.2 %slice-start = ((s8[7962624]{0:T(1024)(128)(4,1)}), s8[4194304]{0:T(1024)(128)(4,1)S(1)}, s32[]{:S(2)}) async-start(s8[7962624]{0:T(1024)(128)(4,1)} %bitcast.13), calls=%async_computation.2 | async-start | bytes 8388608
  33.2 21.2 %slice-start.1 = ((s8[7962624]{0:T(1024)(128)(4,1)}), s8[3768320]{0:T(1024)(128)(4,1)S(1)}, s32[]{:S(2)}) async-start(s8[7962624]{0:T(1024)(128)(4,1)} %bitcast.13), calls=%async_computation.3 | async-start | bytes 7536640
  40.0 11.1 %collective-permute-start = (bf16[720,128]{1,0:T(8,128)(2,1)S(1)}, bf16[720,128]{1,0:T(8,128)(2,1)S(1)}, u32[]{:S(2)}, u32[]{:S(2)}) collective-permute-start(bf16[720,128]{1,0:T(8,128)(2,1)S(1)} %get-tuple-element.17), channel_id=1, source_target_pairs={{0,64},{64,128},{128,192},{192,0},{1,65},{65,129},{129,193},{193,1... | collective-permute-start | bytes 552968 | tf_op jit(solution)/shard_map/ppermute | solution.py:405
  41.6 9.7 %collective-permute-start.1 = (bf16[720,128]{1,0:T(8,128)(2,1)S(1)}, bf16[720,128]{1,0:T(8,128)(2,1)S(1)}, u32[]{:S(2)}, u32[]{:S(2)}) collective-permute-start(bf16[720,128]{1,0:T(8,128)(2,1)S(1)} %get-tuple-element.18), channel_id=1, source_target_pairs={{0,192},{64,0},{128,64},{192,128},{1,193},{65,1},{129,65},{193,129... | collective-permute-start | bytes 552968 | tf_op jit(solution)/shard_map/ppermute | solution.py:406
  43.3 13.7 %collective-permute-start.2 = (bf16[864,128]{1,0:T(8,128)(2,1)S(1)}, bf16[864,128]{1,0:T(8,128)(2,1)S(1)}, u32[]{:S(2)}, u32[]{:S(2)}) collective-permute-start(bf16[864,128]{1,0:T(8,128)(2,1)S(1)} %get-tuple-element.19), channel_id=1, source_target_pairs={{0,64},{64,128},{128,192},{192,0},{1,65},{65,129},{129,193},{193,1... | collective-permute-start | bytes 663560 | tf_op jit(solution)/shard_map/ppermute | solution.py:407
  43.6 13.5 %collective-permute-start.3 = (bf16[864,128]{1,0:T(8,128)(2,1)S(1)}, bf16[864,128]{1,0:T(8,128)(2,1)S(1)}, u32[]{:S(2)}, u32[]{:S(2)}) collective-permute-start(bf16[864,128]{1,0:T(8,128)(2,1)S(1)} %get-tuple-element.20), channel_id=1, source_target_pairs={{0,192},{64,0},{128,64},{192,128},{1,193},{65,1},{129,65},{193,129... | collective-permute-start | bytes 663560 | tf_op jit(solution)/shard_map/ppermute | solution.py:408
  51.2 6.8 %collective-permute-start.4 = (bf16[720,128]{1,0:T(8,128)(2,1)S(1)}, bf16[720,128]{1,0:T(8,128)(2,1)S(1)}, u32[]{:S(2)}, u32[]{:S(2)}) collective-permute-start(bf16[720,128]{1,0:T(8,128)(2,1)S(1)} %collective-permute-done.after_ref.refs_1_), channel_id=1, source_target_pairs={{0,64},{64,128},{128,192},{192,0},{1,65},{65,129},{129,193},{193,1... | collective-permute-start | bytes 552968 | tf_op jit(solution)/shard_map/ppermute | solution.py:418
  51.3 6.7 %collective-permute-start.5 = (bf16[720,128]{1,0:T(8,128)(2,1)S(1)}, bf16[720,128]{1,0:T(8,128)(2,1)S(1)}, u32[]{:S(2)}, u32[]{:S(2)}) collective-permute-start(bf16[720,128]{1,0:T(8,128)(2,1)S(1)} %collective-permute-done.1.also_after_ref.refs_2_), channel_id=1, source_target_pairs={{0,192},{64,0},{128,64},{192,128},{1,193},{65,1},{129,65},{193,129... | collective-permute-start | bytes 552968 | tf_op jit(solution)/shard_map/ppermute | solution.py:419
  58.5 1.9 %collective-permute-start.6 = (bf16[576,384]{1,0:T(8,128)(2,1)S(1)}, bf16[576,384]{1,0:T(8,128)(2,1)S(1)}, u32[]{:S(2)}, u32[]{:S(2)}) collective-permute-start(bf16[576,384]{1,0:T(8,128)(2,1)S(1)} %shard_map.81.refs_8_), channel_id=1, source_target_pairs={{0,1},{1,0},{2,3},{3,2},{4,5},{5,4},{6,7},{7,6},{8,9},{9,8},{10,11... | collective-permute-start | bytes 1327112 | tf_op jit(solution)/shard_map/ppermute | solution.py:439

commit v10 on v9

--- a/solution.py
+++ b/solution.py
@@ -224,11 +224,14 @@
     left_ref[:HALF, :] = attended[:HALF]
 
 
-def attention_grad_kernel(masked_ref, joined_ref, probs_ref, w_out_ref, grad_ref, head_ref):
+def head_grad_kernel(masked_ref, w_out_ref, head_ref):
     masked = masked_ref[...]
     for chunk in range(3):
         columns = slice(chunk * WIDE, (chunk + 1) * WIDE)
         head_ref[:, columns] = dot(masked, w_out_ref[columns, :], NT).astype(BF)
+
+
+def attention_grad_kernel(joined_ref, probs_ref, head_ref, after_ref, also_after_ref, grad_ref):
     patch = lane_patch()
     for head in range(H):
         base, width, inside = window(head)
@@ -253,9 +256,7 @@
                 grad_ref[:, at : at + width] = jnp.where(inside, part, grad_ref[:, at : at + width])
 
 
-def token_grad_kernel(
-    tokens_ref, masked_ref, grad_ref, w_qkv_ref, after_ref, also_after_ref, d_tokens_ref
-):
+def token_grad_kernel(tokens_ref, masked_ref, grad_ref, w_qkv_ref, d_tokens_ref):
     masked = masked_ref[...]
     pieces = []
     for chunk in range(3):
@@ -406,22 +407,29 @@
     right_a = lax.ppermute(left_far, "dp", down)
     left_b = lax.ppermute(right, "dp", up)
     right_b = lax.ppermute(left, "dp", down)
+    head_grads = call(
+        head_grad_kernel,
+        shape((ROWS, D), BF),
+        (masked, w_out),
+        limit=16,
+        flops=int(1e9),
+        data=int(4e6),
+    )
+    far_a = lax.ppermute(left_a, "dp", up)
+    far_b = lax.ppermute(right_a, "dp", down)
     grads = call(
         attention_grad_kernel,
         shape((ROWS, 3 * D), BF),
-        (masked, joined, probs, w_out),
-        scratch=(pltpu.VMEM((ROWS, D), BF),),
-        limit=24,
+        (joined, probs, head_grads, left_a, right_a),
+        far=(3, 4),
+        limit=16,
         flops=int(3e9),
         data=int(16e6),
     )
-    far_a = lax.ppermute(left_a, "dp", up)
-    far_b = lax.ppermute(right_a, "dp", down)
     d_rows = call(
         token_grad_kernel,
         shape((ROWS, D), BF),
-        (kept, masked, grads, w_qkv, left_a, right_a),
-        far=(4, 5),
+        (kept, masked, grads, w_qkv),
         limit=24,
         flops=int(3e9),
         data=int(16e6),

time: 88.6 us -> 88.2 us (level)
    ppermute x1, waiting for transfers between devices: 0.01 us -> 1.35 us  [body(): left_a = lax.ppermute(right_far, 'dp', up)]
    ppermute x1, waiting for transfers between devices: 0.9 us -> 0.01 us  [body(): far_a = lax.ppermute(left_a, 'dp', up)]
    pallas_call x8 -> x9, Pallas kernels: 20.2 us -> 19.9 us  [call(): pl.pallas_call(kernel, out_shape=shapes, in_specs=[pl.BlockSpec(memory_sp...]
where the time goes in v10:
time: 88.2 us; the launch traced here: 88 us
  blocking collectives  25.3 us (29%)
  starting transfers between devices  21.3 us (24%)
  Pallas kernels  19.9 us (23%)
  waiting for transfers between devices  17.3 us (20%)
  local copies, waits for them, and re-layouts  2.09 us (2%)
  between operations  1.43 us (2%)
    all_to_all x1, blocking collectives, body(): lax.all_to_all(merged.reshape(SLOTS, CHUNK, 128), ('y', 'z'), split_axis=...  25.3 us
    pallas_call x9, Pallas kernels, call(): pl.pallas_call(kernel, out_shape=shapes, in_specs=[pl.BlockSpec(memory_sp...  19.9 us
    all_to_all x1, waiting for transfers between devices, body(): lax.all_to_all(packed.reshape(SLOTS, 8, D), ('y', 'z'), split_axis=0, con...  15.6 us
    all_to_all x1, starting transfers between devices, body(): lax.all_to_all(packed.reshape(SLOTS, 8, D), ('y', 'z'), split_axis=0, con...  11.4 us
    ppermute x1, starting transfers between devices, body(): far_b = lax.ppermute(right_a, 'dp', down)  3.09 us
    ppermute x1, starting transfers between devices, body(): right_b = lax.ppermute(left, 'dp', down)  2.97 us
    slice x1, local copies, waits for them, and re-layouts, body(): firsts = tuple((w_qkv[:, kind * D:kind * D + WIDE] for kind in range(3)))  1.98 us
  transfers between devices with their start and end apart: 8, of which 3 were waited for; matrix products, arithmetic and copies ran while one was open for 3% of the time, Pallas kernels for 10%

profile of v10, /device:TPU:32, one launch (start us, length us, event | category | flops | bytes accessed | tf_op | source)
XLA Modules:
  0.0 88.0 jit_solution(7979362134563155102)
XLA Ops:
  0.6 2.2 %shard_map.77 = bf16[256,1152]{1,0:T(8,128)(2,1)} custom-call(bf16[128,1152]{1,0:T(8,128)(2,1)} %bitcast.19, bf16[128,1152]{1,0:T(8,128)(2,1)} %bitcast.20), custom_call_target="tpu_custom_call" | custom-call | tf_op jit(solution)/shard_map/pallas_call | solution.py:45
  2.8 11.4 %all-to-all-start = ((bf16[32,8,1152]{2,1,0:T(8,128)(2,1)}), bf16[32,8,1152]{2,1,0:T(8,128)(2,1)S(1)}, u32[]{:S(2)}, u32[]{:S(2)}) async-start(bf16[32,8,1152]{2,1,0:T(8,128)(2,1)} %bitcast.18), calls=%async_computation | async-start | bytes 1179648 | tf_op jit(solution)/shard_map/all_to_all | solution.py:375
  14.9 0.7 fusion
  15.5 0.1 copy.8.live_ref
  15.6 2.0 %fusion.1 = (bf16[1152,384]{1,0:T(8,128)(2,1)S(1)}, bf16[1152,384]{1,0:T(8,128)(2,1)S(1)}, bf16[1152,384]{1,0:T(8,128)(2,1)S(1)}) fusion(bf16[1152,3456]{1,0:T(8,128)(2,1)} %w_qkv_ref.3), kind=kLoop, calls=%fused_computation.2 | loop fusion | bytes 5308416 | tf_op jit(solution)/shard_map/slice | solution.py:378
  17.6 15.6 %all-to-all-done = bf16[32,8,1152]{2,1,0:T(8,128)(2,1)S(1)} async-done(((bf16[32,8,1152]{2,1,0:T(8,128)(2,1)}), bf16[32,8,1152]{2,1,0:T(8,128)(2,1)S(1)}, u32[]{:S(2)}, u32[]{:S(2)}) %all-to-all-start) | async-done | bytes 589856 | tf_op jit(solution)/shard_map/all_to_all | solution.py:375
  33.2 0.0 copy-start
  33.2 6.2 %shard_map.78 = (bf16[128,1152]{1,0:T(8,128)(2,1)S(1)}, bf16[128,1152]{1,0:T(8,128)(2,1)S(1)}, bf16[128,3456]{1,0:T(8,128)(2,1)S(1)}, f32[16,32,128]{2,1,0:T(8,1...) custom-call(s32[1]{0:T(128)} %bitcast.1.place_ref, ...), custom_call_target="tpu_custom_call" | custom-call | flops 2000000000 | bytes 14000000 | tf_op jit(solution)/shard_map/pallas_call | solution.py:45
  39.4 0.0 slice-start
  39.4 1.6 %collective-permute-start = (bf16[720,128]{1,0:T(8,128)(2,1)S(1)}, bf16[720,128]{1,0:T(8,128)(2,1)S(1)}, u32[]{:S(2)}, u32[]{:S(2)}) collective-permute-start(bf16[720,128]{1,0:T(8,128)(2,1)S(1)} %get-tuple-element.17), channel_id=1, source_target_pairs={{0,64},{64,128},{128,192},{192,0},{1,65},{65,129},{129,193},{193,1... | collective-permute-start | bytes 552968 | tf_op jit(solution)/shard_map/ppermute | solution.py:406
  41.0 1.8 %collective-permute-start.1 = (bf16[720,128]{1,0:T(8,128)(2,1)S(1)}, bf16[720,128]{1,0:T(8,128)(2,1)S(1)}, u32[]{:S(2)}, u32[]{:S(2)}) collective-permute-start(bf16[720,128]{1,0:T(8,128)(2,1)S(1)} %get-tuple-element.18), channel_id=1, source_target_pairs={{0,192},{64,0},{128,64},{192,128},{1,193},{65,1},{129,65},{193,129... | collective-permute-start | bytes 552968 | tf_op jit(solution)/shard_map/ppermute | solution.py:407
  42.8 0.3 collective-permute-start.2
  43.0 3.0 %collective-permute-start.3 = (bf16[864,128]{1,0:T(8,128)(2,1)S(1)}, bf16[864,128]{1,0:T(8,128)(2,1)S(1)}, u32[]{:S(2)}, u32[]{:S(2)}) collective-permute-start(bf16[864,128]{1,0:T(8,128)(2,1)S(1)} %get-tuple-element.20), channel_id=1, source_target_pairs={{0,192},{64,0},{128,64},{192,128},{1,193},{65,1},{129,65},{193,129... | collective-permute-start | bytes 663560 | tf_op jit(solution)/shard_map/ppermute | solution.py:409
  46.0 0.0 copy-done
  46.0 0.9 %shard_map.79.head_ref = bf16[128,1152]{1,0:T(8,128)(2,1)S(1)} custom-call(bf16[128,1152]{1,0:T(8,128)(2,1)S(1)} %get-tuple-element.22.masked_ref, bf16[1152,1152]{1,0:T(8,128)(2,1)S(1)} %copy-done), custom_call_target="tpu_custom_call" | custom-call | flops 1000000000 | bytes 4000000 | tf_op jit(solution)/shard_map/pallas_call | solution.py:45
  46.9 1.3 %collective-permute-done.after_ref.refs_1_ = bf16[720,128]{1,0:T(8,128)(2,1)S(1)} collective-permute-done((bf16[720,128]{1,0:T(8,128)(2,1)S(1)}, bf16[720,128]{1,0:T(8,128)(2,1)S(1)}, u32[]{:S(2)}, u32[]{:S(2)}) %collective-permute-start) | collective-permute-done | bytes 184352 | tf_op jit(solution)/shard_map/ppermute | solution.py:406
  48.2 0.1 collective-permute-start.4
  48.4 0.0 collective-permute-done.1.also_after_ref.refs_2_
  48.4 3.1 %collective-permute-start.5 = (bf16[720,128]{1,0:T(8,128)(2,1)S(1)}, bf16[720,128]{1,0:T(8,128)(2,1)S(1)}, u32[]{:S(2)}, u32[]{:S(2)}) collective-permute-start(bf16[720,128]{1,0:T(8,128)(2,1)S(1)} %collective-permute-done.1.also_after_ref.refs_2_), channel_id=1, source_target_pairs={{0,192},{64,0},{128,64},{192,128},{1,193},{65,1},{129,65},{193,129... | collective-permute-start | bytes 552968 | tf_op jit(solution)/shard_map/ppermute | solution.py:419
  51.5 0.0 slice-start.1
  51.5 4.0 %shard_map.80.grad_ref = bf16[128,3456]{1,0:T(8,128)(2,1)S(1)} custom-call(bf16[128,3456]{1,0:T(8,128)(2,1)S(1)} %get-tuple-element.23.joined_ref, f32[16,32,128]{2,1,0:T(8,128)S(1)} %get-tuple-element.24.probs_ref, bf16[128,1152]{1,0:T(8,128)(2,1)S(1)} %shard_map.79.head_ref, bf16[720,128]{1,0:T(8,128)(2,1)S(1)} %collective-permute-done.after_ref.refs_1_, ...), custom_call_target="tpu_custom_call" | custom-call | flops 3000000000 | bytes 16000000 | tf_op jit(solution)/shard_map/pallas_call | solution.py:45
  55.4 0.0 slice-done
  55.5 0.0 slice-done.1
  55.5 2.6 %shard_map.81.refs_7_ = bf16[128,1152]{1,0:T(8,128)(2,1)S(1)} custom-call(bf16[128,1152]{1,0:T(8,128)(2,1)S(1)} %get-tuple-element.21.tokens_ref, bf16[128,1152]{1,0:T(8,128)(2,1)S(1)} %get-tuple-element.22.masked_ref, bf16[128,3456]{1,0:T(8,128)(2,1)S(1)} %shard_map.80.grad_ref, bf16[1152,3456]{1,0:T(8,128)(2,1)S(1)} %bitcast.14), custom_call_target="tpu_custom_call" | custom-call | flops 3000000000 | bytes 16000000 | tf_op jit(solution)/shard_map/pallas_call | solution.py:45
  58.1 0.0 collective-permute-done.2.refs_3_
  58.1 0.0 collective-permute-done.3.refs_4_
  58.1 0.0 collective-permute-done.4.refs_5_
  58.1 0.0 collective-permute-done.5.refs_6_
  58.1 0.5 shard_map.82.refs_8_
  58.6 0.1 collective-permute-start.6
  58.7 1.5 %shard_map.83 = (f32[576,384]{1,0:T(8,128)S(1)}, bf16[2560,128]{1,0:T(8,128)(2,1)S(1)}, bf16[640,432]{1,0:T(8,128)(2,1)S(1)}) custom-call(s32[1]{0:T(128)} %bitcast.core_ref, bf16[1440,128]{1,0:T(8,128)(2,1)S(1)} %get-tuple-element.16.refs_0_, bf16[720,128]{1,0:T(8,128)(2,1)S(1)} %collective-permute-done.after_ref.refs_1_, ...), custom_call_target="tpu_custom_call" | custom-call | flops 1000000000 | bytes 4000000 | tf_op jit(solution)/shard_map/pallas_call | solution.py:45
  60.2 0.3 collective-permute-done.6.got_ref
  60.5 0.9 shard_map.84
  61.4 25.3 %all_to_all.10 = bf16[32,80,128]{2,1,0:T(8,128)(2,1)S(1)} all-to-all(bf16[32,80,128]{2,1,0:T(8,128)(2,1)S(1)} %bitcast.16), channel_id=1, replica_groups=mesh['dp'=4,'y'=4,'z'=8,'core'=2] {'y','z'}, dimensions={0} | all-to-all | bytes 1310720 | tf_op jit(solution)/shard_map/all_to_all | solution.py:464
  86.7 1.3 %shard_map.85 = (bf16[128,1152]{1,0:T(8,128)(2,1)}, f32[18,288]{1,0:T(8,128)}) custom-call(bf16[2560,128]{1,0:T(8,128)(2,1)S(1)} %bitcast.15), custom_call_target="tpu_custom_call" | custom-call | tf_op jit(solution)/shard_map/pallas_call | solution.py:45
  (1 shorter events, 0.0 us)
Async XLA Ops:
  2.8 30.4 %all-to-all-start = ((bf16[32,8,1152]{2,1,0:T(8,128)(2,1)}), bf16[32,8,1152]{2,1,0:T(8,128)(2,1)S(1)}, u32[]{:S(2)}, u32[]{:S(2)}) async-start(bf16[32,8,1152]{2,1,0:T(8,128)(2,1)} %bitcast.18), calls=%async_computation | async-start | bytes 1179648 | tf_op jit(solution)/shard_map/all_to_all | solution.py:375
  33.2 12.8 %copy-start = (bf16[1152,1152]{1,0:T(8,128)(2,1)S(1)}, bf16[1152,1152]{1,0:T(8,128)(2,1)}, u32[]{:S(2)}) copy-start(bf16[1152,1152]{1,0:T(8,128)(2,1)} %w_out_ref.1) | copy-start | bytes 7962628
  39.4 16.0 %slice-start = ((s8[7962624]{0:T(1024)(128)(4,1)}), s8[4194304]{0:T(1024)(128)(4,1)S(1)}, s32[]{:S(2)}) async-start(s8[7962624]{0:T(1024)(128)(4,1)} %bitcast.13), calls=%async_computation.2 | async-start | bytes 8388608
  39.4 8.8 %collective-permute-start = (bf16[720,128]{1,0:T(8,128)(2,1)S(1)}, bf16[720,128]{1,0:T(8,128)(2,1)S(1)}, u32[]{:S(2)}, u32[]{:S(2)}) collective-permute-start(bf16[720,128]{1,0:T(8,128)(2,1)S(1)} %get-tuple-element.17), channel_id=1, source_target_pairs={{0,64},{64,128},{128,192},{192,0},{1,65},{65,129},{129,193},{193,1... | collective-permute-start | bytes 552968 | tf_op jit(solution)/shard_map/ppermute | solution.py:406
  41.0 7.4 %collective-permute-start.1 = (bf16[720,128]{1,0:T(8,128)(2,1)S(1)}, bf16[720,128]{1,0:T(8,128)(2,1)S(1)}, u32[]{:S(2)}, u32[]{:S(2)}) collective-permute-start(bf16[720,128]{1,0:T(8,128)(2,1)S(1)} %get-tuple-element.18), channel_id=1, source_target_pairs={{0,192},{64,0},{128,64},{192,128},{1,193},{65,1},{129,65},{193,129... | collective-permute-start | bytes 552968 | tf_op jit(solution)/shard_map/ppermute | solution.py:407
  42.8 15.3 %collective-permute-start.2 = (bf16[864,128]{1,0:T(8,128)(2,1)S(1)}, bf16[864,128]{1,0:T(8,128)(2,1)S(1)}, u32[]{:S(2)}, u32[]{:S(2)}) collective-permute-start(bf16[864,128]{1,0:T(8,128)(2,1)S(1)} %get-tuple-element.19), channel_id=1, source_target_pairs={{0,64},{64,128},{128,192},{192,0},{1,65},{65,129},{129,193},{193,1... | collective-permute-start | bytes 663560 | tf_op jit(solution)/shard_map/ppermute | solution.py:408
  43.0 15.0 %collective-permute-start.3 = (bf16[864,128]{1,0:T(8,128)(2,1)S(1)}, bf16[864,128]{1,0:T(8,128)(2,1)S(1)}, u32[]{:S(2)}, u32[]{:S(2)}) collective-permute-start(bf16[864,128]{1,0:T(8,128)(2,1)S(1)} %get-tuple-element.20), channel_id=1, source_target_pairs={{0,192},{64,0},{128,64},{192,128},{1,193},{65,1},{129,65},{193,129... | collective-permute-start | bytes 663560 | tf_op jit(solution)/shard_map/ppermute | solution.py:409
  48.2 9.8 %collective-permute-start.4 = (bf16[720,128]{1,0:T(8,128)(2,1)S(1)}, bf16[720,128]{1,0:T(8,128)(2,1)S(1)}, u32[]{:S(2)}, u32[]{:S(2)}) collective-permute-start(bf16[720,128]{1,0:T(8,128)(2,1)S(1)} %collective-permute-done.after_ref.refs_1_), channel_id=1, source_target_pairs={{0,64},{64,128},{128,192},{192,0},{1,65},{65,129},{129,193},{193,1... | collective-permute-start | bytes 552968 | tf_op jit(solution)/shard_map/ppermute | solution.py:418
  48.4 9.7 %collective-permute-start.5 = (bf16[720,128]{1,0:T(8,128)(2,1)S(1)}, bf16[720,128]{1,0:T(8,128)(2,1)S(1)}, u32[]{:S(2)}, u32[]{:S(2)}) collective-permute-start(bf16[720,128]{1,0:T(8,128)(2,1)S(1)} %collective-permute-done.1.also_after_ref.refs_2_), channel_id=1, source_target_pairs={{0,192},{64,0},{128,64},{192,128},{1,193},{65,1},{129,65},{193,129... | collective-permute-start | bytes 552968 | tf_op jit(solution)/shard_map/ppermute | solution.py:419
  51.5 4.0 %slice-start.1 = ((s8[7962624]{0:T(1024)(128)(4,1)}), s8[3768320]{0:T(1024)(128)(4,1)S(1)}, s32[]{:S(2)}) async-start(s8[7962624]{0:T(1024)(128)(4,1)} %bitcast.13), calls=%async_computation.3 | async-start | bytes 7536640
  58.6 1.9 %collective-permute-start.6 = (bf16[576,384]{1,0:T(8,128)(2,1)S(1)}, bf16[576,384]{1,0:T(8,128)(2,1)S(1)}, u32[]{:S(2)}, u32[]{:S(2)}) collective-permute-start(bf16[576,384]{1,0:T(8,128)(2,1)S(1)} %shard_map.82.refs_8_), channel_id=1, source_target_pairs={{0,1},{1,0},{2,3},{3,2},{4,5},{5,4},{6,7},{7,6},{8,9},{9,8},{10,11... | collective-permute-start | bytes 1327112 | tf_op jit(solution)/shard_map/ppermute | solution.py:447

commit v11 on v9

--- a/solution.py
+++ b/solution.py
@@ -25,6 +25,7 @@
 TOKEN_ROWS = 36
 PAYLOAD = D + COLS
 HALF = D // 2
+EARLY_HEADS = 5
 EXP_SCALE = SCALE * math.log2(math.e)
 
 NN = (((1,), (0,)), ((), ()))
@@ -224,13 +225,9 @@
     left_ref[:HALF, :] = attended[:HALF]
 
 
-def attention_grad_kernel(masked_ref, joined_ref, probs_ref, w_out_ref, grad_ref, head_ref):
-    masked = masked_ref[...]
-    for chunk in range(3):
-        columns = slice(chunk * WIDE, (chunk + 1) * WIDE)
-        head_ref[:, columns] = dot(masked, w_out_ref[columns, :], NT).astype(BF)
+def attention_grads(heads, joined_ref, probs_ref, head_ref, grad_ref, stride, fresh):
     patch = lane_patch()
-    for head in range(H):
+    for head in heads:
         base, width, inside = window(head)
         queries = only(inside, joined_ref[:, base : base + width])
         keys_in = joined_ref[:, D + base : D + base + width]
@@ -246,21 +243,36 @@
             dot(spread(probs, patch), head_grad).astype(BF),
         )
         for index, part in enumerate(parts):
-            at = index * D + base
-            if head == 0:
+            at = index * stride + base
+            if fresh and head == heads[0]:
                 grad_ref[:, at : at + width] = part
             else:
                 grad_ref[:, at : at + width] = jnp.where(inside, part, grad_ref[:, at : at + width])
 
 
-def token_grad_kernel(
-    tokens_ref, masked_ref, grad_ref, w_qkv_ref, after_ref, also_after_ref, d_tokens_ref
+def early_grad_kernel(masked_ref, joined_ref, probs_ref, w_out_ref, head_ref, early_ref):
+    masked = masked_ref[...]
+    for chunk in range(3):
+        columns = slice(chunk * WIDE, (chunk + 1) * WIDE)
+        head_ref[:, columns] = dot(masked, w_out_ref[columns, :], NT).astype(BF)
+    attention_grads(range(EARLY_HEADS), joined_ref, probs_ref, head_ref, early_ref, WIDE, True)
+
+
+def late_grad_kernel(
+    tokens_ref, masked_ref, joined_ref, probs_ref, head_ref, early_ref, w_qkv_ref,
+    after_ref, also_after_ref, d_tokens_ref, grad_ref, weight_ref, sem,
 ):
+    weights = pltpu.make_async_copy(w_qkv_ref, weight_ref, sem)
+    weights.start()
+    for kind in range(3):
+        grad_ref[:, kind * D : kind * D + WIDE] = early_ref[:, kind * WIDE : (kind + 1) * WIDE]
+    attention_grads(range(EARLY_HEADS, H), joined_ref, probs_ref, head_ref, grad_ref, D, False)
     masked = masked_ref[...]
+    weights.wait()
     pieces = []
     for chunk in range(3):
         rows = slice(chunk * WIDE, (chunk + 1) * WIDE)
-        pieces.append(dot(grad_ref[...], w_qkv_ref[rows, :], NT))
+        pieces.append(dot(grad_ref[...], weight_ref[rows, :], NT))
     normed_grad = jnp.concatenate(pieces, axis=1)
     normalized, inverse = row_stats(tokens_ref[...])
     mean_grad = jnp.mean(normed_grad, axis=-1, keepdims=True)
@@ -406,25 +418,29 @@
     right_a = lax.ppermute(left_far, "dp", down)
     left_b = lax.ppermute(right, "dp", up)
     right_b = lax.ppermute(left, "dp", down)
-    grads = call(
-        attention_grad_kernel,
-        shape((ROWS, 3 * D), BF),
+    head_grads, early = call(
+        early_grad_kernel,
+        (shape((ROWS, D), BF), shape((ROWS, 3 * WIDE), BF)),
         (masked, joined, probs, w_out),
-        scratch=(pltpu.VMEM((ROWS, D), BF),),
-        limit=24,
-        flops=int(3e9),
-        data=int(16e6),
+        limit=16,
+        flops=int(2e9),
+        data=int(8e6),
     )
     far_a = lax.ppermute(left_a, "dp", up)
     far_b = lax.ppermute(right_a, "dp", down)
     d_rows = call(
-        token_grad_kernel,
+        late_grad_kernel,
         shape((ROWS, D), BF),
-        (kept, masked, grads, w_qkv, left_a, right_a),
-        far=(4, 5),
-        limit=24,
-        flops=int(3e9),
-        data=int(16e6),
+        (kept, masked, joined, probs, head_grads, early, w_qkv, left_a, right_a),
+        scratch=(
+            pltpu.VMEM((ROWS, 3 * D), BF),
+            pltpu.VMEM((D, 3 * D), BF),
+            pltpu.SemaphoreType.DMA,
+        ),
+        far=(6, 7, 8),
+        limit=48,
+        flops=int(6e9),
+        data=int(32e6),
     )
     payloads = (core.reshape(1), own, left_a, right_a, left_b, right_b, far_a, far_b)
     send = call(

time: 88.6 us -> 90 us (1.016)
  Pallas kernels: 20.2 us -> 22.8 us
    pallas_call x8, Pallas kernels: 20.2 us -> 22.8 us  [call(): pl.pallas_call(kernel, out_shape=shapes, in_specs=[pl.BlockSpec(memory_sp...]
  transfers between devices with their start and end apart: 8 -> 8, of which waited for: 3 -> 2; matrix products, arithmetic and copies ran while one was open for 3% -> 3% of each run, Pallas kernels for 10% -> 13%
where the time goes in v11:
time: 90 us; the launch traced here: 89.7 us
  blocking collectives  25.5 us (28%)
  Pallas kernels  22.8 us (25%)
  starting transfers between devices  21.3 us (24%)
  waiting for transfers between devices  16 us (18%)
  local copies, waits for them, and re-layouts  2.08 us (2%)
  between operations  1.41 us (2%)
    all_to_all x1, blocking collectives, body(): lax.all_to_all(merged.reshape(SLOTS, CHUNK, 128), ('y', 'z'), split_axis=...  25.5 us
    pallas_call x8, Pallas kernels, call(): pl.pallas_call(kernel, out_shape=shapes, in_specs=[pl.BlockSpec(memory_sp...  22.8 us
    all_to_all x1, waiting for transfers between devices, body(): lax.all_to_all(packed.reshape(SLOTS, 8, D), ('y', 'z'), split_axis=0, con...  15.6 us
    all_to_all x1, starting transfers between devices, body(): lax.all_to_all(packed.reshape(SLOTS, 8, D), ('y', 'z'), split_axis=0, con...  11.4 us
    ppermute x1, starting transfers between devices, body(): far_b = lax.ppermute(right_a, 'dp', down)  3.22 us
    ppermute x1, starting transfers between devices, body(): right_b = lax.ppermute(left, 'dp', down)  2.94 us
    slice x1, local copies, waits for them, and re-layouts, body(): firsts = tuple((w_qkv[:, kind * D:kind * D + WIDE] for kind in range(3)))  1.98 us
  transfers between devices with their start and end apart: 8, of which 2 were waited for; matrix products, arithmetic and copies ran while one was open for 3% of the time, Pallas kernels for 13%

profile of v11, /device:TPU:32, one launch (start us, length us, event | category | flops | bytes accessed | tf_op | source)
XLA Modules:
  0.0 89.7 jit_solution(5244289573468739822)
XLA Ops:
  0.6 2.2 %shard_map.77 = bf16[256,1152]{1,0:T(8,128)(2,1)} custom-call(bf16[128,1152]{1,0:T(8,128)(2,1)} %bitcast.17, bf16[128,1152]{1,0:T(8,128)(2,1)} %bitcast.18), custom_call_target="tpu_custom_call" | custom-call | tf_op jit(solution)/shard_map/pallas_call | solution.py:46
  2.8 11.4 %all-to-all-start = ((bf16[32,8,1152]{2,1,0:T(8,128)(2,1)}), bf16[32,8,1152]{2,1,0:T(8,128)(2,1)S(1)}, u32[]{:S(2)}, u32[]{:S(2)}) async-start(bf16[32,8,1152]{2,1,0:T(8,128)(2,1)} %bitcast.16), calls=%async_computation | async-start | bytes 1179648 | tf_op jit(solution)/shard_map/all_to_all | solution.py:386
  14.9 0.7 fusion
  15.5 0.1 copy.8.live_ref
  15.6 2.0 %fusion.1 = (bf16[1152,384]{1,0:T(8,128)(2,1)S(1)}, bf16[1152,384]{1,0:T(8,128)(2,1)S(1)}, bf16[1152,384]{1,0:T(8,128)(2,1)S(1)}) fusion(bf16[1152,3456]{1,0:T(8,128)(2,1)} %w_qkv_ref.3), kind=kLoop, calls=%fused_computation.2 | loop fusion | bytes 5308416 | tf_op jit(solution)/shard_map/slice | solution.py:389
  17.6 15.6 %all-to-all-done = bf16[32,8,1152]{2,1,0:T(8,128)(2,1)S(1)} async-done(((bf16[32,8,1152]{2,1,0:T(8,128)(2,1)}), bf16[32,8,1152]{2,1,0:T(8,128)(2,1)S(1)}, u32[]{:S(2)}, u32[]{:S(2)}) %all-to-all-start) | async-done | bytes 589856 | tf_op jit(solution)/shard_map/all_to_all | solution.py:386
  33.2 0.0 copy-start
  33.2 6.2 %shard_map.78 = (bf16[128,1152]{1,0:T(8,128)(2,1)S(1)}, bf16[128,1152]{1,0:T(8,128)(2,1)S(1)}, bf16[128,3456]{1,0:T(8,128)(2,1)S(1)}, f32[16,32,128]{2,1,0:T(8,1...) custom-call(s32[1]{0:T(128)} %bitcast.1.place_ref, ...), custom_call_target="tpu_custom_call" | custom-call | flops 2000000000 | bytes 14000000 | tf_op jit(solution)/shard_map/pallas_call | solution.py:46
  39.4 1.6 %collective-permute-start = (bf16[720,128]{1,0:T(8,128)(2,1)S(1)}, bf16[720,128]{1,0:T(8,128)(2,1)S(1)}, u32[]{:S(2)}, u32[]{:S(2)}) collective-permute-start(bf16[720,128]{1,0:T(8,128)(2,1)S(1)} %get-tuple-element.19), channel_id=1, source_target_pairs={{0,64},{64,128},{128,192},{192,0},{1,65},{65,129},{129,193},{193,1... | collective-permute-start | bytes 552968 | tf_op jit(solution)/shard_map/ppermute | solution.py:417
  41.0 1.8 %collective-permute-start.1 = (bf16[720,128]{1,0:T(8,128)(2,1)S(1)}, bf16[720,128]{1,0:T(8,128)(2,1)S(1)}, u32[]{:S(2)}, u32[]{:S(2)}) collective-permute-start(bf16[720,128]{1,0:T(8,128)(2,1)S(1)} %get-tuple-element.20), channel_id=1, source_target_pairs={{0,192},{64,0},{128,64},{192,128},{1,193},{65,1},{129,65},{193,129... | collective-permute-start | bytes 552968 | tf_op jit(solution)/shard_map/ppermute | solution.py:418
  42.7 0.3 collective-permute-start.2
  43.0 2.9 %collective-permute-start.3 = (bf16[864,128]{1,0:T(8,128)(2,1)S(1)}, bf16[864,128]{1,0:T(8,128)(2,1)S(1)}, u32[]{:S(2)}, u32[]{:S(2)}) collective-permute-start(bf16[864,128]{1,0:T(8,128)(2,1)S(1)} %get-tuple-element.22), channel_id=1, source_target_pairs={{0,192},{64,0},{128,64},{192,128},{1,193},{65,1},{129,65},{193,129... | collective-permute-start | bytes 663560 | tf_op jit(solution)/shard_map/ppermute | solution.py:420
  46.0 0.0 copy-done
  46.0 2.0 %shard_map.79 = (bf16[128,1152]{1,0:T(8,128)(2,1)S(1)}, bf16[128,1152]{1,0:T(8,128)(2,1)S(1)}) custom-call(bf16[128,1152]{1,0:T(8,128)(2,1)S(1)} %get-tuple-element.24.masked_ref, bf16[128,3456]{1,0:T(8,128)(2,1)S(1)} %get-tuple-element.25.joined_ref, f32[16,32,128]{2,1,0:T(8,128)S(1)} %get-tuple-element.26.probs_ref, bf16[1152,1152]{1,0:T(8,128)(2,1)S(1)} %copy-done), custom_call_target="tpu_custom_call" | custom-call | flops 2000000000 | bytes 8000000 | tf_op jit(solution)/shard_map/pallas_call | solution.py:46
  48.0 0.0 collective-permute-done.after_ref.refs_1_
  48.0 0.1 collective-permute-start.4
  48.1 0.0 collective-permute-done.1.also_after_ref.refs_2_
  48.1 3.2 %collective-permute-start.5 = (bf16[720,128]{1,0:T(8,128)(2,1)S(1)}, bf16[720,128]{1,0:T(8,128)(2,1)S(1)}, u32[]{:S(2)}, u32[]{:S(2)}) collective-permute-start(bf16[720,128]{1,0:T(8,128)(2,1)S(1)} %collective-permute-done.1.also_after_ref.refs_2_), channel_id=1, source_target_pairs={{0,192},{64,0},{128,64},{192,128},{1,193},{65,1},{129,65},{193,129... | collective-permute-start | bytes 552968 | tf_op jit(solution)/shard_map/ppermute | solution.py:430
  51.4 8.3 %shard_map.80.refs_7_ = bf16[128,1152]{1,0:T(8,128)(2,1)S(1)} custom-call(bf16[128,1152]{1,0:T(8,128)(2,1)S(1)} %get-tuple-element.23.tokens_ref, bf16[128,1152]{1,0:T(8,128)(2,1)S(1)} %get-tuple-element.24.masked_ref, bf16[128,3456]{1,0:T(8,128)(2,1)S(1)} %get-tuple-element.25.joined_ref, f32[16,32,128]{2,1,0:T(8,128)S(1)} %get-tuple-element.26.probs_ref, ...), custom_call_target="tpu_custom_call" | custom-call | flops 6000000000 | bytes 32000000 | tf_op jit(solution)/shard_map/pallas_call | solution.py:46
  59.7 0.0 collective-permute-done.2.refs_3_
  59.7 0.0 collective-permute-done.3.refs_4_
  59.7 0.0 collective-permute-done.4.refs_5_
  59.7 0.0 collective-permute-done.5.refs_6_
  59.8 0.5 shard_map.81.refs_8_
  60.3 0.1 collective-permute-start.6
  60.4 1.5 %shard_map.82 = (f32[576,384]{1,0:T(8,128)S(1)}, bf16[2560,128]{1,0:T(8,128)(2,1)S(1)}, bf16[640,432]{1,0:T(8,128)(2,1)S(1)}) custom-call(s32[1]{0:T(128)} %bitcast.core_ref, bf16[1440,128]{1,0:T(8,128)(2,1)S(1)} %get-tuple-element.18.refs_0_, bf16[720,128]{1,0:T(8,128)(2,1)S(1)} %collective-permute-done.after_ref.refs_1_, ...), custom_call_target="tpu_custom_call" | custom-call | flops 1000000000 | bytes 4000000 | tf_op jit(solution)/shard_map/pallas_call | solution.py:46
  61.8 0.3 collective-permute-done.6.got_ref
  62.1 0.9 shard_map.83
  63.0 25.5 %all_to_all.10 = bf16[32,80,128]{2,1,0:T(8,128)(2,1)S(1)} all-to-all(bf16[32,80,128]{2,1,0:T(8,128)(2,1)S(1)} %bitcast.14), channel_id=1, replica_groups=mesh['dp'=4,'y'=4,'z'=8,'core'=2] {'y','z'}, dimensions={0} | all-to-all | bytes 1310720 | tf_op jit(solution)/shard_map/all_to_all | solution.py:472
  88.5 1.3 %shard_map.84 = (bf16[128,1152]{1,0:T(8,128)(2,1)}, f32[18,288]{1,0:T(8,128)}) custom-call(bf16[2560,128]{1,0:T(8,128)(2,1)S(1)} %bitcast.13), custom_call_target="tpu_custom_call" | custom-call | tf_op jit(solution)/shard_map/pallas_call | solution.py:46
Async XLA Ops:
  2.8 30.4 %all-to-all-start = ((bf16[32,8,1152]{2,1,0:T(8,128)(2,1)}), bf16[32,8,1152]{2,1,0:T(8,128)(2,1)S(1)}, u32[]{:S(2)}, u32[]{:S(2)}) async-start(bf16[32,8,1152]{2,1,0:T(8,128)(2,1)} %bitcast.16), calls=%async_computation | async-start | bytes 1179648 | tf_op jit(solution)/shard_map/all_to_all | solution.py:386
  33.2 12.7 %copy-start = (bf16[1152,1152]{1,0:T(8,128)(2,1)S(1)}, bf16[1152,1152]{1,0:T(8,128)(2,1)}, u32[]{:S(2)}) copy-start(bf16[1152,1152]{1,0:T(8,128)(2,1)} %w_out_ref.1) | copy-start | bytes 7962628
  39.4 8.6 %collective-permute-start = (bf16[720,128]{1,0:T(8,128)(2,1)S(1)}, bf16[720,128]{1,0:T(8,128)(2,1)S(1)}, u32[]{:S(2)}, u32[]{:S(2)}) collective-permute-start(bf16[720,128]{1,0:T(8,128)(2,1)S(1)} %get-tuple-element.19), channel_id=1, source_target_pairs={{0,64},{64,128},{128,192},{192,0},{1,65},{65,129},{129,193},{193,1... | collective-permute-start | bytes 552968 | tf_op jit(solution)/shard_map/ppermute | solution.py:417
  41.0 7.1 %collective-permute-start.1 = (bf16[720,128]{1,0:T(8,128)(2,1)S(1)}, bf16[720,128]{1,0:T(8,128)(2,1)S(1)}, u32[]{:S(2)}, u32[]{:S(2)}) collective-permute-start(bf16[720,128]{1,0:T(8,128)(2,1)S(1)} %get-tuple-element.20), channel_id=1, source_target_pairs={{0,192},{64,0},{128,64},{192,128},{1,193},{65,1},{129,65},{193,129... | collective-permute-start | bytes 552968 | tf_op jit(solution)/shard_map/ppermute | solution.py:418
  42.7 17.0 %collective-permute-start.2 = (bf16[864,128]{1,0:T(8,128)(2,1)S(1)}, bf16[864,128]{1,0:T(8,128)(2,1)S(1)}, u32[]{:S(2)}, u32[]{:S(2)}) collective-permute-start(bf16[864,128]{1,0:T(8,128)(2,1)S(1)} %get-tuple-element.21), channel_id=1, source_target_pairs={{0,64},{64,128},{128,192},{192,0},{1,65},{65,129},{129,193},{193,1... | collective-permute-start | bytes 663560 | tf_op jit(solution)/shard_map/ppermute | solution.py:419
  43.0 16.7 %collective-permute-start.3 = (bf16[864,128]{1,0:T(8,128)(2,1)S(1)}, bf16[864,128]{1,0:T(8,128)(2,1)S(1)}, u32[]{:S(2)}, u32[]{:S(2)}) collective-permute-start(bf16[864,128]{1,0:T(8,128)(2,1)S(1)} %get-tuple-element.22), channel_id=1, source_target_pairs={{0,192},{64,0},{128,64},{192,128},{1,193},{65,1},{129,65},{193,129... | collective-permute-start | bytes 663560 | tf_op jit(solution)/shard_map/ppermute | solution.py:420
  48.0 11.7 %collective-permute-start.4 = (bf16[720,128]{1,0:T(8,128)(2,1)S(1)}, bf16[720,128]{1,0:T(8,128)(2,1)S(1)}, u32[]{:S(2)}, u32[]{:S(2)}) collective-permute-start(bf16[720,128]{1,0:T(8,128)(2,1)S(1)} %collective-permute-done.after_ref.refs_1_), channel_id=1, source_target_pairs={{0,64},{64,128},{128,192},{192,0},{1,65},{65,129},{129,193},{193,1... | collective-permute-start | bytes 552968 | tf_op jit(solution)/shard_map/ppermute | solution.py:429
  48.1 11.6 %collective-permute-start.5 = (bf16[720,128]{1,0:T(8,128)(2,1)S(1)}, bf16[720,128]{1,0:T(8,128)(2,1)S(1)}, u32[]{:S(2)}, u32[]{:S(2)}) collective-permute-start(bf16[720,128]{1,0:T(8,128)(2,1)S(1)} %collective-permute-done.1.also_after_ref.refs_2_), channel_id=1, source_target_pairs={{0,192},{64,0},{128,64},{192,128},{1,193},{65,1},{129,65},{193,129... | collective-permute-start | bytes 552968 | tf_op jit(solution)/shard_map/ppermute | solution.py:430
  60.3 1.9 %collective-permute-start.6 = (bf16[576,384]{1,0:T(8,128)(2,1)S(1)}, bf16[576,384]{1,0:T(8,128)(2,1)S(1)}, u32[]{:S(2)}, u32[]{:S(2)}) collective-permute-start(bf16[576,384]{1,0:T(8,128)(2,1)S(1)} %shard_map.81.refs_8_), channel_id=1, source_target_pairs={{0,1},{1,0},{2,3},{3,2},{4,5},{5,4},{6,7},{7,6},{8,9},{9,8},{10,11... | collective-permute-start | bytes 1327112 | tf_op jit(solution)/shard_map/ppermute | solution.py:455

commit v12 on v11

--- a/solution.py
+++ b/solution.py
@@ -259,20 +259,19 @@
 
 
 def late_grad_kernel(
-    tokens_ref, masked_ref, joined_ref, probs_ref, head_ref, early_ref, w_qkv_ref,
-    after_ref, also_after_ref, d_tokens_ref, grad_ref, weight_ref, sem,
+    joined_ref, probs_ref, head_ref, early_ref, after_ref, also_after_ref, grad_ref
 ):
-    weights = pltpu.make_async_copy(w_qkv_ref, weight_ref, sem)
-    weights.start()
     for kind in range(3):
         grad_ref[:, kind * D : kind * D + WIDE] = early_ref[:, kind * WIDE : (kind + 1) * WIDE]
     attention_grads(range(EARLY_HEADS, H), joined_ref, probs_ref, head_ref, grad_ref, D, False)
+
+
+def token_grad_kernel(tokens_ref, masked_ref, grad_ref, w_qkv_ref, d_tokens_ref):
     masked = masked_ref[...]
-    weights.wait()
     pieces = []
     for chunk in range(3):
         rows = slice(chunk * WIDE, (chunk + 1) * WIDE)
-        pieces.append(dot(grad_ref[...], weight_ref[rows, :], NT))
+        pieces.append(dot(grad_ref[...], w_qkv_ref[rows, :], NT))
     normed_grad = jnp.concatenate(pieces, axis=1)
     normalized, inverse = row_stats(tokens_ref[...])
     mean_grad = jnp.mean(normed_grad, axis=-1, keepdims=True)
@@ -428,19 +427,22 @@
     )
     far_a = lax.ppermute(left_a, "dp", up)
     far_b = lax.ppermute(right_a, "dp", down)
+    grads = call(
+        late_grad_kernel,
+        shape((ROWS, 3 * D), BF),
+        (joined, probs, head_grads, early, left_a, right_a),
+        far=(4, 5),
+        limit=16,
+        flops=int(3e9),
+        data=int(16e6),
+    )
     d_rows = call(
-        late_grad_kernel,
+        token_grad_kernel,
         shape((ROWS, D), BF),
-        (kept, masked, joined, probs, head_grads, early, w_qkv, left_a, right_a),
-        scratch=(
-            pltpu.VMEM((ROWS, 3 * D), BF),
-            pltpu.VMEM((D, 3 * D), BF),
-            pltpu.SemaphoreType.DMA,
-        ),
-        far=(6, 7, 8),
-        limit=48,
-        flops=int(6e9),
-        data=int(32e6),
+        (kept, masked, grads, w_qkv),
+        limit=24,
+        flops=int(3e9),
+        data=int(16e6),
     )
     payloads = (core.reshape(1), own, left_a, right_a, left_b, right_b, far_a, far_b)
     send = call(

time: 90 us -> 87 us (0.967)
  Pallas kernels: 22.8 us -> 19.8 us
    pallas_call x8 -> x9, Pallas kernels: 22.8 us -> 19.8 us  [call(): pl.pallas_call(kernel, out_shape=shapes, in_specs=[pl.BlockSpec(memory_sp...]
  transfers between devices with their start and end apart: 8 -> 8, of which waited for: 2 -> 2; matrix products, arithmetic and copies ran while one was open for 3% -> 3% of each run, Pallas kernels for 13% -> 10%
where the time goes in v12:
time: 87 us; the launch traced here: 86.7 us
  blocking collectives  25.5 us (29%)
  starting transfers between devices  21.3 us (24%)
  Pallas kernels  19.8 us (23%)
  waiting for transfers between devices  16 us (18%)
  local copies, waits for them, and re-layouts  2.09 us (2%)
  between operations  1.45 us (2%)
    all_to_all x1, blocking collectives, body(): lax.all_to_all(merged.reshape(SLOTS, CHUNK, 128), ('y', 'z'), split_axis=...  25.5 us
    pallas_call x9, Pallas kernels, call(): pl.pallas_call(kernel, out_shape=shapes, in_specs=[pl.BlockSpec(memory_sp...  19.8 us
    all_to_all x1, waiting for transfers between devices, body(): lax.all_to_all(packed.reshape(SLOTS, 8, D), ('y', 'z'), split_axis=0, con...  15.6 us
    all_to_all x1, starting transfers between devices, body(): lax.all_to_all(packed.reshape(SLOTS, 8, D), ('y', 'z'), split_axis=0, con...  11.4 us
    ppermute x1, starting transfers between devices, body(): far_b = lax.ppermute(right_a, 'dp', down)  3.22 us
    ppermute x1, starting transfers between devices, body(): right_b = lax.ppermute(left, 'dp', down)  2.95 us
    slice x1, local copies, waits for them, and re-layouts, body(): firsts = tuple((w_qkv[:, kind * D:kind * D + WIDE] for kind in range(3)))  1.98 us
    ppermute x1, starting transfers between devices, body(): right_a = lax.ppermute(left_far, 'dp', down)  1.76 us
  transfers between devices with their start and end apart: 8, of which 2 were waited for; matrix products, arithmetic and copies ran while one was open for 3% of the time, Pallas kernels for 10%

profile of v12, /device:TPU:32, one launch (start us, length us, event | category | flops | bytes accessed | tf_op | source)
XLA Modules:
  0.0 86.7 jit_solution(12615270805247872008)
XLA Ops:
  0.6 2.2 %shard_map.77 = bf16[256,1152]{1,0:T(8,128)(2,1)} custom-call(bf16[128,1152]{1,0:T(8,128)(2,1)} %bitcast.19, bf16[128,1152]{1,0:T(8,128)(2,1)} %bitcast.20), custom_call_target="tpu_custom_call" | custom-call | tf_op jit(solution)/shard_map/pallas_call | solution.py:46
  2.9 11.4 %all-to-all-start = ((bf16[32,8,1152]{2,1,0:T(8,128)(2,1)}), bf16[32,8,1152]{2,1,0:T(8,128)(2,1)S(1)}, u32[]{:S(2)}, u32[]{:S(2)}) async-start(bf16[32,8,1152]{2,1,0:T(8,128)(2,1)} %bitcast.18), calls=%async_computation | async-start | bytes 1179648 | tf_op jit(solution)/shard_map/all_to_all | solution.py:385
  14.9 0.7 fusion
  15.6 0.1 copy.8.live_ref
  15.7 2.0 %fusion.1 = (bf16[1152,384]{1,0:T(8,128)(2,1)S(1)}, bf16[1152,384]{1,0:T(8,128)(2,1)S(1)}, bf16[1152,384]{1,0:T(8,128)(2,1)S(1)}) fusion(bf16[1152,3456]{1,0:T(8,128)(2,1)} %w_qkv_ref.3), kind=kLoop, calls=%fused_computation.2 | loop fusion | bytes 5308416 | tf_op jit(solution)/shard_map/slice | solution.py:388
  17.6 15.6 %all-to-all-done = bf16[32,8,1152]{2,1,0:T(8,128)(2,1)S(1)} async-done(((bf16[32,8,1152]{2,1,0:T(8,128)(2,1)}), bf16[32,8,1152]{2,1,0:T(8,128)(2,1)S(1)}, u32[]{:S(2)}, u32[]{:S(2)}) %all-to-all-start) | async-done | bytes 589856 | tf_op jit(solution)/shard_map/all_to_all | solution.py:385
  33.3 0.0 copy-start
  33.3 6.2 %shard_map.78 = (bf16[128,1152]{1,0:T(8,128)(2,1)S(1)}, bf16[128,1152]{1,0:T(8,128)(2,1)S(1)}, bf16[128,3456]{1,0:T(8,128)(2,1)S(1)}, f32[16,32,128]{2,1,0:T(8,1...) custom-call(s32[1]{0:T(128)} %bitcast.1.place_ref, ...), custom_call_target="tpu_custom_call" | custom-call | flops 2000000000 | bytes 14000000 | tf_op jit(solution)/shard_map/pallas_call | solution.py:46
  39.4 1.6 %collective-permute-start = (bf16[720,128]{1,0:T(8,128)(2,1)S(1)}, bf16[720,128]{1,0:T(8,128)(2,1)S(1)}, u32[]{:S(2)}, u32[]{:S(2)}) collective-permute-start(bf16[720,128]{1,0:T(8,128)(2,1)S(1)} %get-tuple-element.19), channel_id=1, source_target_pairs={{0,64},{64,128},{128,192},{192,0},{1,65},{65,129},{129,193},{193,1... | collective-permute-start | bytes 552968 | tf_op jit(solution)/shard_map/ppermute | solution.py:416
  41.0 1.8 %collective-permute-start.1 = (bf16[720,128]{1,0:T(8,128)(2,1)S(1)}, bf16[720,128]{1,0:T(8,128)(2,1)S(1)}, u32[]{:S(2)}, u32[]{:S(2)}) collective-permute-start(bf16[720,128]{1,0:T(8,128)(2,1)S(1)} %get-tuple-element.20), channel_id=1, source_target_pairs={{0,192},{64,0},{128,64},{192,128},{1,193},{65,1},{129,65},{193,129... | collective-permute-start | bytes 552968 | tf_op jit(solution)/shard_map/ppermute | solution.py:417
  42.8 0.3 collective-permute-start.2
  43.0 3.0 %collective-permute-start.3 = (bf16[864,128]{1,0:T(8,128)(2,1)S(1)}, bf16[864,128]{1,0:T(8,128)(2,1)S(1)}, u32[]{:S(2)}, u32[]{:S(2)}) collective-permute-start(bf16[864,128]{1,0:T(8,128)(2,1)S(1)} %get-tuple-element.22), channel_id=1, source_target_pairs={{0,192},{64,0},{128,64},{192,128},{1,193},{65,1},{129,65},{193,129... | collective-permute-start | bytes 663560 | tf_op jit(solution)/shard_map/ppermute | solution.py:419
  46.0 0.0 copy-done
  46.0 0.0 slice-start
  46.0 2.0 %shard_map.79 = (bf16[128,1152]{1,0:T(8,128)(2,1)S(1)}, bf16[128,1152]{1,0:T(8,128)(2,1)S(1)}) custom-call(bf16[128,1152]{1,0:T(8,128)(2,1)S(1)} %get-tuple-element.24.masked_ref, bf16[128,3456]{1,0:T(8,128)(2,1)S(1)} %get-tuple-element.25.joined_ref, f32[16,32,128]{2,1,0:T(8,128)S(1)} %get-tuple-element.26.probs_ref, bf16[1152,1152]{1,0:T(8,128)(2,1)S(1)} %copy-done), custom_call_target="tpu_custom_call" | custom-call | flops 2000000000 | bytes 8000000 | tf_op jit(solution)/shard_map/pallas_call | solution.py:46
  48.0 0.0 collective-permute-done.after_ref.refs_1_
  48.0 0.1 collective-permute-start.4
  48.1 0.0 collective-permute-done.1.also_after_ref.refs_2_
  48.1 3.2 %collective-permute-start.5 = (bf16[720,128]{1,0:T(8,128)(2,1)S(1)}, bf16[720,128]{1,0:T(8,128)(2,1)S(1)}, u32[]{:S(2)}, u32[]{:S(2)}) collective-permute-start(bf16[720,128]{1,0:T(8,128)(2,1)S(1)} %collective-permute-done.1.also_after_ref.refs_2_), channel_id=1, source_target_pairs={{0,192},{64,0},{128,64},{192,128},{1,193},{65,1},{129,65},{193,129... | collective-permute-start | bytes 552968 | tf_op jit(solution)/shard_map/ppermute | solution.py:429
  51.4 0.0 slice-start.1
  51.4 2.7 %shard_map.80.grad_ref = bf16[128,3456]{1,0:T(8,128)(2,1)S(1)} custom-call(bf16[128,3456]{1,0:T(8,128)(2,1)S(1)} %get-tuple-element.25.joined_ref, f32[16,32,128]{2,1,0:T(8,128)S(1)} %get-tuple-element.26.probs_ref, bf16[128,1152]{1,0:T(8,128)(2,1)S(1)} %get-tuple-element.27.head_ref, bf16[128,1152]{1,0:T(8,128)(2,1)S(1)} %get-tuple-element.28.early_ref, ...), custom_call_target="tpu_custom_call" | custom-call | flops 3000000000 | bytes 16000000 | tf_op jit(solution)/shard_map/pallas_call | solution.py:46
  54.1 0.0 slice-done
  54.1 0.0 slice-done.1
  54.1 2.6 %shard_map.81.refs_7_ = bf16[128,1152]{1,0:T(8,128)(2,1)S(1)} custom-call(bf16[128,1152]{1,0:T(8,128)(2,1)S(1)} %get-tuple-element.23.tokens_ref, bf16[128,1152]{1,0:T(8,128)(2,1)S(1)} %get-tuple-element.24.masked_ref, bf16[128,3456]{1,0:T(8,128)(2,1)S(1)} %shard_map.80.grad_ref, bf16[1152,3456]{1,0:T(8,128)(2,1)S(1)} %bitcast.14), custom_call_target="tpu_custom_call" | custom-call | flops 3000000000 | bytes 16000000 | tf_op jit(solution)/shard_map/pallas_call | solution.py:46
  56.7 0.0 collective-permute-done.2.refs_3_
  56.7 0.0 collective-permute-done.3.refs_4_
  56.7 0.0 collective-permute-done.4.refs_5_
  56.8 0.0 collective-permute-done.5.refs_6_
  56.8 0.5 shard_map.82.refs_8_
  57.3 0.1 collective-permute-start.6
  57.4 1.5 %shard_map.83 = (f32[576,384]{1,0:T(8,128)S(1)}, bf16[2560,128]{1,0:T(8,128)(2,1)S(1)}, bf16[640,432]{1,0:T(8,128)(2,1)S(1)}) custom-call(s32[1]{0:T(128)} %bitcast.core_ref, bf16[1440,128]{1,0:T(8,128)(2,1)S(1)} %get-tuple-element.18.refs_0_, bf16[720,128]{1,0:T(8,128)(2,1)S(1)} %collective-permute-done.after_ref.refs_1_, ...), custom_call_target="tpu_custom_call" | custom-call | flops 1000000000 | bytes 4000000 | tf_op jit(solution)/shard_map/pallas_call | solution.py:46
  58.8 0.3 collective-permute-done.6.got_ref
  59.1 0.9 shard_map.84
  60.0 25.5 %all_to_all.10 = bf16[32,80,128]{2,1,0:T(8,128)(2,1)S(1)} all-to-all(bf16[32,80,128]{2,1,0:T(8,128)(2,1)S(1)} %bitcast.16), channel_id=1, replica_groups=mesh['dp'=4,'y'=4,'z'=8,'core'=2] {'y','z'}, dimensions={0} | all-to-all | bytes 1310720 | tf_op jit(solution)/shard_map/all_to_all | solution.py:474
  85.5 1.3 %shard_map.85 = (bf16[128,1152]{1,0:T(8,128)(2,1)}, f32[18,288]{1,0:T(8,128)}) custom-call(bf16[2560,128]{1,0:T(8,128)(2,1)S(1)} %bitcast.15), custom_call_target="tpu_custom_call" | custom-call | tf_op jit(solution)/shard_map/pallas_call | solution.py:46
  (1 shorter events, 0.0 us)
Async XLA Ops:
  2.9 30.4 %all-to-all-start = ((bf16[32,8,1152]{2,1,0:T(8,128)(2,1)}), bf16[32,8,1152]{2,1,0:T(8,128)(2,1)S(1)}, u32[]{:S(2)}, u32[]{:S(2)}) async-start(bf16[32,8,1152]{2,1,0:T(8,128)(2,1)} %bitcast.18), calls=%async_computation | async-start | bytes 1179648 | tf_op jit(solution)/shard_map/all_to_all | solution.py:385
  33.3 12.7 %copy-start = (bf16[1152,1152]{1,0:T(8,128)(2,1)S(1)}, bf16[1152,1152]{1,0:T(8,128)(2,1)}, u32[]{:S(2)}) copy-start(bf16[1152,1152]{1,0:T(8,128)(2,1)} %w_out_ref.1) | copy-start | bytes 7962628
  39.4 8.6 %collective-permute-start = (bf16[720,128]{1,0:T(8,128)(2,1)S(1)}, bf16[720,128]{1,0:T(8,128)(2,1)S(1)}, u32[]{:S(2)}, u32[]{:S(2)}) collective-permute-start(bf16[720,128]{1,0:T(8,128)(2,1)S(1)} %get-tuple-element.19), channel_id=1, source_target_pairs={{0,64},{64,128},{128,192},{192,0},{1,65},{65,129},{129,193},{193,1... | collective-permute-start | bytes 552968 | tf_op jit(solution)/shard_map/ppermute | solution.py:416
  41.0 7.1 %collective-permute-start.1 = (bf16[720,128]{1,0:T(8,128)(2,1)S(1)}, bf16[720,128]{1,0:T(8,128)(2,1)S(1)}, u32[]{:S(2)}, u32[]{:S(2)}) collective-permute-start(bf16[720,128]{1,0:T(8,128)(2,1)S(1)} %get-tuple-element.20), channel_id=1, source_target_pairs={{0,192},{64,0},{128,64},{192,128},{1,193},{65,1},{129,65},{193,129... | collective-permute-start | bytes 552968 | tf_op jit(solution)/shard_map/ppermute | solution.py:417
  42.8 14.0 %collective-permute-start.2 = (bf16[864,128]{1,0:T(8,128)(2,1)S(1)}, bf16[864,128]{1,0:T(8,128)(2,1)S(1)}, u32[]{:S(2)}, u32[]{:S(2)}) collective-permute-start(bf16[864,128]{1,0:T(8,128)(2,1)S(1)} %get-tuple-element.21), channel_id=1, source_target_pairs={{0,64},{64,128},{128,192},{192,0},{1,65},{65,129},{129,193},{193,1... | collective-permute-start | bytes 663560 | tf_op jit(solution)/shard_map/ppermute | solution.py:418
  43.0 13.7 %collective-permute-start.3 = (bf16[864,128]{1,0:T(8,128)(2,1)S(1)}, bf16[864,128]{1,0:T(8,128)(2,1)S(1)}, u32[]{:S(2)}, u32[]{:S(2)}) collective-permute-start(bf16[864,128]{1,0:T(8,128)(2,1)S(1)} %get-tuple-element.22), channel_id=1, source_target_pairs={{0,192},{64,0},{128,64},{192,128},{1,193},{65,1},{129,65},{193,129... | collective-permute-start | bytes 663560 | tf_op jit(solution)/shard_map/ppermute | solution.py:419
  46.0 8.1 %slice-start = ((s8[7962624]{0:T(1024)(128)(4,1)}), s8[4194304]{0:T(1024)(128)(4,1)S(1)}, s32[]{:S(2)}) async-start(s8[7962624]{0:T(1024)(128)(4,1)} %bitcast.13), calls=%async_computation.2 | async-start | bytes 8388608
  48.0 8.7 %collective-permute-start.4 = (bf16[720,128]{1,0:T(8,128)(2,1)S(1)}, bf16[720,128]{1,0:T(8,128)(2,1)S(1)}, u32[]{:S(2)}, u32[]{:S(2)}) collective-permute-start(bf16[720,128]{1,0:T(8,128)(2,1)S(1)} %collective-permute-done.after_ref.refs_1_), channel_id=1, source_target_pairs={{0,64},{64,128},{128,192},{192,0},{1,65},{65,129},{129,193},{193,1... | collective-permute-start | bytes 552968 | tf_op jit(solution)/shard_map/ppermute | solution.py:428
  48.1 8.6 %collective-permute-start.5 = (bf16[720,128]{1,0:T(8,128)(2,1)S(1)}, bf16[720,128]{1,0:T(8,128)(2,1)S(1)}, u32[]{:S(2)}, u32[]{:S(2)}) collective-permute-start(bf16[720,128]{1,0:T(8,128)(2,1)S(1)} %collective-permute-done.1.also_after_ref.refs_2_), channel_id=1, source_target_pairs={{0,192},{64,0},{128,64},{192,128},{1,193},{65,1},{129,65},{193,129... | collective-permute-start | bytes 552968 | tf_op jit(solution)/shard_map/ppermute | solution.py:429
  51.4 2.8 %slice-start.1 = ((s8[7962624]{0:T(1024)(128)(4,1)}), s8[3768320]{0:T(1024)(128)(4,1)S(1)}, s32[]{:S(2)}) async-start(s8[7962624]{0:T(1024)(128)(4,1)} %bitcast.13), calls=%async_computation.3 | async-start | bytes 7536640
  57.3 1.9 %collective-permute-start.6 = (bf16[576,384]{1,0:T(8,128)(2,1)S(1)}, bf16[576,384]{1,0:T(8,128)(2,1)S(1)}, u32[]{:S(2)}, u32[]{:S(2)}) collective-permute-start(bf16[576,384]{1,0:T(8,128)(2,1)S(1)} %shard_map.82.refs_8_), channel_id=1, source_target_pairs={{0,1},{1,0},{2,3},{3,2},{4,5},{5,4},{6,7},{7,6},{8,9},{9,8},{10,11... | collective-permute-start | bytes 1327112 | tf_op jit(solution)/shard_map/ppermute | solution.py:457

commit v13 on v12

--- a/solution.py
+++ b/solution.py
@@ -26,6 +26,7 @@
 PAYLOAD = D + COLS
 HALF = D // 2
 EARLY_HEADS = 5
+PART = ROWS // 4
 EXP_SCALE = SCALE * math.log2(math.e)
 
 NN = (((1,), (0,)), ((), ()))
@@ -74,7 +75,7 @@
 
 def source_row(packed):
     inner = packed % 8
-    return packed // 8 * PATCHES + inner % PATCHES + jnp.where(inner >= PATCHES, ROWS // 2, 0)
+    return packed // 8 * PATCHES + inner % PATCHES + jnp.where(inner >= PATCHES, PART, 0)
 
 
 def patch_row(packed):
@@ -83,27 +84,26 @@
 
 
 def pack_kernel(tokens_ref, d_out_ref, packed_ref, both_ref, out_ref, sems, out_sems):
-    part = ROWS // 2
     copies = [
         pltpu.make_async_copy(
-            ref.at[pl.ds(half * part, part)],
-            both_ref.at[pl.ds(half * ROWS + i * part, part)],
-            sems.at[half * 2 + i],
+            ref.at[pl.ds(quarter * PART, PART)],
+            both_ref.at[pl.ds(quarter * 2 * PART + i * PART, PART)],
+            sems.at[quarter * 2 + i],
         )
-        for half in range(2)
+        for quarter in range(4)
         for i, ref in enumerate((tokens_ref, d_out_ref))
     ]
     for copy in copies:
         copy.start()
-    chooser = pick((ROWS, ROWS), source_row(row_index(ROWS)), 1)
+    chooser = pick((2 * PART, 2 * PART), source_row(row_index(2 * PART)), 1)
     outs = []
-    for half in range(2):
-        for copy in copies[half * 2 : half * 2 + 2]:
+    for quarter in range(4):
+        for copy in copies[quarter * 2 : quarter * 2 + 2]:
             copy.wait()
-        rows = slice(half * ROWS, (half + 1) * ROWS)
+        rows = slice(quarter * 2 * PART, (quarter + 1) * 2 * PART)
         out_ref[rows, :] = dot(chooser, both_ref[rows, :]).astype(BF)
-        span = pl.ds(half * ROWS, ROWS)
-        out = pltpu.make_async_copy(out_ref.at[span], packed_ref.at[span], out_sems.at[half])
+        span = pl.ds(quarter * 2 * PART, 2 * PART)
+        out = pltpu.make_async_copy(out_ref.at[span], packed_ref.at[span], out_sems.at[quarter])
         out.start()
         outs.append(out)
     for out in outs:
@@ -375,8 +375,8 @@
         scratch=(
             pltpu.VMEM((256, D), BF),
             pltpu.VMEM((256, D), BF),
+            pltpu.SemaphoreType.DMA((8,)),
             pltpu.SemaphoreType.DMA((4,)),
-            pltpu.SemaphoreType.DMA((2,)),
         ),
         limit=60,
         far=(0, 1),

time: 87 us -> 87.2 us (level)
  no operation moved by 1% of the time
where the time goes in v13:
time: 87.2 us; the launch traced here: 86.9 us
  blocking collectives  25.5 us (29%)
  starting transfers between devices  21.3 us (24%)
  Pallas kernels  20 us (23%)
  waiting for transfers between devices  16 us (18%)
  local copies, waits for them, and re-layouts  2.09 us (2%)
  between operations  1.45 us (2%)
    all_to_all x1, blocking collectives, body(): lax.all_to_all(merged.reshape(SLOTS, CHUNK, 128), ('y', 'z'), split_axis=...  25.5 us
    pallas_call x9, Pallas kernels, call(): pl.pallas_call(kernel, out_shape=shapes, in_specs=[pl.BlockSpec(memory_sp...  20 us
    all_to_all x1, waiting for transfers between devices, body(): lax.all_to_all(packed.reshape(SLOTS, 8, D), ('y', 'z'), split_axis=0, con...  15.6 us
    all_to_all x1, starting transfers between devices, body(): lax.all_to_all(packed.reshape(SLOTS, 8, D), ('y', 'z'), split_axis=0, con...  11.4 us
    ppermute x1, starting transfers between devices, body(): far_b = lax.ppermute(right_a, 'dp', down)  3.22 us
    ppermute x1, starting transfers between devices, body(): right_b = lax.ppermute(left, 'dp', down)  2.94 us
    slice x1, local copies, waits for them, and re-layouts, body(): firsts = tuple((w_qkv[:, kind * D:kind * D + WIDE] for kind in range(3)))  1.98 us
  transfers between devices with their start and end apart: 8, of which 2 were waited for; matrix products, arithmetic and copies ran while one was open for 3% of the time, Pallas kernels for 10%

profile of v13, /device:TPU:32, one launch (start us, length us, event | category | flops | bytes accessed | tf_op | source)
XLA Modules:
  0.0 86.9 jit_solution(12528578972952899133)
XLA Ops:
  0.6 2.4 %shard_map.77 = bf16[256,1152]{1,0:T(8,128)(2,1)} custom-call(bf16[128,1152]{1,0:T(8,128)(2,1)} %bitcast.19, bf16[128,1152]{1,0:T(8,128)(2,1)} %bitcast.20), custom_call_target="tpu_custom_call" | custom-call | tf_op jit(solution)/shard_map/pallas_call | solution.py:47
  3.0 11.4 %all-to-all-start = ((bf16[32,8,1152]{2,1,0:T(8,128)(2,1)}), bf16[32,8,1152]{2,1,0:T(8,128)(2,1)S(1)}, u32[]{:S(2)}, u32[]{:S(2)}) async-start(bf16[32,8,1152]{2,1,0:T(8,128)(2,1)} %bitcast.18), calls=%async_computation | async-start | bytes 1179648 | tf_op jit(solution)/shard_map/all_to_all | solution.py:385
  15.1 0.7 fusion
  15.7 0.1 copy.8.live_ref
  15.8 2.0 %fusion.1 = (bf16[1152,384]{1,0:T(8,128)(2,1)S(1)}, bf16[1152,384]{1,0:T(8,128)(2,1)S(1)}, bf16[1152,384]{1,0:T(8,128)(2,1)S(1)}) fusion(bf16[1152,3456]{1,0:T(8,128)(2,1)} %w_qkv_ref.3), kind=kLoop, calls=%fused_computation.2 | loop fusion | bytes 5308416 | tf_op jit(solution)/shard_map/slice | solution.py:388
  17.8 15.6 %all-to-all-done = bf16[32,8,1152]{2,1,0:T(8,128)(2,1)S(1)} async-done(((bf16[32,8,1152]{2,1,0:T(8,128)(2,1)}), bf16[32,8,1152]{2,1,0:T(8,128)(2,1)S(1)}, u32[]{:S(2)}, u32[]{:S(2)}) %all-to-all-start) | async-done | bytes 589856 | tf_op jit(solution)/shard_map/all_to_all | solution.py:385
  33.4 0.0 copy-start
  33.4 6.2 %shard_map.78 = (bf16[128,1152]{1,0:T(8,128)(2,1)S(1)}, bf16[128,1152]{1,0:T(8,128)(2,1)S(1)}, bf16[128,3456]{1,0:T(8,128)(2,1)S(1)}, f32[16,32,128]{2,1,0:T(8,1...) custom-call(s32[1]{0:T(128)} %bitcast.1.place_ref, ...), custom_call_target="tpu_custom_call" | custom-call | flops 2000000000 | bytes 14000000 | tf_op jit(solution)/shard_map/pallas_call | solution.py:47
  39.6 1.6 %collective-permute-start = (bf16[720,128]{1,0:T(8,128)(2,1)S(1)}, bf16[720,128]{1,0:T(8,128)(2,1)S(1)}, u32[]{:S(2)}, u32[]{:S(2)}) collective-permute-start(bf16[720,128]{1,0:T(8,128)(2,1)S(1)} %get-tuple-element.19), channel_id=1, source_target_pairs={{0,64},{64,128},{128,192},{192,0},{1,65},{65,129},{129,193},{193,1... | collective-permute-start | bytes 552968 | tf_op jit(solution)/shard_map/ppermute | solution.py:416
  41.2 1.7 %collective-permute-start.1 = (bf16[720,128]{1,0:T(8,128)(2,1)S(1)}, bf16[720,128]{1,0:T(8,128)(2,1)S(1)}, u32[]{:S(2)}, u32[]{:S(2)}) collective-permute-start(bf16[720,128]{1,0:T(8,128)(2,1)S(1)} %get-tuple-element.20), channel_id=1, source_target_pairs={{0,192},{64,0},{128,64},{192,128},{1,193},{65,1},{129,65},{193,129... | collective-permute-start | bytes 552968 | tf_op jit(solution)/shard_map/ppermute | solution.py:417
  42.9 0.3 collective-permute-start.2
  43.2 2.9 %collective-permute-start.3 = (bf16[864,128]{1,0:T(8,128)(2,1)S(1)}, bf16[864,128]{1,0:T(8,128)(2,1)S(1)}, u32[]{:S(2)}, u32[]{:S(2)}) collective-permute-start(bf16[864,128]{1,0:T(8,128)(2,1)S(1)} %get-tuple-element.22), channel_id=1, source_target_pairs={{0,192},{64,0},{128,64},{192,128},{1,193},{65,1},{129,65},{193,129... | collective-permute-start | bytes 663560 | tf_op jit(solution)/shard_map/ppermute | solution.py:419
  46.2 0.0 copy-done
  46.2 0.0 slice-start
  46.2 2.0 %shard_map.79 = (bf16[128,1152]{1,0:T(8,128)(2,1)S(1)}, bf16[128,1152]{1,0:T(8,128)(2,1)S(1)}) custom-call(bf16[128,1152]{1,0:T(8,128)(2,1)S(1)} %get-tuple-element.24.masked_ref, bf16[128,3456]{1,0:T(8,128)(2,1)S(1)} %get-tuple-element.25.joined_ref, f32[16,32,128]{2,1,0:T(8,128)S(1)} %get-tuple-element.26.probs_ref, bf16[1152,1152]{1,0:T(8,128)(2,1)S(1)} %copy-done), custom_call_target="tpu_custom_call" | custom-call | flops 2000000000 | bytes 8000000 | tf_op jit(solution)/shard_map/pallas_call | solution.py:47
  48.2 0.0 collective-permute-done.after_ref.refs_1_
  48.2 0.1 collective-permute-start.4
  48.3 0.0 collective-permute-done.1.also_after_ref.refs_2_
  48.3 3.2 %collective-permute-start.5 = (bf16[720,128]{1,0:T(8,128)(2,1)S(1)}, bf16[720,128]{1,0:T(8,128)(2,1)S(1)}, u32[]{:S(2)}, u32[]{:S(2)}) collective-permute-start(bf16[720,128]{1,0:T(8,128)(2,1)S(1)} %collective-permute-done.1.also_after_ref.refs_2_), channel_id=1, source_target_pairs={{0,192},{64,0},{128,64},{192,128},{1,193},{65,1},{129,65},{193,129... | collective-permute-start | bytes 552968 | tf_op jit(solution)/shard_map/ppermute | solution.py:429
  51.5 0.0 slice-start.1
  51.5 2.7 %shard_map.80.grad_ref = bf16[128,3456]{1,0:T(8,128)(2,1)S(1)} custom-call(bf16[128,3456]{1,0:T(8,128)(2,1)S(1)} %get-tuple-element.25.joined_ref, f32[16,32,128]{2,1,0:T(8,128)S(1)} %get-tuple-element.26.probs_ref, bf16[128,1152]{1,0:T(8,128)(2,1)S(1)} %get-tuple-element.27.head_ref, bf16[128,1152]{1,0:T(8,128)(2,1)S(1)} %get-tuple-element.28.early_ref, ...), custom_call_target="tpu_custom_call" | custom-call | flops 3000000000 | bytes 16000000 | tf_op jit(solution)/shard_map/pallas_call | solution.py:47
  54.3 0.0 slice-done
  54.3 0.0 slice-done.1
  54.3 2.6 %shard_map.81.refs_7_ = bf16[128,1152]{1,0:T(8,128)(2,1)S(1)} custom-call(bf16[128,1152]{1,0:T(8,128)(2,1)S(1)} %get-tuple-element.23.tokens_ref, bf16[128,1152]{1,0:T(8,128)(2,1)S(1)} %get-tuple-element.24.masked_ref, bf16[128,3456]{1,0:T(8,128)(2,1)S(1)} %shard_map.80.grad_ref, bf16[1152,3456]{1,0:T(8,128)(2,1)S(1)} %bitcast.14), custom_call_target="tpu_custom_call" | custom-call | flops 3000000000 | bytes 16000000 | tf_op jit(solution)/shard_map/pallas_call | solution.py:47
  56.9 0.0 collective-permute-done.2.refs_3_
  56.9 0.0 collective-permute-done.3.refs_4_
  56.9 0.0 collective-permute-done.4.refs_5_
  56.9 0.0 collective-permute-done.5.refs_6_
  56.9 0.5 shard_map.82.refs_8_
  57.4 0.1 collective-permute-start.6
  57.5 1.5 %shard_map.83 = (f32[576,384]{1,0:T(8,128)S(1)}, bf16[2560,128]{1,0:T(8,128)(2,1)S(1)}, bf16[640,432]{1,0:T(8,128)(2,1)S(1)}) custom-call(s32[1]{0:T(128)} %bitcast.core_ref, bf16[1440,128]{1,0:T(8,128)(2,1)S(1)} %get-tuple-element.18.refs_0_, bf16[720,128]{1,0:T(8,128)(2,1)S(1)} %collective-permute-done.after_ref.refs_1_, ...), custom_call_target="tpu_custom_call" | custom-call | flops 1000000000 | bytes 4000000 | tf_op jit(solution)/shard_map/pallas_call | solution.py:47
  59.0 0.3 collective-permute-done.6.got_ref
  59.3 0.9 shard_map.84
  60.2 25.5 %all_to_all.10 = bf16[32,80,128]{2,1,0:T(8,128)(2,1)S(1)} all-to-all(bf16[32,80,128]{2,1,0:T(8,128)(2,1)S(1)} %bitcast.16), channel_id=1, replica_groups=mesh['dp'=4,'y'=4,'z'=8,'core'=2] {'y','z'}, dimensions={0} | all-to-all | bytes 1310720 | tf_op jit(solution)/shard_map/all_to_all | solution.py:474
  85.6 1.3 %shard_map.85 = (bf16[128,1152]{1,0:T(8,128)(2,1)}, f32[18,288]{1,0:T(8,128)}) custom-call(bf16[2560,128]{1,0:T(8,128)(2,1)S(1)} %bitcast.15), custom_call_target="tpu_custom_call" | custom-call | tf_op jit(solution)/shard_map/pallas_call | solution.py:47
  (1 shorter events, 0.0 us)
Async XLA Ops:
  3.0 30.4 %all-to-all-start = ((bf16[32,8,1152]{2,1,0:T(8,128)(2,1)}), bf16[32,8,1152]{2,1,0:T(8,128)(2,1)S(1)}, u32[]{:S(2)}, u32[]{:S(2)}) async-start(bf16[32,8,1152]{2,1,0:T(8,128)(2,1)} %bitcast.18), calls=%async_computation | async-start | bytes 1179648 | tf_op jit(solution)/shard_map/all_to_all | solution.py:385
  33.4 12.7 %copy-start = (bf16[1152,1152]{1,0:T(8,128)(2,1)S(1)}, bf16[1152,1152]{1,0:T(8,128)(2,1)}, u32[]{:S(2)}) copy-start(bf16[1152,1152]{1,0:T(8,128)(2,1)} %w_out_ref.1) | copy-start | bytes 7962628
  39.6 8.6 %collective-permute-start = (bf16[720,128]{1,0:T(8,128)(2,1)S(1)}, bf16[720,128]{1,0:T(8,128)(2,1)S(1)}, u32[]{:S(2)}, u32[]{:S(2)}) collective-permute-start(bf16[720,128]{1,0:T(8,128)(2,1)S(1)} %get-tuple-element.19), channel_id=1, source_target_pairs={{0,64},{64,128},{128,192},{192,0},{1,65},{65,129},{129,193},{193,1... | collective-permute-start | bytes 552968 | tf_op jit(solution)/shard_map/ppermute | solution.py:416
  41.2 7.1 %collective-permute-start.1 = (bf16[720,128]{1,0:T(8,128)(2,1)S(1)}, bf16[720,128]{1,0:T(8,128)(2,1)S(1)}, u32[]{:S(2)}, u32[]{:S(2)}) collective-permute-start(bf16[720,128]{1,0:T(8,128)(2,1)S(1)} %get-tuple-element.20), channel_id=1, source_target_pairs={{0,192},{64,0},{128,64},{192,128},{1,193},{65,1},{129,65},{193,129... | collective-permute-start | bytes 552968 | tf_op jit(solution)/shard_map/ppermute | solution.py:417
  42.9 14.0 %collective-permute-start.2 = (bf16[864,128]{1,0:T(8,128)(2,1)S(1)}, bf16[864,128]{1,0:T(8,128)(2,1)S(1)}, u32[]{:S(2)}, u32[]{:S(2)}) collective-permute-start(bf16[864,128]{1,0:T(8,128)(2,1)S(1)} %get-tuple-element.21), channel_id=1, source_target_pairs={{0,64},{64,128},{128,192},{192,0},{1,65},{65,129},{129,193},{193,1... | collective-permute-start | bytes 663560 | tf_op jit(solution)/shard_map/ppermute | solution.py:418
  43.2 13.7 %collective-permute-start.3 = (bf16[864,128]{1,0:T(8,128)(2,1)S(1)}, bf16[864,128]{1,0:T(8,128)(2,1)S(1)}, u32[]{:S(2)}, u32[]{:S(2)}) collective-permute-start(bf16[864,128]{1,0:T(8,128)(2,1)S(1)} %get-tuple-element.22), channel_id=1, source_target_pairs={{0,192},{64,0},{128,64},{192,128},{1,193},{65,1},{129,65},{193,129... | collective-permute-start | bytes 663560 | tf_op jit(solution)/shard_map/ppermute | solution.py:419
  46.2 8.1 %slice-start = ((s8[7962624]{0:T(1024)(128)(4,1)}), s8[4194304]{0:T(1024)(128)(4,1)S(1)}, s32[]{:S(2)}) async-start(s8[7962624]{0:T(1024)(128)(4,1)} %bitcast.13), calls=%async_computation.2 | async-start | bytes 8388608
  48.2 8.7 %collective-permute-start.4 = (bf16[720,128]{1,0:T(8,128)(2,1)S(1)}, bf16[720,128]{1,0:T(8,128)(2,1)S(1)}, u32[]{:S(2)}, u32[]{:S(2)}) collective-permute-start(bf16[720,128]{1,0:T(8,128)(2,1)S(1)} %collective-permute-done.after_ref.refs_1_), channel_id=1, source_target_pairs={{0,64},{64,128},{128,192},{192,0},{1,65},{65,129},{129,193},{193,1... | collective-permute-start | bytes 552968 | tf_op jit(solution)/shard_map/ppermute | solution.py:428
  48.3 8.6 %collective-permute-start.5 = (bf16[720,128]{1,0:T(8,128)(2,1)S(1)}, bf16[720,128]{1,0:T(8,128)(2,1)S(1)}, u32[]{:S(2)}, u32[]{:S(2)}) collective-permute-start(bf16[720,128]{1,0:T(8,128)(2,1)S(1)} %collective-permute-done.1.also_after_ref.refs_2_), channel_id=1, source_target_pairs={{0,192},{64,0},{128,64},{192,128},{1,193},{65,1},{129,65},{193,129... | collective-permute-start | bytes 552968 | tf_op jit(solution)/shard_map/ppermute | solution.py:429
  51.5 2.8 %slice-start.1 = ((s8[7962624]{0:T(1024)(128)(4,1)}), s8[3768320]{0:T(1024)(128)(4,1)S(1)}, s32[]{:S(2)}) async-start(s8[7962624]{0:T(1024)(128)(4,1)} %bitcast.13), calls=%async_computation.3 | async-start | bytes 7536640
  57.4 1.9 %collective-permute-start.6 = (bf16[576,384]{1,0:T(8,128)(2,1)S(1)}, bf16[576,384]{1,0:T(8,128)(2,1)S(1)}, u32[]{:S(2)}, u32[]{:S(2)}) collective-permute-start(bf16[576,384]{1,0:T(8,128)(2,1)S(1)} %shard_map.82.refs_8_), channel_id=1, source_target_pairs={{0,1},{1,0},{2,3},{3,2},{4,5},{5,4},{6,7},{7,6},{8,9},{9,8},{10,11... | collective-permute-start | bytes 1327112 | tf_op jit(solution)/shard_map/ppermute | solution.py:457
